TPU v7x, 512 devices: a whole 4x4x16 slice. The times are simulated.
512 devices in a mesh: band: 16 (over y, z_hi, core), fft: 32 (over x, z_lo).
Axes of the slice: x: 4, y: 4, z: 16 (z_hi: 2, z_lo: 8; z = z_hi * 8 + z_lo), core: 2. Of those that a mesh axis runs over, the one named last changes fastest.
Arguments:
- trial_block: float32 [128, 200704], P('band', 'fft'), may hold values from -0.013671875 to 0.013671875
- all_bands: float32 [512, 200704], P('band', 'fft'), may hold values from -6 to 6
- potential: float32 [192, 192, 192], P('fft'), may hold values from -1.5 to 1
- positions: int32 [4096], replicated, may hold values from 0 to 36863, as said below
- sphere_slots: int32 [200704], P('fft'), may hold values from 0 to 24575, as said below
Outputs:
- intersection: float32 [512, 128], P(('band', 'fft'))
- projected: float32 [512, 128], P(('band', 'fft'))
Inputs may be any that keep to these rules, and one draw needn't show every extreme that they name: `positions`: the 4096 entries are distinct; every column has wrapped frequencies wrap(g1), wrap(g2) in -32 to 31, and all such columns occur once, in any order. `sphere_slots`: each fft device's 6272 entries are distinct and ascending; for each local column c they are exactly the slots whose wrapped g3 runs from -h to h for some h of the column, at least 1.
All inputs are finite; a program needn't handle non-finite values.
Results may differ from a plain program's by a relative error of at most 0.000073.
Values sent between devices are 32-bit elements; how exact they have to be, the bound alone decides.
No kernel may reach another device: no remote copies, remote signals or barrier semaphores. Data moves between devices by JAX's collectives and lax.ppermute only.
A program may use at most 128 MiB of HBM per device.

v0:
```python
import math

import jax
import jax.numpy as jnp
from jax import lax
from jax.sharding import PartitionSpec as P

K = 64


def cas_matrix(length):
    row_ids = lax.broadcasted_iota(jnp.int32, (length, length), 0)
    col_ids = lax.broadcasted_iota(jnp.int32, (length, length), 1)
    angle = (row_ids * col_ids % length).astype(jnp.float32) * (2.0 * math.pi / length)
    return (jnp.cos(angle) + jnp.sin(angle)) * (1.0 / math.sqrt(length))


def wrapped(values, length):
    return values - length * (values >= length // 2).astype(jnp.int32)


def apply_hamiltonian(trial_block, potential, positions, sphere_slots):
    precise = lax.Precision.HIGHEST
    band_count = trial_block.shape[0]
    planes = potential.shape[0]
    grid_cells = potential.shape[1]
    cols_dev = positions.shape[0] // lax.axis_size("fft")
    box_side = K
    box_half = box_side // 2
    cas_rows = cas_matrix(grid_cells)
    box_table = cas_rows[(lax.iota(jnp.int32, box_side) - box_half) % grid_cells]
    freq_one = wrapped(positions // grid_cells, grid_cells)
    freq_two = wrapped(positions % grid_cells, grid_cells)
    box_index = (freq_one + box_half) * box_side + (freq_two + box_half)
    radial_all = (freq_one * freq_one + freq_two * freq_two).astype(jnp.float32)
    radial_mine = lax.dynamic_slice_in_dim(radial_all, lax.axis_index("fft") * cols_dev, cols_dev)
    height = sphere_slots // cols_dev
    local_col = sphere_slots % cols_dev
    selector = (local_col[:, None] == lax.broadcasted_iota(jnp.int32, (1, cols_dev), 1)).astype(
        jnp.float32
    )
    radial = jnp.dot(selector, radial_mine, precision=precise)
    freq_three = wrapped(height, grid_cells)
    kinetic = 2.0 * (radial + (freq_three * freq_three).astype(jnp.float32)) / (box_side * box_side)
    packed_grid = (
        jnp.zeros((band_count, grid_cells * cols_dev), jnp.float32)
        .at[:, sphere_slots]
        .set(trial_block)
    )
    columns = packed_grid.reshape(band_count, grid_cells, cols_dev)
    z_mixed = jnp.einsum("zg,bgc->bzc", cas_rows, columns, precision=precise)
    gathered = lax.all_to_all(z_mixed, "fft", split_axis=1, concat_axis=2, tiled=True)
    item_count = gathered.shape[0]
    box_grid = jnp.zeros((item_count, planes, box_side * box_side), jnp.float32)
    box_grid = (
        box_grid.at[:, :, box_index].set(gathered).reshape(item_count, planes, box_side, box_side)
    )
    y_mixed = jnp.einsum("bzxy,yv->bzxv", box_grid, box_table, precision=precise)
    real_field = jnp.einsum("bzxv,xu->bzuv", y_mixed, box_table, precision=precise) * potential
    y_back = jnp.einsum("bzuv,yv->bzuy", real_field, box_table, precision=precise)
    x_back = jnp.einsum("bzuy,xu->bzxy", y_back, box_table, precision=precise)
    picked = x_back.reshape(item_count, planes, box_side * box_side)[:, :, box_index]
    returned = lax.all_to_all(picked, "fft", split_axis=2, concat_axis=1, tiled=True)
    back_cols = jnp.einsum("gz,bzc->bgc", cas_rows, returned, precision=precise)
    return (
        back_cols.reshape(band_count, grid_cells * cols_dev)[:, sphere_slots]
        + kinetic * trial_block
    )


def per_device(trial_block, all_bands, potential, positions, sphere_slots):
    precise = lax.Precision.HIGHEST
    applied = apply_hamiltonian(trial_block, potential, positions, sphere_slots)
    incoming = (
        lax.all_gather(trial_block, "band", axis=0, tiled=True),
        lax.all_gather(applied, "band", axis=0, tiled=True),
    )
    piece_rows = incoming[0].shape[0]
    joined = jnp.concatenate((incoming[0], incoming[1]), axis=0)
    products = jnp.einsum("ag,bg->ab", all_bands, joined, precision=precise)
    first = products[:, :piece_rows]
    second = products[:, piece_rows:]
    intersection = first
    projected = second
    intersection, projected = (
        lax.psum_scatter(intersection, "fft", scatter_dimension=0, tiled=True),
        lax.psum_scatter(projected, "fft", scatter_dimension=0, tiled=True),
    )
    return (intersection, projected)


def solution(mesh):
    placed = (P("band", "fft"), P("band", "fft"), P("fft", None, None), P(), P("fft"))
    return jax.shard_map(
        per_device,
        mesh=mesh,
        in_specs=placed,
        out_specs=(P(("band", "fft"), None), P(("band", "fft"), None)),
        check_vma=False,
    )
```

profile of v0, /device:TPU:8, one launch (start us, length us, event | category | flops | bytes accessed | tf_op | source)
XLA Modules:
  0.0 1119.9 jit_solution(14865070981563719035)
XLA Ops:
  11.1 29.5 %scatter_custom_fusion = f32[8,24576]{0,1:T(8,128)} fusion(s32[6272]{0:T(1024)S(1)} %get-tuple-element.9, f32[6272,8]{1,0:T(8,128)} %copy.59, f32[]{:T(128)} %constant.85.clone.1), kind=kCustom, calls=%fused_computation.11 | custom fusion | bytes 786944 | tf_op jit(solution)/shard_map/scatter | solution.py:48
  40.6 7.4 copy.60
  51.0 15.4 %all-to-all-start = ((f32[8,192,128]{2,0,1:T(8,128)}), f32[8,192,128]{2,0,1:T(8,128)S(1)}, u32[]{:S(2)}, u32[]{:S(2)}) async-start(f32[8,192,128]{2,0,1:T(8,128)} %copy.61), calls=%async_computation | async-start | bytes 1572864 | tf_op jit(solution)/shard_map/all_to_all | solution.py:52
  68.7 47.0 %all-to-all-done = f32[8,192,128]{2,0,1:T(8,128)S(1)} async-done(((f32[8,192,128]{2,0,1:T(8,128)}), f32[8,192,128]{2,0,1:T(8,128)S(1)}, u32[]{:S(2)}, u32[]{:S(2)}) %all-to-all-start) | async-done | bytes 786464 | tf_op jit(solution)/shard_map/all_to_all | solution.py:52
  115.7 8.9 copy.63
  124.6 6.0 broadcast_in_dim.8
  130.6 415.6 %scatter_fusion = f32[8,6,4096]{1,0,2:T(8,128)} fusion(f32[8,6,4096]{1,0,2:T(8,128)} %broadcast_in_dim.8, s32[4096]{0:T(1024)S(1)} %get-tuple-element.5, f32[4096,8,6]{2,1,0:T(8,128)} %copy.63), kind=kCustom, calls=%fused_computation.4 | custom fusion | bytes 2375680 | tf_op jit(solution)/shard_map/scatter | solution.py:56
  546.2 10.6 copy.64
  559.6 7.8 fusion.24
  567.4 21.3 %fusion = f32[8,6,192,64]{2,3,1,0:T(8,128)S(1)} fusion(f32[192,8,6,192]{3,0,2,1:T(8,128)S(1)} %fusion.24, f32[6,192,192]{2,1,0:T(8,128)S(1)} %copy-done.2, f32[64,192]{1,0:T(8,128)S(1)} %gather_fusion), kind=kOutput, calls=%fused_computation.6 | convolution fusion | flops 1360723968 | bytes 10371072 | tf_op jit(solution)/shard_map/bzuv,yv->bzuy/dot_general | solution.py:60
  588.7 4.7 convolution_bitcast_fusion
  593.4 9.0 copy.78
  602.3 36.7 %gather_fusion.1 = f32[4096,8,6]{2,1,0:T(8,128)} fusion(f32[8,6,4096]{1,0,2:T(8,128)} %bitcast.68, s32[4096]{0:T(1024)S(1)} %get-tuple-element.4), kind=kCustom, calls=%fused_computation.1 | custom fusion | bytes 1589248 | tf_op jit(solution)/shard_map/gather | solution.py:62
  639.0 11.3 %bitcast_bitcast_fusion.1 = f32[4096,8,6]{2,1,0:T(8,128)} fusion(f32[4096,8,6]{2,1,0:T(8,128)} %gather_fusion.1), kind=kLoop, calls=%fused_computation.82 | loop fusion | bytes 1572864
  650.3 16.4 %reshape.111 = f32[32,1,6144]{2,1,0:T(1,128)} reshape(f32[4096,8,6]{2,1,0:T(8,128)} %bitcast_bitcast_fusion.1) | data formatting | bytes 1572864
  666.7 5.3 all-to-all-start.1
  674.0 37.1 %all-to-all-done.1 = f32[32,1,6144]{2,1,0:T(1,128)S(1)} async-done(((f32[32,1,6144]{2,1,0:T(1,128)}), f32[32,1,6144]{2,1,0:T(1,128)S(1)}, u32[]{:S(2)}, u32[]{:S(2)}) %all-to-all-start.1) | async-done | bytes 786464 | tf_op jit(solution)/shard_map/all_to_all | solution.py:63
  714.1 19.9 %reshape.112 = f32[4096,8,6]{2,1,0:T(8,128)} reshape(f32[32,6144]{1,0:T(8,128)S(1)} %reduce.2) | data formatting | bytes 1572864
  734.0 9.8 copy.68
  745.6 6.7 copy.77
  752.2 17.1 %gather_fusion.2 = f32[6272,8]{1,0:T(8,128)} fusion(f32[8,24576]{0,1:T(8,128)} %bitcast.69, s32[7168]{0:T(1024)S(1)} %pad_clamp_fusion), kind=kCustom, calls=%fused_computation.2 | custom fusion | bytes 426496 | tf_op jit(solution)/shard_map/gather | solution.py:66
  774.0 102.7 %all-gather.5.cloned.1.call-done = f32[128,6272]{1,0:T(8,128)} async-done(((f32[8,6272]{1,0:T(8,128)}), f32[128,6272]{1,0:T(8,128)}) %all-gather.5.cloned.1.call-update) | async-done | bytes 3211280 | tf_op jit(solution)/shard_map/all_gather | solution.py:76
  876.7 8.3 fusion.10
  885.1 226.5 %all-reduce.2 = (f32[32,128]{1,0:T(8,128)S(1)}, f32[32,128]{1,0:T(8,128)S(1)}) all-reduce(f32[32,128]{1,0:T(8,128)S(1)} %get-tuple-element.7, f32[32,128]{1,0:T(8,128)S(1)} %get-tuple-element.6), channel_id=2, replica_groups=mesh['band'=16,'fft'=32] {'fft'}, use_global_device_ids=true, to_apply=%region_2.3.clone | all-reduce | flops 8192 | bytes 65536
  (37 shorter events, 24.4 us)
Async XLA Ops:
  7.2 869.6 %copy-start = (f32[32,6272]{1,0:T(8,128)S(1)}, f32[32,6272]{1,0:T(8,128)}, u32[]{:S(2)}) copy-start(f32[32,6272]{1,0:T(8,128)} %param.6) | copy-start | bytes 2408452
  40.6 28.1 %copy-start.4 = (s32[4096]{0:T(1024)S(1)}, s32[4096]{0:T(1024)}, u32[]{:S(2)}) copy-start(s32[4096]{0:T(1024)} %param.8) | copy-start | bytes 49156
  51.0 64.6 %all-to-all-start = ((f32[8,192,128]{2,0,1:T(8,128)}), f32[8,192,128]{2,0,1:T(8,128)S(1)}, u32[]{:S(2)}, u32[]{:S(2)}) async-start(f32[8,192,128]{2,0,1:T(8,128)} %copy.61), calls=%async_computation | async-start | bytes 1572864 | tf_op jit(solution)/shard_map/all_to_all | solution.py:52
  66.4 707.6 %all-gather.3.cloned.1.call-start = ((), (), s32[]{:S(2)}) async-start(), calls=%async_computation.2 | async-start | bytes 3411968 | tf_op jit(solution)/shard_map/all_gather | solution.py:75
  559.6 7.9 copy-start.2
  650.3 23.7 %copy-start.3 = (s32[6272]{0:T(1024)S(1)}, s32[6272]{0:T(1024)}, u32[]{:S(2)}) copy-start(s32[6272]{0:T(1024)} %param.9) | copy-start | bytes 75268
  666.7 44.4 %all-to-all-start.1 = ((f32[32,1,6144]{2,1,0:T(1,128)}), f32[32,1,6144]{2,1,0:T(1,128)S(1)}, u32[]{:S(2)}, u32[]{:S(2)}) async-start(f32[32,1,6144]{2,1,0:T(1,128)} %reshape.111), calls=%async_computation.1 | async-start | bytes 1572864 | tf_op jit(solution)/shard_map/all_to_all | solution.py:63
  672.0 204.7 %all-gather.5.cloned.1.call-start = ((), (), s32[]{:S(2)}) async-start(), calls=%async_computation.3 | async-start | bytes 3411968 | tf_op jit(solution)/shard_map/all_gather | solution.py:76
  745.5 26.4 %copy-start.1 = (f32[8,6272]{1,0:T(8,128)S(1)}, f32[8,6272]{1,0:T(8,128)}, u32[]{:S(2)}) copy-start(f32[8,6272]{1,0:T(8,128)} %param.5) | copy-start | bytes 602116
Sparse Core Ops, SparseCore 0:
  70.4 112.6 all-gather.2
  772.9 103.8 all-gather.4
where the time goes:
time: 1140 us; the launch traced here: 1120 us
  local copies, waits for them, and re-layouts  615 us (54%)
  blocking collectives  226 us (20%)
  waiting for transfers between devices  187 us (16%)
  matrix products  50.1 us (4%)
  starting transfers between devices  20.8 us (2%)
  between operations  14.6 us (1%)
    scatter x1, local copies, waits for them, and re-layouts, apply_hamiltonian(): box_grid.at[:, :, box_index].set(gathered)  416 us
    unnamed x1, blocking collectives  226 us
    all_gather x1, waiting for transfers between devices, per_device(): lax.all_gather(applied, 'band', axis=0, tiled=True)  103 us
    unnamed x16, local copies, waits for them, and re-layouts  53 us
    all_to_all x1, waiting for transfers between devices, apply_hamiltonian(): lax.all_to_all(z_mixed, 'fft', split_axis=1, concat_axis=2, tiled=True)  47 us
    all_to_all x1, waiting for transfers between devices, apply_hamiltonian(): lax.all_to_all(picked, 'fft', split_axis=2, concat_axis=1, tiled=True)  37.1 us
    gather x1, local copies, waits for them, and re-layouts, apply_hamiltonian(): x_back.reshape(item_count, planes, box_side * box_side)[:, :, box_index]  36.7 us
    scatter x1, local copies, waits for them, and re-layouts, apply_hamiltonian(): packed_grid = jnp.zeros((band_count, grid_cells * cols_dev), jnp.float32)...  29.5 us
  transfers between devices with their start and end apart: 4, of which 3 were waited for; matrix products, arithmetic and copies ran while one was open for 55% of the time, Pallas kernels for 0%

commit v1 on v0

v1 whole, which is shorter than its diff:
```python
import functools
import math

import jax
import jax.numpy as jnp
import numpy as np
from jax import lax
from jax.experimental import pallas as pl
from jax.experimental.pallas import tpu as pltpu
from jax.sharding import PartitionSpec as P

K = 64
LANES = 128
F32 = jnp.float32
BF16 = jnp.bfloat16


def cas_matrix(length):
    ids = np.arange(length)
    angle = (ids[:, None] * ids[None, :] % length) * (2.0 * math.pi / length)
    return ((np.cos(angle) + np.sin(angle)) / math.sqrt(length)).astype(np.float32)


def halves(table):
    high = table.astype(jnp.bfloat16)
    low = (table - high.astype(np.float32)).astype(jnp.bfloat16)
    return high, low


def split(values):
    high = values.astype(BF16)
    low = (values - high.astype(F32)).astype(BF16)
    return high, low


def dot(left, right):
    return jnp.dot(left, right, preferred_element_type=F32)


def wrapped(values, length):
    return jnp.where(values >= length // 2, values - length, values)


def take_lanes(row, lanes):
    return jnp.take_along_axis(row, lanes, axis=1, mode="promise_in_bounds")


def column_box(positions, grid_cells):
    first = lax.shift_right_logical(lax.shift_right_logical(positions, 6) * 43691, 17)
    second = positions - first * grid_cells
    return wrapped(first, grid_cells), wrapped(second, grid_cells)


def tables_kernel(grid_cells, slots_ref, positions_ref, where_ref, start_ref, inverse_ref, box_ref):
    rows = slots_ref.shape[0]
    column = slots_ref[...] & (LANES - 1)
    lane_ids = lax.broadcasted_iota(jnp.int32, (LANES, LANES), 0)
    counts = jnp.zeros((LANES, LANES), F32)
    ones = jnp.ones((8, LANES), BF16)
    total = jnp.zeros((8, LANES), F32)
    nt = (((1,), (1,)), ((), ()))
    for row in range(rows):
        hit = (column[row : row + 1, :] == lane_ids).astype(BF16)
        total = total + lax.dot_general(ones, hit, nt, preferred_element_type=F32)
    reach = (total[0:1, :] - 1.0) * 0.5
    height = lax.broadcasted_iota(jnp.int32, (grid_cells, LANES), 0)
    away = jnp.abs(wrapped(height, grid_cells)).astype(F32)
    valid = away <= reach
    valid_one = valid.astype(BF16)
    before = (
        lax.broadcasted_iota(jnp.int32, (LANES, LANES), 0)
        < lax.broadcasted_iota(jnp.int32, (LANES, LANES), 1)
    ).astype(BF16)
    rank = dot(valid_one, before)
    in_row = dot(valid_one, jnp.ones((LANES, LANES), BF16)).astype(BF16)
    below = (
        lax.broadcasted_iota(jnp.int32, (grid_cells, grid_cells), 0)
        > lax.broadcasted_iota(jnp.int32, (grid_cells, grid_cells), 1)
    ).astype(BF16)
    start = dot(below, in_row)
    start_ref[...] = start.astype(jnp.int32)
    where_ref[...] = jnp.where(valid, start + rank, -1.0).astype(jnp.int32)
    first, second = column_box(positions_ref[...], grid_cells)
    box = (first + K // 2) * K + second + K // 2
    box_ref[...] = box
    sources = positions_ref.shape[0]
    blocks = sources
    block_ids = lax.broadcasted_iota(jnp.int32, (blocks, LANES), 0)
    own_lane = lax.broadcasted_iota(jnp.int32, (blocks, LANES), 1).astype(F32)
    inverse = jnp.zeros((2 * blocks, LANES), F32)
    for source in range(sources):
        place = box[source : source + 1, :]
        in_block = lax.shift_right_logical(place, 7) == block_ids
        left = jnp.concatenate(
            [jnp.where(in_block, float(source), 0.0), jnp.where(in_block, own_lane, 0.0)], axis=0
        ).astype(BF16)
        right = ((place & (LANES - 1)) == lane_ids).astype(BF16)
        inverse = inverse + lax.dot_general(left, right, nt, preferred_element_type=F32)
    inverse_ref[...] = inverse.astype(jnp.int32)


def forward_kernel(bands, grid_cells, starts, trial_ref, where_ref, cas_ref, out_ref, dense):
    last = trial_ref.shape[1] // LANES - 1

    def expand(height, carry):
        row = lax.shift_right_logical(starts[height], 7)
        after = jnp.minimum(row + 1, last)
        here = trial_ref[:, pl.ds(pl.multiple_of(row * LANES, LANES), LANES)]
        there = trial_ref[:, pl.ds(pl.multiple_of(after * LANES, LANES), LANES)]
        place = jnp.broadcast_to(where_ref[pl.ds(height, 1), :], (bands, LANES)) - row * LANES
        lanes = place & (LANES - 1)
        value = jnp.where(place < LANES, take_lanes(here, lanes), take_lanes(there, lanes))
        dense[pl.ds(pl.multiple_of(height * bands, bands), bands), :] = jnp.where(
            place < 0, 0.0, value
        )
        return carry

    lax.fori_loop(0, grid_cells, expand, 0, unroll=8)
    for band in range(0, bands, 2):
        pair = jnp.concatenate(
            [dense[pl.ds(band + side, grid_cells, stride=bands), :] for side in range(2)], axis=1
        )
        high, low = split(pair)
        mixed = dot(cas_ref[...], jnp.concatenate([high, low, high], axis=0))
        for side in range(2):
            out_ref[pl.ds(band + side, grid_cells, stride=bands), :] = mixed[
                :, side * LANES : (side + 1) * LANES
            ]


def plane_kernel(
    bands,
    sources,
    inverse_ref,
    box_ref,
    y_ref,
    x_ref,
    x_back_ref,
    y_back_ref,
    potential_ref,
    columns_ref,
    out_ref,
    boxes,
):
    grid_cells = potential_ref.shape[1]
    blocks = sources

    def fill(block, carry):
        source_of = jnp.broadcast_to(inverse_ref[pl.ds(block, 1), :], (bands, LANES))
        lane_of = jnp.broadcast_to(inverse_ref[pl.ds(block + blocks, 1), :], (bands, LANES))
        value = jnp.zeros((bands, LANES), F32)
        for source in range(sources):
            value = jnp.where(
                source_of == source, take_lanes(columns_ref[source, 0], lane_of), value
            )
        boxes[pl.ds(pl.multiple_of(block * bands, bands), bands), :] = value
        return carry

    lax.fori_loop(0, blocks, fill, 0)
    stacked = jnp.concatenate(
        [boxes[pl.ds(band, blocks, stride=bands), :] for band in range(bands)], axis=0
    )
    high, low = split(stacked)
    wide = dot(jnp.concatenate([high, low, high], axis=1), y_ref[...])
    half_width = wide.shape[1] // 2
    potential = potential_ref[0]
    back = []
    for band in range(bands):
        mine = wide[band * blocks : (band + 1) * blocks, :]
        mine = jnp.concatenate([mine[:, :half_width], mine[:, half_width:]], axis=0)
        high, low = split(mine)
        field = dot(x_ref[...], jnp.concatenate([high, low, high], axis=0))
        high, low = split(field[:, :grid_cells] * potential)
        both = dot(x_back_ref[...], high)
        back.append(both[:K] + both[K:] + dot(x_back_ref[:K, :], low))
    total = None
    for side in range(2):
        part = jnp.concatenate(
            [one[side * blocks : (side + 1) * blocks, :] for one in back], axis=0
        )
        high, low = split(part)
        term = dot(high, y_back_ref[side, 0]) + dot(low, y_back_ref[side, 0])
        term = term + dot(high, y_back_ref[side, 1])
        total = term if total is None else total + term
    for band in range(bands):
        boxes[pl.ds(band, blocks, stride=bands), :] = total[band * blocks : (band + 1) * blocks, :]

    def pick(source, carry):
        place = jnp.broadcast_to(box_ref[pl.ds(source, 1), :], (bands, LANES))
        lane_of = place & (LANES - 1)
        block_of = lax.shift_right_logical(place, 7)
        value = jnp.zeros((bands, LANES), F32)
        for block in range(blocks):
            value = jnp.where(
                block_of == block,
                take_lanes(boxes[block * bands : (block + 1) * bands, :], lane_of),
                value,
            )
        out_ref[source, 0] = value
        return carry

    lax.fori_loop(0, sources, pick, 0)


def backward_kernel(
    bands,
    grid_cells,
    starts,
    trial_ref,
    slots_ref,
    own_ref,
    cas_ref,
    returned_ref,
    out_ref,
    dense,
):
    for band in range(0, bands, 2):
        pair = jnp.concatenate(
            [returned_ref[pl.ds(band + side, grid_cells, stride=bands), :] for side in range(2)],
            axis=1,
        )
        high, low = split(pair)
        mixed = dot(cas_ref[...], jnp.concatenate([high, low, high], axis=0))
        for side in range(2):
            dense[pl.ds(band + side, grid_cells, stride=bands), :] = mixed[
                :, side * LANES : (side + 1) * LANES
            ]
    rows = slots_ref.shape[0]
    first, second = column_box(own_ref[...], grid_cells)
    radial = jnp.broadcast_to((first * first + second * second).astype(F32), (bands, LANES))
    for row in range(rows):
        slots = jnp.broadcast_to(slots_ref[row : row + 1, :], (bands, LANES))
        height = wrapped(lax.shift_right_logical(slots, 7), grid_cells)
        around = take_lanes(radial, slots & (LANES - 1))
        kinetic = 2.0 * (around + (height * height).astype(F32)) / (K * K)
        cut = slice(row * LANES, (row + 1) * LANES)
        out_ref[:, cut] = kinetic * trial_ref[:, cut]

    def compact(height, carry):
        values = dense[pl.ds(pl.multiple_of(height * bands, bands), bands), :]
        row = lax.shift_right_logical(starts[height], 7)
        for step in range(2):
            near = row + step
            if step:
                near = jnp.minimum(near, rows - 1)
            slots = jnp.broadcast_to(slots_ref[pl.ds(near, 1), :], (bands, LANES))
            mask = lax.shift_right_logical(slots, 7) == height
            if step:
                mask = mask & (near > row)
            cut = pl.ds(pl.multiple_of(near * LANES, LANES), LANES)
            out_ref[:, cut] += jnp.where(mask, take_lanes(values, slots & (LANES - 1)), 0.0)
        return carry

    lax.fori_loop(0, grid_cells, compact, 0, unroll=4)


def constant_tables(grid_cells):
    cas = cas_matrix(grid_cells)
    box_table = cas[(np.arange(K) - K // 2) % grid_cells]
    high, low = halves(cas)
    cas_three = np.concatenate([high, high, low], axis=1)
    padded = -(-grid_cells // LANES) * LANES
    sides = np.zeros((2, K, 2, padded), np.float32)
    for side in range(2):
        sides[side, :, side, :grid_cells] = box_table
    high, low = halves(sides.reshape(2 * K, 2 * padded))
    y_three = np.concatenate([high, high, low], axis=0)
    order = np.concatenate([np.arange(0, K, 2), np.arange(1, K, 2)])
    high, low = halves(box_table[order])
    x_three = np.concatenate([high, high, low], axis=0).T
    x_back = np.concatenate([high, low], axis=0)
    back = np.zeros((2, grid_cells, 2, K), np.float32)
    for side in range(2):
        back[side, :, side, :] = box_table.T
    high, low = halves(back.reshape(2, grid_cells, 2 * K))
    y_back = np.stack([high, low], axis=1)
    return tuple(jnp.asarray(one) for one in (cas_three, y_three, x_three, x_back, y_back))


def whole(array):
    return pl.BlockSpec(array.shape, lambda *_: (0,) * array.ndim)


def apply_hamiltonian(trial_block, potential, positions, sphere_slots):
    bands, coefs = trial_block.shape
    planes, grid_cells = potential.shape[:2]
    fft_size = lax.axis_size("fft")
    slots = sphere_slots.reshape(coefs // LANES, LANES)
    position_rows = positions.reshape(fft_size, LANES)
    own = lax.dynamic_slice_in_dim(position_rows, lax.axis_index("fft"), 1)
    cas_three, y_three, x_three, x_back, y_back = constant_tables(grid_cells)
    i32 = functools.partial(jax.ShapeDtypeStruct, dtype=jnp.int32)
    f32 = functools.partial(jax.ShapeDtypeStruct, dtype=F32)
    params = pltpu.CompilerParams(vmem_limit_bytes=48 * 2**20)
    where, start, inverse, box = pl.pallas_call(
        functools.partial(tables_kernel, grid_cells),
        out_shape=(
            i32((grid_cells, LANES)),
            i32((grid_cells, LANES)),
            i32((2 * fft_size, LANES)),
            i32((fft_size, LANES)),
        ),
        compiler_params=params,
        name="tables",
    )(slots, position_rows)
    starts = start[:, 0]
    dense_rows = grid_cells * bands
    smem = pl.BlockSpec(memory_space=pltpu.SMEM)
    vmem = pl.BlockSpec(memory_space=pltpu.VMEM)
    mixed = pl.pallas_call(
        functools.partial(forward_kernel, bands, grid_cells),
        out_shape=f32((dense_rows, LANES)),
        in_specs=[smem, vmem, vmem, vmem],
        out_specs=vmem,
        scratch_shapes=[pltpu.VMEM((dense_rows, LANES), F32)],
        compiler_params=params,
        name="forward",
    )(starts, trial_block, where, cas_three)
    gathered = lax.all_to_all(mixed, "fft", 0, 0, tiled=True)
    gathered = gathered.reshape(fft_size, planes, bands, LANES)
    block = pl.BlockSpec((fft_size, 1, bands, LANES), lambda z: (0, z, 0, 0))
    tables = (inverse, box, y_three, x_three, x_back, y_back)
    weighted = pl.pallas_call(
        functools.partial(plane_kernel, bands, fft_size),
        out_shape=f32(gathered.shape),
        grid=(planes,),
        in_specs=[whole(one) for one in tables]
        + [pl.BlockSpec((1, grid_cells, grid_cells), lambda z: (z, 0, 0)), block],
        out_specs=block,
        scratch_shapes=[pltpu.VMEM((fft_size * bands, LANES), F32)],
        compiler_params=params,
        name="planes",
    )(*tables, potential, gathered)
    returned = lax.all_to_all(weighted.reshape(dense_rows, LANES), "fft", 0, 0, tiled=True)
    return pl.pallas_call(
        functools.partial(backward_kernel, bands, grid_cells),
        out_shape=f32((bands, coefs)),
        in_specs=[smem] + [vmem] * 5,
        out_specs=vmem,
        scratch_shapes=[pltpu.VMEM((dense_rows, LANES), F32)],
        compiler_params=params,
        name="backward",
    )(starts, trial_block, slots, own, cas_three, returned)


def contract(all_bands, block):
    gathered = lax.all_gather(block, "band", axis=0, tiled=True)
    products = jnp.einsum("ag,bg->ab", all_bands, gathered, precision=lax.Precision.HIGH)
    parts = lax.all_to_all(products, "fft", 0, 0, tiled=True)
    rows = all_bands.shape[0] // lax.axis_size("fft")
    return jnp.sum(parts.reshape(-1, rows, parts.shape[1]), axis=0)


def per_device(trial_block, all_bands, potential, positions, sphere_slots):
    intersection = contract(all_bands, trial_block)
    applied = apply_hamiltonian(trial_block, potential, positions, sphere_slots)
    projected = contract(all_bands, applied)
    return (intersection, projected)


def solution(mesh):
    placed = (P("band", "fft"), P("band", "fft"), P("fft", None, None), P(), P("fft"))
    return jax.shard_map(
        per_device,
        mesh=mesh,
        in_specs=placed,
        out_specs=(P(("band", "fft"), None), P(("band", "fft"), None)),
        check_vma=False,
    )
```

time: 1140 us -> 324 us (0.28)
  the two profiles are of different devices: /device:TPU:8 before, /device:TPU:1 now
where the time goes in v1:
time: 324 us; the launch traced here: 323 us
  waiting for transfers between devices  195 us (60%)
  Pallas kernels  65.5 us (20%)
  starting transfers between devices  31.4 us (10%)
  between operations  14.2 us (4%)
  matrix products  8.42 us (3%)
  local copies, waits for them, and re-layouts  7.99 us (2%)
    all_gather x2, waiting for transfers between devices, contract(): gathered = lax.all_gather(block, 'band', axis=0, tiled=True)  96.6 us
    pallas_call x1, Pallas kernels, apply_hamiltonian(): pl.pallas_call(functools.partial(plane_kernel, bands, fft_size), out_shap...  51.2 us
    all_to_all x1, waiting for transfers between devices, apply_hamiltonian(): gathered = lax.all_to_all(mixed, 'fft', 0, 0, tiled=True)  47.7 us
    all_to_all x1, waiting for transfers between devices, apply_hamiltonian(): lax.all_to_all(weighted.reshape(dense_rows, LANES), 'fft', 0, 0, tiled=True)  38.9 us
    all_to_all x1, starting transfers between devices, apply_hamiltonian(): gathered = lax.all_to_all(mixed, 'fft', 0, 0, tiled=True)  16.1 us
    all_to_all x2, starting transfers between devices, contract(): parts = lax.all_to_all(products, 'fft', 0, 0, tiled=True)  10.8 us
    all_to_all x2, waiting for transfers between devices, contract(): parts = lax.all_to_all(products, 'fft', 0, 0, tiled=True)  10.8 us
    dot_general x2, matrix products, contract(): jnp.einsum('ag,bg->ab', all_bands, gathered, precision=lax.Precision.HIGH)  8.42 us
  transfers between devices with their start and end apart: 6, of which 4 were waited for; matrix products, arithmetic and copies ran while one was open for 3% of the time, Pallas kernels for 18%

profile of v1, /device:TPU:1, one launch (start us, length us, event | category | flops | bytes accessed | tf_op | source)
XLA Modules:
  0.0 323.3 jit_solution(2749833870480883697)
XLA Ops:
  7.2 0.8 copy-done.8
  8.0 0.7 copy-done.14
  8.7 2.7 tables.1
  12.0 0.9 copy-done.1
  13.0 0.9 copy-done.4
  13.9 4.6 %forward.1 = f32[1536,128]{1,0:T(8,128)} custom-call(s32[192]{0:T(256)S(1)} %slice_reduce_fusion.starts, f32[8,6272]{1,0:T(8,128)S(1)} %copy-done.1, s32[192,128]{1,0:T(8,128)S(1)} %get-tuple-element.9.where_ref, bf16[192,576]{1,0:T(8,128)(2,1)S(1)} %copy-done.4), custom_call_target="tpu_custom_call" | custom-call | tf_op jit(solution)/shard_map/forward/pallas_call | solution.py:310
  18.6 16.1 %all-to-all-start.1 = ((f32[32,48,128]{2,1,0:T(8,128)}), f32[32,48,128]{2,1,0:T(8,128)S(1)}, u32[]{:S(2)}, u32[]{:S(2)}) async-start(f32[32,48,128]{2,1,0:T(8,128)} %bitcast.5), calls=%async_computation.1 | async-start | bytes 1572864 | tf_op jit(solution)/shard_map/all_to_all | solution.py:319
  34.7 0.7 all-gather.3.cloned.1.call-update
  35.4 47.7 %all-to-all-done.1 = f32[32,48,128]{2,1,0:T(8,128)S(1)} async-done(((f32[32,48,128]{2,1,0:T(8,128)}), f32[32,48,128]{2,1,0:T(8,128)S(1)}, u32[]{:S(2)}, u32[]{:S(2)}) %all-to-all-start.1) | async-done | bytes 786464 | tf_op jit(solution)/shard_map/all_to_all | solution.py:319
  83.1 1.0 copy-done.6
  84.1 0.8 copy-done.11
  85.0 0.8 copy-done.13
  85.7 51.2 %planes.1 = f32[32,6,8,128]{3,2,1,0:T(8,128)} custom-call(s32[64,128]{1,0:T(8,128)S(1)} %copy-done.13, s32[32,128]{1,0:T(8,128)S(1)} %get-tuple-element.8.box_ref, bf16[384,512]{1,0:T(8,128)(2,1)S(1)} %copy-done.6, bf16[192,192]{1,0:T(8,128)(2,1)S(1)} %copy-done.10, bf16[128,192]{1,0:T(8,128)(2,1)S(1)} %copy-done.11, bf16[2,2,192,128]{3,2,1,0:T(8,128)(2,1)S(1)} %copy-done.7, ...), custom_call_target="tpu_custom_call" | custom-call | tf_op jit(solution)/shard_map/planes/pallas_call | solution.py:323
  137.0 4.5 %all-to-all-start.2 = ((f32[32,48,128]{2,1,0:T(8,128)}), f32[32,48,128]{2,1,0:T(8,128)S(1)}, u32[]{:S(2)}, u32[]{:S(2)}) async-start(f32[32,48,128]{2,1,0:T(8,128)} %bitcast.7), calls=%async_computation.2 | async-start | bytes 1572864 | tf_op jit(solution)/shard_map/all_to_all | solution.py:334
  141.5 0.7 constant_dynamic-slice_fusion.own_ref
  142.2 38.9 %all-to-all-done.2 = f32[32,48,128]{2,1,0:T(8,128)S(1)} async-done(((f32[32,48,128]{2,1,0:T(8,128)}), f32[32,48,128]{2,1,0:T(8,128)S(1)}, u32[]{:S(2)}, u32[]{:S(2)}) %all-to-all-start.2) | async-done | bytes 786464 | tf_op jit(solution)/shard_map/all_to_all | solution.py:334
  181.1 0.6 copy-done.16
  181.7 7.0 %backward.1 = f32[8,6272]{1,0:T(8,128)} custom-call(s32[192]{0:T(256)S(1)} %copy-done.16, f32[8,6272]{1,0:T(8,128)S(1)} %copy-done.2, s32[49,128]{1,0:T(8,128)S(1)} %bitcast.23, s32[1,128]{1,0:T(1,128)S(1)} %constant_dynamic-slice_fusion.own_ref, bf16[192,576]{1,0:T(8,128)(2,1)S(1)} %copy-done.5, f32[1536,128]{1,0:T(8,128)S(1)} %bitcast.21), custom_call_target="tpu_custom_call" | custom-call | tf_op jit(solution)/shard_map/backward/pallas_call | solution.py:335
  188.8 4.2 %fusion = f32[32,128]{1,0:T(8,128)} fusion(f32[32,6272]{1,0:T(8,128)S(1)} %copy-done, f32[128,6272]{1,0:T(8,128)} %all-gather.3.cloned.1.call-done), kind=kOutput, calls=%fused_computation.2 | convolution fusion | flops 154140672 | bytes 4030464 | tf_op jit(solution)/shard_map/ag,bg->ab/dot_general | solution.py:348
  193.0 5.6 %all-to-all-start = ((f32[32,1,128]{2,1,0:T(1,128)}), f32[32,1,128]{2,1,0:T(1,128)S(1)}, u32[]{:S(2)}, u32[]{:S(2)}) async-start(f32[32,1,128]{2,1,0:T(1,128)} %bitcast.1), calls=%async_computation | async-start | bytes 32768 | tf_op jit(solution)/shard_map/all_to_all | solution.py:349
  198.6 96.5 %all-gather.5.cloned.1.call-done = f32[128,6272]{1,0:T(8,128)} async-done(((f32[8,6272]{1,0:T(8,128)}), f32[128,6272]{1,0:T(8,128)}) %all-gather.5.cloned.1.call-update) | async-done | bytes 3211280 | tf_op jit(solution)/shard_map/all_gather | solution.py:347
  295.1 4.2 %fusion.1 = f32[128,32]{0,1:T(8,128)} fusion(f32[128,6272]{1,0:T(8,128)} %all-gather.5.cloned.1.call-done, f32[32,6272]{1,0:T(8,128)S(1)} %copy-done), kind=kOutput, calls=%fused_computation.3 | convolution fusion | flops 154140672 | bytes 4030464 | tf_op jit(solution)/shard_map/ag,bg->ab/dot_general | solution.py:348
  299.3 5.2 %all-to-all-start.3 = ((f32[32,1,128]{2,1,0:T(1,128)}), f32[32,1,128]{2,1,0:T(1,128)S(1)}, u32[]{:S(2)}, u32[]{:S(2)}) async-start(f32[32,1,128]{2,1,0:T(1,128)} %bitcast.11), calls=%async_computation.3 | async-start | bytes 32768 | tf_op jit(solution)/shard_map/all_to_all | solution.py:349
  305.1 10.8 %all-to-all-done.3 = f32[32,1,128]{2,1,0:T(1,128)S(1)} async-done(((f32[32,1,128]{2,1,0:T(1,128)}), f32[32,1,128]{2,1,0:T(1,128)S(1)}, u32[]{:S(2)}, u32[]{:S(2)}) %all-to-all-start.3) | async-done | bytes 16416 | tf_op jit(solution)/shard_map/all_to_all | solution.py:349
  (34 shorter events, 1.9 us)
Async XLA Ops:
  7.2 181.6 %copy-start = (f32[32,6272]{1,0:T(8,128)S(1)}, f32[32,6272]{1,0:T(8,128)}, u32[]{:S(2)}) copy-start(f32[32,6272]{1,0:T(8,128)} %param.11) | copy-start | bytes 2408452
  7.2 0.8 copy-start.8
  8.0 0.7 copy-start.14
  8.7 74.4 %copy-start.10 = (bf16[192,192]{1,0:T(8,128)(2,1)S(1)}, bf16[192,192]{1,0:T(8,128)(2,1)}, u32[]{:S(2)}) copy-start(bf16[192,192]{1,0:T(8,128)(2,1)} %constant.22.clone.x_ref) | copy-start | bytes 221188
  11.4 0.6 copy-start.12
  12.0 6.5 %copy-start.15 = (s32[192]{0:T(256)}, s32[192]{0:T(256)S(1)}, u32[]{:S(2)}) copy-start(s32[192]{0:T(256)S(1)} %slice_reduce_fusion.starts) | copy-start | bytes 2308
  12.0 0.9 copy-start.1
  13.0 0.9 copy-start.4
  13.9 69.2 %copy-start.3 = (f32[6,192,192]{2,1,0:T(8,128)S(1)}, f32[6,192,192]{2,1,0:T(8,128)}, u32[]{:S(2)}) copy-start(f32[6,192,192]{2,1,0:T(8,128)} %potential_ref.1) | copy-start | bytes 2654212
  13.9 69.2 %copy-start.7 = (bf16[2,2,192,128]{3,2,1,0:T(8,128)(2,1)S(1)}, bf16[2,2,192,128]{3,2,1,0:T(8,128)(2,1)}, u32[]{:S(2)}) copy-start(bf16[2,2,192,128]{3,2,1,0:T(8,128)(2,1)} %constant.24.clone.y_back_ref) | copy-start | bytes 589828
  18.6 162.5 %copy-start.2 = (f32[8,6272]{1,0:T(8,128)S(1)}, f32[8,6272]{1,0:T(8,128)}, u32[]{:S(2)}) copy-start(f32[8,6272]{1,0:T(8,128)} %trial_ref.3) | copy-start | bytes 602116
  18.6 162.5 %copy-start.5 = (bf16[192,576]{1,0:T(8,128)(2,1)S(1)}, bf16[192,576]{1,0:T(8,128)(2,1)}, u32[]{:S(2)}) copy-start(bf16[192,576]{1,0:T(8,128)(2,1)} %constant.20.clone.cas_ref) | copy-start | bytes 663556
  18.6 162.5 %copy-start.9 = (s32[6272]{0:T(1024)S(1)}, s32[6272]{0:T(1024)}, u32[]{:S(2)}) copy-start(s32[6272]{0:T(1024)} %param.14) | copy-start | bytes 75268
  18.6 64.5 %all-to-all-start.1 = ((f32[32,48,128]{2,1,0:T(8,128)}), f32[32,48,128]{2,1,0:T(8,128)S(1)}, u32[]{:S(2)}, u32[]{:S(2)}) async-start(f32[32,48,128]{2,1,0:T(8,128)} %bitcast.5), calls=%async_computation.1 | async-start | bytes 1572864 | tf_op jit(solution)/shard_map/all_to_all | solution.py:319
  34.6 154.1 %all-gather.3.cloned.1.call-start = ((), (), s32[]{:S(2)}) async-start(), calls=%async_computation.4 | async-start | bytes 3411968 | tf_op jit(solution)/shard_map/all_gather | solution.py:347
  83.1 1.0 copy-start.6
  84.1 0.8 copy-start.11
  85.0 0.8 copy-start.13
  137.0 44.1 %all-to-all-start.2 = ((f32[32,48,128]{2,1,0:T(8,128)}), f32[32,48,128]{2,1,0:T(8,128)S(1)}, u32[]{:S(2)}, u32[]{:S(2)}) async-start(f32[32,48,128]{2,1,0:T(8,128)} %bitcast.7), calls=%async_computation.2 | async-start | bytes 1572864 | tf_op jit(solution)/shard_map/all_to_all | solution.py:334
  141.4 153.7 %all-gather.5.cloned.1.call-start = ((), (), s32[]{:S(2)}) async-start(), calls=%async_computation.5 | async-start | bytes 3411968 | tf_op jit(solution)/shard_map/all_gather | solution.py:347
  181.1 0.7 copy-start.16
  193.0 106.3 %all-to-all-start = ((f32[32,1,128]{2,1,0:T(1,128)}), f32[32,1,128]{2,1,0:T(1,128)S(1)}, u32[]{:S(2)}, u32[]{:S(2)}) async-start(f32[32,1,128]{2,1,0:T(1,128)} %bitcast.1), calls=%async_computation | async-start | bytes 32768 | tf_op jit(solution)/shard_map/all_to_all | solution.py:349
  299.3 16.6 %all-to-all-start.3 = ((f32[32,1,128]{2,1,0:T(1,128)}), f32[32,1,128]{2,1,0:T(1,128)S(1)}, u32[]{:S(2)}, u32[]{:S(2)}) async-start(f32[32,1,128]{2,1,0:T(1,128)} %bitcast.11), calls=%async_computation.3 | async-start | bytes 32768 | tf_op jit(solution)/shard_map/all_to_all | solution.py:349
Sparse Core Ops, SparseCore 0:
  38.7 113.9 all-gather.2
  188.9 106.1 all-gather.4

commit v2 on v1

--- a/solution.py
+++ b/solution.py
@@ -7,10 +7,16 @@
 from jax import lax
 from jax.experimental import pallas as pl
 from jax.experimental.pallas import tpu as pltpu
+from jax.sharding import Mesh
 from jax.sharding import PartitionSpec as P
 
 K = 64
 LANES = 128
+SIZES = (4, 2, 2, 4, 8)
+BAND = ("y", "zh", "c")
+FFT = ("x", "zl")
+SIDE = ("y", "c")
+NEAR = ("y", "c", "x")
 F32 = jnp.float32
 BF16 = jnp.bfloat16
 
@@ -128,9 +134,17 @@
             ]
 
 
+def potential_kernel(filter_ref, filter_t_ref, potential_ref, out_ref):
+    for plane in range(potential_ref.shape[0]):
+        high, low = split(potential_ref[plane])
+        rows = dot(filter_ref[...], jnp.concatenate([high, low, high], axis=0))
+        high, low = split(rows)
+        out_ref[plane] = (
+            dot(high, filter_t_ref[0]) + dot(low, filter_t_ref[0]) + dot(high, filter_t_ref[1])
+        )
+
+
 def plane_kernel(
-    bands,
-    sources,
     inverse_ref,
     box_ref,
     y_ref,
@@ -142,61 +156,72 @@
     out_ref,
     boxes,
 ):
-    grid_cells = potential_ref.shape[1]
+    sources, planes, bands = columns_ref.shape[:3]
     blocks = sources
 
     def fill(block, carry):
         source_of = jnp.broadcast_to(inverse_ref[pl.ds(block, 1), :], (bands, LANES))
         lane_of = jnp.broadcast_to(inverse_ref[pl.ds(block + blocks, 1), :], (bands, LANES))
-        value = jnp.zeros((bands, LANES), F32)
+        values = [jnp.zeros((bands, LANES), F32) for _ in range(planes)]
         for source in range(sources):
-            value = jnp.where(
-                source_of == source, take_lanes(columns_ref[source, 0], lane_of), value
-            )
-        boxes[pl.ds(pl.multiple_of(block * bands, bands), bands), :] = value
+            here = source_of == source
+            for plane in range(planes):
+                values[plane] = jnp.where(
+                    here, take_lanes(columns_ref[source, plane], lane_of), values[plane]
+                )
+        for plane in range(planes):
+            boxes[plane, pl.ds(pl.multiple_of(block * bands, bands), bands), :] = values[plane]
         return carry
 
     lax.fori_loop(0, blocks, fill, 0)
-    stacked = jnp.concatenate(
-        [boxes[pl.ds(band, blocks, stride=bands), :] for band in range(bands)], axis=0
-    )
-    high, low = split(stacked)
-    wide = dot(jnp.concatenate([high, low, high], axis=1), y_ref[...])
-    half_width = wide.shape[1] // 2
-    potential = potential_ref[0]
-    back = []
-    for band in range(bands):
-        mine = wide[band * blocks : (band + 1) * blocks, :]
-        mine = jnp.concatenate([mine[:, :half_width], mine[:, half_width:]], axis=0)
-        high, low = split(mine)
-        field = dot(x_ref[...], jnp.concatenate([high, low, high], axis=0))
-        high, low = split(field[:, :grid_cells] * potential)
-        both = dot(x_back_ref[...], high)
-        back.append(both[:K] + both[K:] + dot(x_back_ref[:K, :], low))
-    total = None
-    for side in range(2):
-        part = jnp.concatenate(
-            [one[side * blocks : (side + 1) * blocks, :] for one in back], axis=0
+
+    def transform(plane, carry):
+        stacked = jnp.concatenate(
+            [boxes[plane, pl.ds(band, blocks, stride=bands), :] for band in range(bands)], axis=0
         )
-        high, low = split(part)
-        term = dot(high, y_back_ref[side, 0]) + dot(low, y_back_ref[side, 0])
-        term = term + dot(high, y_back_ref[side, 1])
-        total = term if total is None else total + term
-    for band in range(bands):
-        boxes[pl.ds(band, blocks, stride=bands), :] = total[band * blocks : (band + 1) * blocks, :]
+        high, low = split(stacked)
+        wide = dot(jnp.concatenate([high, low, high], axis=1), y_ref[...])
+        potential = potential_ref[plane]
+        potential = jnp.concatenate([potential, potential], axis=1)
+        back = []
+        for band in range(0, bands, 2):
+            pair = []
+            for one in (band, band + 1):
+                mine = wide[one * blocks : (one + 1) * blocks, :]
+                pair.append(jnp.concatenate([mine[:, :LANES], mine[:, LANES:]], axis=0))
+            high, low = split(jnp.concatenate(pair, axis=1))
+            field = dot(x_ref[...], jnp.concatenate([high, low, high], axis=0))
+            high, low = split(field * potential)
+            both = dot(x_back_ref[...], high)
+            both = both[:K] + both[K:] + dot(x_back_ref[:K, :], low)
+            for side in range(2):
+                one = both[:, side * LANES : (side + 1) * LANES]
+                back.append(jnp.concatenate([one[:blocks], one[blocks:]], axis=1))
+        high, low = split(jnp.concatenate(back, axis=0))
+        total = dot(high, y_back_ref[0]) + dot(low, y_back_ref[0]) + dot(high, y_back_ref[1])
+        for band in range(bands):
+            boxes[plane, pl.ds(band, blocks, stride=bands), :] = total[
+                band * blocks : (band + 1) * blocks, :
+            ]
+        return carry
+
+    lax.fori_loop(0, planes, transform, 0)
 
     def pick(source, carry):
         place = jnp.broadcast_to(box_ref[pl.ds(source, 1), :], (bands, LANES))
         lane_of = place & (LANES - 1)
         block_of = lax.shift_right_logical(place, 7)
-        value = jnp.zeros((bands, LANES), F32)
+        values = [jnp.zeros((bands, LANES), F32) for _ in range(planes)]
         for block in range(blocks):
-            value = jnp.where(
-                block_of == block,
-                take_lanes(boxes[block * bands : (block + 1) * bands, :], lane_of),
-                value,
-            )
-        out_ref[source, 0] = value
+            here = block_of == block
+            for plane in range(planes):
+                values[plane] = jnp.where(
+                    here,
+                    take_lanes(boxes[plane, block * bands : (block + 1) * bands, :], lane_of),
+                    values[plane],
+                )
+        for plane in range(planes):
+            out_ref[source, plane] = values[plane]
         return carry
 
     lax.fori_loop(0, sources, pick, 0)
@@ -213,6 +238,7 @@
     returned_ref,
     out_ref,
     dense,
+    packed,
 ):
     for band in range(0, bands, 2):
         pair = jnp.concatenate(
@@ -226,15 +252,7 @@
                 :, side * LANES : (side + 1) * LANES
             ]
     rows = slots_ref.shape[0]
-    first, second = column_box(own_ref[...], grid_cells)
-    radial = jnp.broadcast_to((first * first + second * second).astype(F32), (bands, LANES))
-    for row in range(rows):
-        slots = jnp.broadcast_to(slots_ref[row : row + 1, :], (bands, LANES))
-        height = wrapped(lax.shift_right_logical(slots, 7), grid_cells)
-        around = take_lanes(radial, slots & (LANES - 1))
-        kinetic = 2.0 * (around + (height * height).astype(F32)) / (K * K)
-        cut = slice(row * LANES, (row + 1) * LANES)
-        out_ref[:, cut] = kinetic * trial_ref[:, cut]
+    packed[...] = jnp.zeros_like(packed)
 
     def compact(height, carry):
         values = dense[pl.ds(pl.multiple_of(height * bands, bands), bands), :]
@@ -245,50 +263,68 @@
                 near = jnp.minimum(near, rows - 1)
             slots = jnp.broadcast_to(slots_ref[pl.ds(near, 1), :], (bands, LANES))
             mask = lax.shift_right_logical(slots, 7) == height
-            if step:
-                mask = mask & (near > row)
-            cut = pl.ds(pl.multiple_of(near * LANES, LANES), LANES)
-            out_ref[:, cut] += jnp.where(mask, take_lanes(values, slots & (LANES - 1)), 0.0)
+            packed[near] = jnp.where(mask, take_lanes(values, slots & (LANES - 1)), packed[near])
         return carry
 
     lax.fori_loop(0, grid_cells, compact, 0, unroll=4)
+    first, second = column_box(own_ref[...], grid_cells)
+    radial = jnp.broadcast_to((first * first + second * second).astype(F32), (bands, LANES))
+    parts, _, width = out_ref.shape
+    each = width // LANES
+    for row in range(parts * each):
+        cut = slice(row % each * LANES, (row % each + 1) * LANES)
+        if row >= rows:
+            out_ref[row // each, :, cut] = jnp.zeros((bands, LANES), F32)
+            continue
+        slots = jnp.broadcast_to(slots_ref[row : row + 1, :], (bands, LANES))
+        height = wrapped(lax.shift_right_logical(slots, 7), grid_cells)
+        around = take_lanes(radial, slots & (LANES - 1))
+        kinetic = 2.0 * (around + (height * height).astype(F32)) / (K * K)
+        trial = trial_ref[:, row * LANES : (row + 1) * LANES]
+        out_ref[row // each, :, cut] = packed[row] + kinetic * trial
 
 
 def constant_tables(grid_cells):
-    cas = cas_matrix(grid_cells)
-    box_table = cas[(np.arange(K) - K // 2) % grid_cells]
-    high, low = halves(cas)
-    cas_three = np.concatenate([high, high, low], axis=1)
-    padded = -(-grid_cells // LANES) * LANES
-    sides = np.zeros((2, K, 2, padded), np.float32)
+    fine = 2 * K
+    cas_three = np.concatenate([halves(cas_matrix(grid_cells))[i] for i in (0, 0, 1)], axis=1)
+    theta = (np.arange(fine) + 0.5) / fine
+    full = np.arange(grid_cells) / grid_cells
+    box = np.arange(K) - K // 2
+    angle = 2.0 * math.pi * box[:, None] * theta[None, :]
+    box_table = ((np.cos(angle) + np.sin(angle)) / math.sqrt(fine)).astype(np.float32)
+    waves = 2.0 * math.pi * np.arange(1, K)
+    apart = theta[:, None] - full[None, :]
+    project = 1.0 + 2.0 * np.cos(waves[:, None, None] * apart[None]).sum(axis=0)
+    edge = 2.0 * math.pi * K
+    project = project + np.sin(edge * theta)[:, None] * np.sin(edge * full)[None, :]
+    project = (project / grid_cells).astype(np.float32)
+    high, low = halves(project)
+    filter_three = np.concatenate([high, high, low], axis=1)
+    filter_back = np.stack([high.T, low.T])
+    sides = np.zeros((2, K, 2, fine), np.float32)
     for side in range(2):
-        sides[side, :, side, :grid_cells] = box_table
-    high, low = halves(sides.reshape(2 * K, 2 * padded))
+        sides[side, :, side, :] = box_table
+    high, low = halves(sides.reshape(2 * K, 2 * fine))
     y_three = np.concatenate([high, high, low], axis=0)
+    y_back = np.stack([high.T, low.T])
     order = np.concatenate([np.arange(0, K, 2), np.arange(1, K, 2)])
     high, low = halves(box_table[order])
     x_three = np.concatenate([high, high, low], axis=0).T
     x_back = np.concatenate([high, low], axis=0)
-    back = np.zeros((2, grid_cells, 2, K), np.float32)
-    for side in range(2):
-        back[side, :, side, :] = box_table.T
-    high, low = halves(back.reshape(2, grid_cells, 2 * K))
-    y_back = np.stack([high, low], axis=1)
-    return tuple(jnp.asarray(one) for one in (cas_three, y_three, x_three, x_back, y_back))
-
-
-def whole(array):
-    return pl.BlockSpec(array.shape, lambda *_: (0,) * array.ndim)
-
-
-def apply_hamiltonian(trial_block, potential, positions, sphere_slots):
+    tables = (cas_three, filter_three, filter_back, y_three, x_three, x_back, y_back)
+    return tuple(jnp.asarray(one) for one in tables)
+
+
+def apply_hamiltonian(trial_block, potential, positions, sphere_slots, pieces):
+    parts = pieces.shape[0]
     bands, coefs = trial_block.shape
     planes, grid_cells = potential.shape[:2]
-    fft_size = lax.axis_size("fft")
-    slots = sphere_slots.reshape(coefs // LANES, LANES)
+    fft_size = lax.axis_size(FFT)
+    rows = coefs // LANES
+    slots = sphere_slots.reshape(rows, LANES)
     position_rows = positions.reshape(fft_size, LANES)
-    own = lax.dynamic_slice_in_dim(position_rows, lax.axis_index("fft"), 1)
-    cas_three, y_three, x_three, x_back, y_back = constant_tables(grid_cells)
+    own = lax.dynamic_slice_in_dim(position_rows, lax.axis_index(FFT), 1)
+    cas_three, filter_three, filter_back, *plane_tables = constant_tables(grid_cells)
     i32 = functools.partial(jax.ShapeDtypeStruct, dtype=jnp.int32)
     f32 = functools.partial(jax.ShapeDtypeStruct, dtype=F32)
     params = pltpu.CompilerParams(vmem_limit_bytes=48 * 2**20)
@@ -316,54 +352,83 @@
         compiler_params=params,
         name="forward",
     )(starts, trial_block, where, cas_three)
-    gathered = lax.all_to_all(mixed, "fft", 0, 0, tiled=True)
+    filtered = pl.pallas_call(
+        potential_kernel,
+        out_shape=f32((planes, 2 * K, 2 * K)),
+        compiler_params=params,
+        cost_estimate=pl.CostEstimate(flops=4 * 10**9, bytes_accessed=4 * 10**6, transcendentals=0),
+        name="filter",
+    )(filter_three, filter_back, potential)
+    gathered = lax.all_to_all(mixed, FFT, 0, 0, tiled=True)
+    gathered, pieces = lax.optimization_barrier((gathered, pieces))
+    pieces = lax.all_to_all(pieces, SIDE, 0, 0, tiled=True)
     gathered = gathered.reshape(fft_size, planes, bands, LANES)
-    block = pl.BlockSpec((fft_size, 1, bands, LANES), lambda z: (0, z, 0, 0))
-    tables = (inverse, box, y_three, x_three, x_back, y_back)
     weighted = pl.pallas_call(
-        functools.partial(plane_kernel, bands, fft_size),
+        plane_kernel,
         out_shape=f32(gathered.shape),
-        grid=(planes,),
-        in_specs=[whole(one) for one in tables]
-        + [pl.BlockSpec((1, grid_cells, grid_cells), lambda z: (z, 0, 0)), block],
-        out_specs=block,
-        scratch_shapes=[pltpu.VMEM((fft_size * bands, LANES), F32)],
+        scratch_shapes=[pltpu.VMEM((planes, fft_size * bands, LANES), F32)],
         compiler_params=params,
+        cost_estimate=pl.CostEstimate(
+            flops=25 * 10**9, bytes_accessed=60 * 10**6, transcendentals=0
+        ),
         name="planes",
-    )(*tables, potential, gathered)
-    returned = lax.all_to_all(weighted.reshape(dense_rows, LANES), "fft", 0, 0, tiled=True)
-    return pl.pallas_call(
+    )(inverse, box, *plane_tables, filtered, gathered)
+    weighted, pieces = lax.optimization_barrier((weighted, pieces))
+    returned = lax.all_to_all(weighted.reshape(dense_rows, LANES), FFT, 0, 0, tiled=True)
+    width = pieces.shape[2]
+    joined = pl.pallas_call(
         functools.partial(backward_kernel, bands, grid_cells),
-        out_shape=f32((bands, coefs)),
+        out_shape=f32((parts, bands, width)),
         in_specs=[smem] + [vmem] * 5,
         out_specs=vmem,
-        scratch_shapes=[pltpu.VMEM((dense_rows, LANES), F32)],
+        scratch_shapes=[
+            pltpu.VMEM((dense_rows, LANES), F32),
+            pltpu.VMEM((rows, bands, LANES), F32),
+        ],
         compiler_params=params,
         name="backward",
     )(starts, trial_block, slots, own, cas_three, returned)
-
-
-def contract(all_bands, block):
-    gathered = lax.all_gather(block, "band", axis=0, tiled=True)
-    products = jnp.einsum("ag,bg->ab", all_bands, gathered, precision=lax.Precision.HIGH)
-    parts = lax.all_to_all(products, "fft", 0, 0, tiled=True)
-    rows = all_bands.shape[0] // lax.axis_size("fft")
-    return jnp.sum(parts.reshape(-1, rows, parts.shape[1]), axis=0)
+    return joined, pieces
+
+
+def other_half(block):
+    return lax.ppermute(block, "zh", ((0, 1), (1, 0)))
 
 
 def per_device(trial_block, all_bands, potential, positions, sphere_slots):
-    intersection = contract(all_bands, trial_block)
-    applied = apply_hamiltonian(trial_block, potential, positions, sphere_slots)
-    projected = contract(all_bands, applied)
-    return (intersection, projected)
+    parts = lax.axis_size(SIDE)
+    bands = trial_block.shape[0]
+    rows, coefs = all_bands.shape
+    width = -(-coefs // (LANES * parts)) * LANES
+    pieces = jnp.concatenate([all_bands, trial_block], axis=0)
+    pieces = jnp.pad(pieces, ((0, 0), (0, parts * width - coefs)))
+    pieces = pieces.reshape(rows + bands, parts, width).transpose(1, 0, 2)
+    applied, pieces = apply_hamiltonian(trial_block, potential, positions, sphere_slots, pieces)
+    trial = pieces[:, rows:].reshape(parts * bands, width)
+    pieces = pieces[:, :rows].reshape(parts * rows, width)
+    applied = lax.all_to_all(applied, SIDE, 0, 0, tiled=True).reshape(parts * bands, width)
+    products = []
+    for block in (trial, applied):
+        block = jnp.concatenate([block, other_half(block)], axis=0)
+        products.append(jnp.einsum("ag,bg->ab", pieces, block, precision=lax.Precision.HIGH))
+    products = jnp.concatenate(products, axis=1)
+    columns = products.shape[1]
+    near = lax.all_to_all(products, NEAR, 0, 0, tiled=True)
+    near = jnp.sum(near.reshape(lax.axis_size(NEAR), -1, columns), axis=0)
+    far = lax.all_to_all(near, "zl", 0, 0, tiled=True)
+    total = jnp.sum(far, axis=0).reshape(2, 2, SIZES[0], SIZES[2], bands)
+    total = jnp.where(lax.axis_index("zh") == 0, total, total[:, ::-1])
+    total = total.transpose(0, 2, 1, 3, 4).reshape(2, 1, -1)
+    return (total[0], total[1])
 
 
 def solution(mesh):
-    placed = (P("band", "fft"), P("band", "fft"), P("fft", None, None), P(), P("fft"))
+    axes = Mesh(mesh.devices.reshape(SIZES), ("y", "zh", "c", "x", "zl"))
+    placed = (P(BAND, FFT), P(BAND, FFT), P(FFT, None, None), P(), P(FFT))
     return jax.shard_map(
         per_device,
-        mesh=mesh,
+        mesh=axes,
         in_specs=placed,
-        out_specs=(P(("band", "fft"), None), P(("band", "fft"), None)),
+        out_specs=(P(BAND + FFT, None), P(BAND + FFT, None)),
         check_vma=False,
     )

time: 324 us -> 247 us (0.76)
  waiting for transfers between devices: 195 us -> 110 us
  starting transfers between devices: 31.4 us -> 65 us
  Pallas kernels: 65.5 us -> 41.2 us
  blocking collectives: 0 us -> 16.8 us
  between operations: 14.2 us -> 0.88 us
  matrix products: 8.42 us -> 1.07 us
    all_gather x2 -> x0, waiting for transfers between devices: 96.6 us -> none  [contract(): gathered = lax.all_gather(block, 'band', axis=0, tiled=True)]
    pallas_call x1 -> x2, Pallas kernels: 51.2 us -> 26.8 us  [the longest x1 25.7 us: apply_hamiltonian(): pl.pallas_call(plane_kernel, out_shape=f32(gathered.shape), scratch_shape...]
    all_to_all x4 -> x5, starting transfers between devices: 31.3 us -> 49.1 us  [the longest x1 15.9 us: apply_hamiltonian(): gathered = lax.all_to_all(mixed, FFT, 0, 0, tiled=True)]
    all_to_all x0 -> x1, blocking collectives: none -> 16.8 us  [per_device(): near = lax.all_to_all(products, NEAR, 0, 0, tiled=True)]
    ppermute x0 -> x2, starting transfers between devices: none -> 15.9 us  [other_half(): return lax.ppermute(block, 'zh', ((0, 1), (1, 0)))]
    ppermute x0 -> x2, waiting for transfers between devices: none -> 11.4 us  [other_half(): return lax.ppermute(block, 'zh', ((0, 1), (1, 0)))]
    dot_general x2, matrix products: 8.42 us -> 1.07 us  [per_device(): jnp.einsum('ag,bg->ab', pieces, block, precision=lax.Precision.HIGH)]
    unnamed x34 -> x31, local copies, waits for them, and re-layouts: 7.18 us -> 5.05 us
  transfers between devices with their start and end apart: 6 -> 7, of which waited for: 4 -> 5; matrix products, arithmetic and copies ran while one was open for 3% -> 1% of each run, Pallas kernels for 18% -> 14%
where the time goes in v2:
time: 247 us; the launch traced here: 246 us
  waiting for transfers between devices  110 us (45%)
  starting transfers between devices  65 us (26%)
  Pallas kernels  41.2 us (17%)
  blocking collectives  16.8 us (7%)
  local copies, waits for them, and re-layouts  10.5 us (4%)
    all_to_all x1, waiting for transfers between devices, apply_hamiltonian(): lax.all_to_all(weighted.reshape(dense_rows, LANES), FFT, 0, 0, tiled=True)  46.3 us
    all_to_all x1, waiting for transfers between devices, apply_hamiltonian(): gathered = lax.all_to_all(mixed, FFT, 0, 0, tiled=True)  36.9 us
    pallas_call x1, Pallas kernels, apply_hamiltonian(): pl.pallas_call(plane_kernel, out_shape=f32(gathered.shape), scratch_shape...  25.7 us
    all_to_all x1, blocking collectives, per_device(): near = lax.all_to_all(products, NEAR, 0, 0, tiled=True)  16.8 us
    all_to_all x1, starting transfers between devices, apply_hamiltonian(): gathered = lax.all_to_all(mixed, FFT, 0, 0, tiled=True)  15.9 us
    ppermute x2, starting transfers between devices, other_half(): return lax.ppermute(block, 'zh', ((0, 1), (1, 0)))  15.9 us
    all_to_all x1, starting transfers between devices, per_device(): far = lax.all_to_all(near, 'zl', 0, 0, tiled=True)  14.7 us
    ppermute x2, waiting for transfers between devices, other_half(): return lax.ppermute(block, 'zh', ((0, 1), (1, 0)))  11.4 us
  transfers between devices with their start and end apart: 7, of which 5 were waited for; matrix products, arithmetic and copies ran while one was open for 1% of the time, Pallas kernels for 14%

profile of v2, /device:TPU:1, one launch (start us, length us, event | category | flops | bytes accessed | tf_op | source)
XLA Modules:
  0.0 245.7 jit_solution(15985215427614283817)
XLA Ops:
  0.6 0.7 copy-done.4
  1.4 0.7 copy-done.6
  2.1 2.7 %tables.1 = (s32[192,128]{1,0:T(8,128)S(1)}, s32[192,128]{1,0:T(8,128)S(1)}, s32[64,128]{1,0:T(8,128)S(1)}, s32[32,128]{1,0:T(8,128)S(1)}) custom-call(s32[49,128]{1,0:T(8,128)S(1)} %bitcast.22, s32[32,128]{1,0:T(8,128)S(1)} %bitcast.25), custom_call_target="tpu_custom_call" | custom-call | tf_op jit(solution)/shard_map/tables/pallas_call | solution.py:331
  4.9 0.9 copy-done
  5.9 0.9 copy-done.2
  6.8 4.6 %forward.1 = f32[1536,128]{1,0:T(8,128)} custom-call(s32[192]{0:T(256)S(1)} %slice_reduce_fusion.starts, f32[8,6272]{1,0:T(8,128)S(1)} %copy-done, s32[192,128]{1,0:T(8,128)S(1)} %get-tuple-element.13.where_ref, bf16[192,576]{1,0:T(8,128)(2,1)S(1)} %copy-done.2), custom_call_target="tpu_custom_call" | custom-call | tf_op jit(solution)/shard_map/forward/pallas_call | solution.py:346
  11.4 15.9 %all-to-all-start = ((f32[32,48,128]{2,1,0:T(8,128)}), f32[32,48,128]{2,1,0:T(8,128)S(1)}, u32[]{:S(2)}, u32[]{:S(2)}) async-start(f32[32,48,128]{2,1,0:T(8,128)} %bitcast.2), calls=%async_computation | async-start | bytes 1572864 | tf_op jit(solution)/shard_map/all_to_all | solution.py:362
  27.5 1.3 copy.26
  29.2 1.1 filter.1.potential_ref
  30.3 36.9 %all-to-all-done = f32[32,48,128]{2,1,0:T(8,128)S(1)} async-done(((f32[32,48,128]{2,1,0:T(8,128)}), f32[32,48,128]{2,1,0:T(8,128)S(1)}, u32[]{:S(2)}, u32[]{:S(2)}) %all-to-all-start) | async-done | bytes 786464 | tf_op jit(solution)/shard_map/all_to_all | solution.py:362
  67.2 2.5 %copy.22 = f32[8,40,896]{2,1,0:T(8,128)} copy(f32[8,40,896]{2,0,1:T(8,128)} %bitcast.28) | data formatting | bytes 2293760 | tf_op jit(solution)/shard_map/optimization_barrier | solution.py:363
  69.7 6.4 %all-to-all-start.1 = ((f32[8,40,896]{2,1,0:T(8,128)}), f32[8,40,896]{2,1,0:T(8,128)S(1)}, u32[]{:S(2)}, u32[]{:S(2)}) async-start(f32[8,40,896]{2,1,0:T(8,128)} %copy.22), calls=%async_computation.1 | async-start | bytes 2293760 | tf_op jit(solution)/shard_map/all_to_all | solution.py:364
  76.1 25.7 %planes.1 = f32[32,6,8,128]{3,2,1,0:T(8,128)} custom-call(s32[64,128]{1,0:T(8,128)S(1)} %get-tuple-element.10.inverse_ref, s32[32,128]{1,0:T(8,128)S(1)} %get-tuple-element.11.box_ref, bf16[384,256]{1,0:T(8,128)(2,1)S(1)} %copy-done.8, bf16[128,192]{1,0:T(8,128)(2,1)S(1)} %copy-done.12, bf16[128,128]{1,0:T(8,128)(2,1)S(1)} %copy-done.13, ...), custom_call_target="tpu_custom_call" | custom-call | flops 24999999488 | bytes 60000000 | tf_op jit(solution)/shard_map/planes/pallas_call | solution.py:366
  101.8 5.3 %all-to-all-start.2 = ((f32[32,48,128]{2,1,0:T(8,128)}), f32[32,48,128]{2,1,0:T(8,128)S(1)}, u32[]{:S(2)}, u32[]{:S(2)}) async-start(f32[32,48,128]{2,1,0:T(8,128)} %bitcast.8), calls=%async_computation.2 | async-start | bytes 1572864 | tf_op jit(solution)/shard_map/all_to_all | solution.py:377
  107.2 7.9 %collective-permute-start = (f32[64,896]{1,0:T(8,128)S(1)}, f32[64,896]{1,0:T(8,128)S(1)}, u32[]{:S(2)}, u32[]{:S(2)}) collective-permute-start(f32[64,896]{1,0:T(8,128)S(1)} %slice_bitcast_fusion), channel_id=1, source_target_pairs={{0,64},{64,0},{1,65},{65,1},{2,66},{66,2},{3,67},{67,3},{4,68},{68... | collective-permute-start | bytes 688136 | tf_op jit(solution)/shard_map/ppermute | solution.py:395
  115.8 46.3 %all-to-all-done.2 = f32[32,48,128]{2,1,0:T(8,128)S(1)} async-done(((f32[32,48,128]{2,1,0:T(8,128)}), f32[32,48,128]{2,1,0:T(8,128)S(1)}, u32[]{:S(2)}, u32[]{:S(2)}) %all-to-all-start.2) | async-done | bytes 786464 | tf_op jit(solution)/shard_map/all_to_all | solution.py:377
  162.1 7.0 %backward.1 = f32[8,8,896]{2,1,0:T(8,128)} custom-call(s32[192]{0:T(256)S(1)} %slice_reduce_fusion.starts, f32[8,6272]{1,0:T(8,128)S(1)} %copy-done.1, s32[49,128]{1,0:T(8,128)S(1)} %bitcast.23, s32[1,128]{1,0:T(1,128)S(1)} %constant_dynamic-slice_fusion.own_ref, bf16[192,576]{1,0:T(8,128)(2,1)S(1)} %copy-done.3, f32[1536,128]{1,0:T(8,128)S(1)} %bitcast.20), custom_call_target="tpu_custom_call" | custom-call | tf_op jit(solution)/shard_map/backward/pallas_call | solution.py:379
  169.1 6.9 %all-to-all-start.3 = ((f32[8,8,896]{2,1,0:T(8,128)}), f32[8,8,896]{2,1,0:T(8,128)S(1)}, u32[]{:S(2)}, u32[]{:S(2)}) async-start(f32[8,8,896]{2,1,0:T(8,128)} %backward.1), calls=%async_computation.3 | async-start | bytes 458752 | tf_op jit(solution)/shard_map/all_to_all | solution.py:409
  176.1 6.1 %all-to-all-done.3 = f32[8,8,896]{2,1,0:T(8,128)S(1)} async-done(((f32[8,8,896]{2,1,0:T(8,128)}), f32[8,8,896]{2,1,0:T(8,128)S(1)}, u32[]{:S(2)}, u32[]{:S(2)}) %all-to-all-start.3) | async-done | bytes 229408 | tf_op jit(solution)/shard_map/all_to_all | solution.py:409
  182.2 7.9 %collective-permute-start.1 = (f32[64,896]{1,0:T(8,128)S(1)}, f32[64,896]{1,0:T(8,128)S(1)}, u32[]{:S(2)}, u32[]{:S(2)}) collective-permute-start(f32[64,896]{1,0:T(8,128)S(1)} %bitcast.31), channel_id=1, source_target_pairs={{0,64},{64,0},{1,65},{65,1},{2,66},{66,2},{3,67},{67,3},{4,68},{68... | collective-permute-start | bytes 688136 | tf_op jit(solution)/shard_map/ppermute | solution.py:395
  190.7 11.4 %collective-permute-done.1 = f32[64,896]{1,0:T(8,128)S(1)} collective-permute-done((f32[64,896]{1,0:T(8,128)S(1)}, f32[64,896]{1,0:T(8,128)S(1)}, u32[]{:S(2)}, u32[]{:S(2)}) %collective-permute-start.1) | collective-permute-done | bytes 229408 | tf_op jit(solution)/shard_map/ppermute | solution.py:395
  202.8 16.8 %all_to_all.51 = f32[32,8,256]{2,1,0:T(8,128)S(1)} all-to-all(f32[32,8,256]{2,1,0:T(8,128)S(1)} %bitcast.30), channel_id=1, replica_groups=mesh['y'=4,'zh'=2,'c'=2,'x'=4,'zl'=8] {'y','c','x'}, dimensions={0} | all-to-all | bytes 524288 | tf_op jit(solution)/shard_map/all_to_all | solution.py:416
  220.3 14.7 %all-to-all-start.5 = ((f32[8,1,256]{2,1,0:T(1,128)}), f32[8,1,256]{2,1,0:T(1,128)S(1)}, u32[]{:S(2)}, u32[]{:S(2)}) async-start(f32[8,1,256]{2,1,0:T(1,128)} %all_to_all.43), calls=%async_computation.5 | async-start | bytes 16384 | tf_op jit(solution)/shard_map/all_to_all | solution.py:418
  234.9 9.3 %all-to-all-done.5 = f32[8,1,256]{2,1,0:T(1,128)S(1)} async-done(((f32[8,1,256]{2,1,0:T(1,128)}), f32[8,1,256]{2,1,0:T(1,128)S(1)}, u32[]{:S(2)}, u32[]{:S(2)}) %all-to-all-start.5) | async-done | bytes 8224 | tf_op jit(solution)/shard_map/all_to_all | solution.py:418
  (47 shorter events, 4.7 us)
Async XLA Ops:
  0.6 0.8 copy-start.4
  1.4 0.7 copy-start.6
  4.9 0.9 copy-start
  5.9 0.9 copy-start.2
  6.8 20.6 %copy-start.1 = (f32[8,6272]{1,0:T(8,128)S(1)}, f32[8,6272]{1,0:T(8,128)}, u32[]{:S(2)}) copy-start(f32[8,6272]{1,0:T(8,128)} %trial_ref.3) | copy-start | bytes 602116
  6.8 20.6 %copy-start.14 = (f32[32,6272]{1,0:T(8,128)S(1)}, f32[32,6272]{1,0:T(8,128)}, u32[]{:S(2)}) copy-start(f32[32,6272]{1,0:T(8,128)} %param.13) | copy-start | bytes 2408452
  11.4 55.8 %all-to-all-start = ((f32[32,48,128]{2,1,0:T(8,128)}), f32[32,48,128]{2,1,0:T(8,128)S(1)}, u32[]{:S(2)}, u32[]{:S(2)}) async-start(f32[32,48,128]{2,1,0:T(8,128)} %bitcast.2), calls=%async_computation | async-start | bytes 1572864 | tf_op jit(solution)/shard_map/all_to_all | solution.py:362
  27.5 1.5 copy-start.7
  27.5 1.6 copy-start.9
  27.5 1.7 copy-start.11
  69.7 6.4 %copy-start.8 = (bf16[384,256]{1,0:T(8,128)(2,1)S(1)}, bf16[384,256]{1,0:T(8,128)(2,1)}, u32[]{:S(2)}) copy-start(bf16[384,256]{1,0:T(8,128)(2,1)} %constant.40.clone.y_ref) | copy-start | bytes 589828
  69.7 6.4 %copy-start.10 = (bf16[2,256,128]{2,1,0:T(8,128)(2,1)S(1)}, bf16[2,256,128]{2,1,0:T(8,128)(2,1)}, u32[]{:S(2)}) copy-start(bf16[2,256,128]{2,1,0:T(8,128)(2,1)} %constant.43.clone.y_back_ref) | copy-start | bytes 393220
  69.7 6.4 %copy-start.12 = (bf16[128,192]{1,0:T(8,128)(2,1)S(1)}, bf16[128,192]{1,0:T(8,128)(2,1)}, u32[]{:S(2)}) copy-start(bf16[128,192]{1,0:T(8,128)(2,1)} %constant.41.clone.x_ref) | copy-start | bytes 147460
  69.7 6.4 %copy-start.13 = (bf16[128,128]{1,0:T(8,128)(2,1)S(1)}, bf16[128,128]{1,0:T(8,128)(2,1)}, u32[]{:S(2)}) copy-start(bf16[128,128]{1,0:T(8,128)(2,1)} %constant.42.clone.x_back_ref) | copy-start | bytes 98308
  69.7 32.1 %all-to-all-start.1 = ((f32[8,40,896]{2,1,0:T(8,128)}), f32[8,40,896]{2,1,0:T(8,128)S(1)}, u32[]{:S(2)}, u32[]{:S(2)}) async-start(f32[8,40,896]{2,1,0:T(8,128)} %copy.22), calls=%async_computation.1 | async-start | bytes 2293760 | tf_op jit(solution)/shard_map/all_to_all | solution.py:364
  101.8 60.2 %copy-start.3 = (bf16[192,576]{1,0:T(8,128)(2,1)S(1)}, bf16[192,576]{1,0:T(8,128)(2,1)}, u32[]{:S(2)}) copy-start(bf16[192,576]{1,0:T(8,128)(2,1)} %constant.37.clone.cas_ref) | copy-start | bytes 663556
  101.8 60.2 %copy-start.5 = (s32[6272]{0:T(1024)S(1)}, s32[6272]{0:T(1024)}, u32[]{:S(2)}) copy-start(s32[6272]{0:T(1024)} %param.16) | copy-start | bytes 75268
  101.8 60.2 %all-to-all-start.2 = ((f32[32,48,128]{2,1,0:T(8,128)}), f32[32,48,128]{2,1,0:T(8,128)S(1)}, u32[]{:S(2)}, u32[]{:S(2)}) async-start(f32[32,48,128]{2,1,0:T(8,128)} %bitcast.8), calls=%async_computation.2 | async-start | bytes 1572864 | tf_op jit(solution)/shard_map/all_to_all | solution.py:377
  107.2 83.0 %collective-permute-start = (f32[64,896]{1,0:T(8,128)S(1)}, f32[64,896]{1,0:T(8,128)S(1)}, u32[]{:S(2)}, u32[]{:S(2)}) collective-permute-start(f32[64,896]{1,0:T(8,128)S(1)} %slice_bitcast_fusion), channel_id=1, source_target_pairs={{0,64},{64,0},{1,65},{65,1},{2,66},{66,2},{3,67},{67,3},{4,68},{68... | collective-permute-start | bytes 688136 | tf_op jit(solution)/shard_map/ppermute | solution.py:395
  169.1 13.1 %all-to-all-start.3 = ((f32[8,8,896]{2,1,0:T(8,128)}), f32[8,8,896]{2,1,0:T(8,128)S(1)}, u32[]{:S(2)}, u32[]{:S(2)}) async-start(f32[8,8,896]{2,1,0:T(8,128)} %backward.1), calls=%async_computation.3 | async-start | bytes 458752 | tf_op jit(solution)/shard_map/all_to_all | solution.py:409
  182.2 19.9 %collective-permute-start.1 = (f32[64,896]{1,0:T(8,128)S(1)}, f32[64,896]{1,0:T(8,128)S(1)}, u32[]{:S(2)}, u32[]{:S(2)}) collective-permute-start(f32[64,896]{1,0:T(8,128)S(1)} %bitcast.31), channel_id=1, source_target_pairs={{0,64},{64,0},{1,65},{65,1},{2,66},{66,2},{3,67},{67,3},{4,68},{68... | collective-permute-start | bytes 688136 | tf_op jit(solution)/shard_map/ppermute | solution.py:395
  220.3 24.0 %all-to-all-start.5 = ((f32[8,1,256]{2,1,0:T(1,128)}), f32[8,1,256]{2,1,0:T(1,128)S(1)}, u32[]{:S(2)}, u32[]{:S(2)}) async-start(f32[8,1,256]{2,1,0:T(1,128)} %all_to_all.43), calls=%async_computation.5 | async-start | bytes 16384 | tf_op jit(solution)/shard_map/all_to_all | solution.py:418

commit v3 on v2

v3 whole, which is shorter than its diff:
```python
import functools
import math

import jax
import jax.numpy as jnp
import numpy as np
from jax import lax
from jax.experimental import pallas as pl
from jax.experimental.pallas import tpu as pltpu
from jax.sharding import Mesh
from jax.sharding import PartitionSpec as P

K = 64
LANES = 128
SIZES = (4, 2, 2, 4, 2, 4)
AXES = ("y", "zh", "c", "x", "l2", "ll")
BAND = ("y", "zh", "c")
FFT = ("x", "l2", "ll")
SIDE = ("y", "c")
NEAR = ("y", "c", "x")
GROUP = ("c", "x", "ll")
BLOCKS = 2
HALF = 4
GANG = BLOCKS * HALF
REACH_ROW, START_ROW, SLOT_ROW, ROWS = 196, 200, 204, 256
F32 = jnp.float32
BF16 = jnp.bfloat16


def cas_matrix(length):
    ids = np.arange(length)
    angle = (ids[:, None] * ids[None, :] % length) * (2.0 * math.pi / length)
    return ((np.cos(angle) + np.sin(angle)) / math.sqrt(length)).astype(np.float32)


def halves(table):
    high = table.astype(jnp.bfloat16)
    low = (table - high.astype(np.float32)).astype(jnp.bfloat16)
    return high, low


def split(values):
    high = values.astype(BF16)
    low = (values - high.astype(F32)).astype(BF16)
    return high, low


def dot(left, right):
    return jnp.dot(left, right, preferred_element_type=F32)


def wrapped(values, length):
    return jnp.where(values >= length // 2, values - length, values)


def take_lanes(row, lanes):
    return jnp.take_along_axis(row, lanes, axis=1, mode="promise_in_bounds")


def column_box(positions, grid_cells):
    first = lax.shift_right_logical(lax.shift_right_logical(positions, 6) * 43691, 17)
    second = positions - first * grid_cells
    return wrapped(first, grid_cells), wrapped(second, grid_cells)


def upper(size):
    ids = [lax.broadcasted_iota(jnp.int32, (size, size), axis) for axis in range(2)]
    return (ids[0] < ids[1]).astype(BF16)


def nt_dot(left, right):
    return lax.dot_general(left, right, (((1,), (1,)), ((), ())), preferred_element_type=F32)


def pack_kernel(
    grid_cells, half, slots_ref, positions_ref, trial_ref, own_ref, send_ref, inverse_ref, box_ref
):
    rows = slots_ref.shape[0]
    first_half = half[0] == 0
    column = slots_ref[...] & (LANES - 1)
    lane_ids = lax.broadcasted_iota(jnp.int32, (LANES, LANES), 0)
    ones = jnp.ones((8, LANES), BF16)
    total = jnp.zeros((8, LANES), F32)
    for row in range(rows):
        hit = (column[row : row + 1, :] == lane_ids).astype(BF16)
        total = total + nt_dot(ones, hit)
    reach = (total - 1.0) * 0.5
    padded = 2 * LANES
    height = lax.broadcasted_iota(jnp.int32, (padded, LANES), 0)
    away = jnp.abs(wrapped(height, grid_cells)).astype(F32)
    valid = ((away <= reach[0:1, :]) & (height < grid_cells)).astype(BF16)
    start = dot(nt_dot(ones, valid).astype(BF16), upper(padded))
    for row in range(rows):
        values = trial_ref[:, row * LANES : (row + 1) * LANES]
        own_ref[row * HALF : (row + 1) * HALF, :] = jnp.where(
            first_half, values[:HALF], values[HALF:]
        )
        send_ref[row * HALF : (row + 1) * HALF, :] = jnp.where(
            first_half, values[HALF:], values[:HALF]
        )
    own_slots = slots_ref[...].astype(F32)
    for packet_ref in (own_ref, send_ref):
        packet_ref[REACH_ROW : REACH_ROW + HALF, :] = reach[:HALF]
        packet_ref[START_ROW : START_ROW + 1, :] = start[:1, :LANES]
        packet_ref[START_ROW + 1 : START_ROW + 2, :] = start[:1, LANES:]
        packet_ref[START_ROW + 2 : SLOT_ROW, :] = jnp.zeros((2, LANES), F32)
        packet_ref[SLOT_ROW : SLOT_ROW + rows, :] = own_slots
        packet_ref[SLOT_ROW + rows :, :] = jnp.zeros((ROWS - SLOT_ROW - rows, LANES), F32)
    first, second = column_box(positions_ref[...], grid_cells)
    box = (first + K // 2) * K + second + K // 2
    box_ref[...] = box
    sources = positions_ref.shape[0]
    blocks = sources
    block_ids = lax.broadcasted_iota(jnp.int32, (blocks, LANES), 0)
    own_lane = lax.broadcasted_iota(jnp.int32, (blocks, LANES), 1).astype(F32)
    inverse = jnp.zeros((2 * blocks, LANES), F32)
    for source in range(sources):
        place = box[source : source + 1, :]
        in_block = lax.shift_right_logical(place, 7) == block_ids
        left = jnp.concatenate(
            [jnp.where(in_block, float(source), 0.0), jnp.where(in_block, own_lane, 0.0)], axis=0
        ).astype(BF16)
        right = ((place & (LANES - 1)) == lane_ids).astype(BF16)
        inverse = inverse + nt_dot(left, right)
    inverse_ref[...] = inverse.astype(jnp.int32)


def z_transform(cas_ref, source_ref, out_ref, grid_cells):
    for block in range(0, GANG, 2):
        pair = jnp.concatenate(
            [source_ref[pl.ds(block + side, grid_cells, stride=GANG), :] for side in range(2)],
            axis=1,
        )
        high, low = split(pair)
        mixed = dot(cas_ref[...], jnp.concatenate([high, low, high], axis=0))
        for side in range(2):
            out_ref[pl.ds(block + side, grid_cells, stride=GANG), :] = mixed[
                :, side * LANES : (side + 1) * LANES
            ]


def forward_kernel(grid_cells, starts, packet_ref, cas_ref, out_ref, places, dense):
    height = lax.broadcasted_iota(jnp.int32, (grid_cells, LANES), 0)
    away = jnp.abs(wrapped(height, grid_cells)).astype(F32)
    ids = [lax.broadcasted_iota(jnp.int32, (grid_cells, grid_cells), axis) for axis in range(2)]
    below = (ids[0] > ids[1]).astype(BF16)
    before = upper(LANES)
    every = jnp.ones((LANES, LANES), BF16)
    for block in range(BLOCKS):
        row = block * ROWS + REACH_ROW
        valid = away <= packet_ref[row : row + 1, :]
        valid_one = valid.astype(BF16)
        rank = dot(valid_one, before).astype(jnp.int32)
        start = dot(below, dot(valid_one, every).astype(BF16)).astype(jnp.int32)
        place = jnp.where(valid, rank + (start & (LANES - 1)), -1)
        for band in range(HALF):
            places[pl.ds(block * HALF + band, grid_cells, stride=GANG), :] = place

    def expand(height, carry):
        rows = [
            block * ROWS + lax.shift_right_logical(starts[block, height], 7) * HALF
            for block in range(BLOCKS)
        ]
        rows = [pl.multiple_of(row, HALF) for row in rows]
        here = jnp.concatenate([packet_ref[pl.ds(row, HALF), :] for row in rows], axis=0)
        there = jnp.concatenate([packet_ref[pl.ds(row + HALF, HALF), :] for row in rows], axis=0)
        cut = pl.ds(pl.multiple_of(height * GANG, GANG), GANG)
        place = places[cut, :]
        lanes = place & (LANES - 1)
        value = jnp.where(place < LANES, take_lanes(here, lanes), take_lanes(there, lanes))
        dense[cut, :] = jnp.where(place < 0, 0.0, value)
        return carry

    lax.fori_loop(0, grid_cells, expand, 0, unroll=4)
    z_transform(cas_ref, dense, out_ref, grid_cells)


def potential_kernel(filter_ref, filter_t_ref, potential_ref, out_ref):
    for plane in range(potential_ref.shape[0]):
        high, low = split(potential_ref[plane])
        rows = dot(filter_ref[...], jnp.concatenate([high, low, high], axis=0))
        high, low = split(rows)
        out_ref[plane] = (
            dot(high, filter_t_ref[0]) + dot(low, filter_t_ref[0]) + dot(high, filter_t_ref[1])
        )


def plane_kernel(
    inverse_ref,
    box_ref,
    y_ref,
    x_ref,
    x_back_ref,
    y_back_ref,
    potential_ref,
    columns_ref,
    out_ref,
    boxes,
    staged,
):
    sources, planes, bands = staged.shape[:3]
    blocks = sources
    cores, runs = bands // HALF, SIZES[5]
    places = [
        (source, plane, core, (((core * SIZES[3] + x) * runs + run) * planes + plane) * GANG + block * HALF)
        for source, (x, block, run) in enumerate(np.ndindex(SIZES[3], BLOCKS, runs))
        for plane in range(planes)
        for core in range(cores)
    ]
    for source, plane, core, row in places:
        staged[source, plane, core * HALF : (core + 1) * HALF] = columns_ref[row : row + HALF, :]

    def fill(block, carry):
        source_of = jnp.broadcast_to(inverse_ref[pl.ds(block, 1), :], (bands, LANES))
        lane_of = jnp.broadcast_to(inverse_ref[pl.ds(block + blocks, 1), :], (bands, LANES))
        values = [jnp.zeros((bands, LANES), F32) for _ in range(planes)]
        for source in range(sources):
            here = source_of == source
            for plane in range(planes):
                values[plane] = jnp.where(
                    here, take_lanes(staged[source, plane], lane_of), values[plane]
                )
        for plane in range(planes):
            boxes[plane, pl.ds(pl.multiple_of(block * bands, bands), bands), :] = values[plane]
        return carry

    lax.fori_loop(0, blocks, fill, 0)

    def transform(plane, carry):
        stacked = jnp.concatenate(
            [boxes[plane, pl.ds(band, blocks, stride=bands), :] for band in range(bands)], axis=0
        )
        high, low = split(stacked)
        wide = dot(jnp.concatenate([high, low, high], axis=1), y_ref[...])
        potential = potential_ref[plane]
        potential = jnp.concatenate([potential, potential], axis=1)
        back = []
        for band in range(0, bands, 2):
            pair = []
            for one in (band, band + 1):
                mine = wide[one * blocks : (one + 1) * blocks, :]
                pair.append(jnp.concatenate([mine[:, :LANES], mine[:, LANES:]], axis=0))
            high, low = split(jnp.concatenate(pair, axis=1))
            field = dot(x_ref[...], jnp.concatenate([high, low, high], axis=0))
            high, low = split(field * potential)
            both = dot(x_back_ref[...], high)
            both = both[:K] + both[K:] + dot(x_back_ref[:K, :], low)
            for side in range(2):
                one = both[:, side * LANES : (side + 1) * LANES]
                back.append(jnp.concatenate([one[:blocks], one[blocks:]], axis=1))
        high, low = split(jnp.concatenate(back, axis=0))
        total = dot(high, y_back_ref[0]) + dot(low, y_back_ref[0]) + dot(high, y_back_ref[1])
        for band in range(bands):
            boxes[plane, pl.ds(band, blocks, stride=bands), :] = total[
                band * blocks : (band + 1) * blocks, :
            ]
        return carry

    lax.fori_loop(0, planes, transform, 0)

    def pick(source, carry):
        place = jnp.broadcast_to(box_ref[pl.ds(source, 1), :], (bands, LANES))
        lane_of = place & (LANES - 1)
        block_of = lax.shift_right_logical(place, 7)
        values = [jnp.zeros((bands, LANES), F32) for _ in range(planes)]
        for block in range(blocks):
            here = block_of == block
            for plane in range(planes):
                values[plane] = jnp.where(
                    here,
                    take_lanes(boxes[plane, block * bands : (block + 1) * bands, :], lane_of),
                    values[plane],
                )
        for plane in range(planes):
            staged[source, plane] = values[plane]
        return carry

    lax.fori_loop(0, sources, pick, 0)
    for source, plane, core, row in places:
        out_ref[row : row + HALF, :] = staged[source, plane, core * HALF : (core + 1) * HALF]


def backward_kernel(
    grid_cells, rows, starts, packet_ref, own_ref, cas_ref, returned_ref, out_ref, dense, packed, slots
):
    z_transform(cas_ref, returned_ref, dense, grid_cells)
    slots[...] = jnp.full(slots.shape, -1, jnp.int32)
    for block in range(BLOCKS):
        first = block * ROWS + SLOT_ROW
        slots[block, :rows] = packet_ref[first : first + rows, :].astype(jnp.int32)
    packed[...] = jnp.zeros_like(packed)

    def for_bands(rows_of):
        return jnp.concatenate([jnp.broadcast_to(row, (HALF, LANES)) for row in rows_of], axis=0)

    def compact(height, carry):
        values = dense[pl.ds(pl.multiple_of(height * GANG, GANG), GANG), :]
        for step in range(2):
            near = [
                lax.shift_right_logical(starts[block, height], 7) + step for block in range(BLOCKS)
            ]
            cuts = [pl.ds(pl.multiple_of(row * HALF, HALF), HALF) for row in near]
            own = for_bands([slots[block, pl.ds(near[block], 1), :] for block in range(BLOCKS)])
            old = jnp.concatenate([packed[block, cuts[block], :] for block in range(BLOCKS)], axis=0)
            mask = lax.shift_right_logical(own, 7) == height
            new = jnp.where(mask, take_lanes(values, own & (LANES - 1)), old)
            for block in range(BLOCKS):
                packed[block, cuts[block], :] = new[block * HALF : (block + 1) * HALF, :]
        return carry

    lax.fori_loop(0, grid_cells, compact, 0, unroll=4)
    first, second = column_box(own_ref[...], grid_cells)
    radial = (first * first + second * second).astype(F32)
    radial = for_bands([radial[block : block + 1, :] for block in range(BLOCKS)])
    parts = out_ref.shape[0] // (SIZES[1] * GANG * 8)
    each = -(-rows // parts)
    for part in range(parts):
        for place in range(8):
            row = part * each + place
            if place >= each or row >= rows:
                value = jnp.zeros((GANG, LANES), F32)
            else:
                own = for_bands([slots[block, row : row + 1, :] for block in range(BLOCKS)])
                height = wrapped(lax.shift_right_logical(own, 7), grid_cells)
                around = take_lanes(radial, own & (LANES - 1))
                kinetic = 2.0 * (around + (height * height).astype(F32)) / (K * K)
                cut = slice(row * HALF, (row + 1) * HALF)
                trial = jnp.concatenate(
                    [packet_ref[block * ROWS + cut.start : block * ROWS + cut.stop, :] for block in range(BLOCKS)],
                    axis=0,
                )
                value = jnp.concatenate([packed[block, cut, :] for block in range(BLOCKS)], axis=0)
                value = value + kinetic * trial
            for zh in range(SIZES[1]):
                to = (part // SIZES[2] * SIZES[1] + zh) * SIZES[2] + part % SIZES[2]
                out_ref[pl.ds(to * GANG * 8 + place, GANG, stride=8), :] = value


def constant_tables(grid_cells):
    fine = 2 * K
    order = np.arange(grid_cells).reshape(SIZES[3], SIZES[2], SIZES[5], -1)
    order = order.transpose(1, 0, 2, 3).reshape(-1)
    high, low = halves(cas_matrix(grid_cells))
    cas_out = np.concatenate([high[order], high[order], low[order]], axis=1)
    cas_back = np.concatenate([high[:, order], high[:, order], low[:, order]], axis=1)
    theta = (np.arange(fine) + 0.5) / fine
    full = np.arange(grid_cells) / grid_cells
    box = np.arange(K) - K // 2
    angle = 2.0 * math.pi * box[:, None] * theta[None, :]
    box_table = ((np.cos(angle) + np.sin(angle)) / math.sqrt(fine)).astype(np.float32)
    waves = 2.0 * math.pi * np.arange(1, K)
    apart = theta[:, None] - full[None, :]
    project = 1.0 + 2.0 * np.cos(waves[:, None, None] * apart[None]).sum(axis=0)
    edge = 2.0 * math.pi * K
    project = project + np.sin(edge * theta)[:, None] * np.sin(edge * full)[None, :]
    project = (project / grid_cells).astype(np.float32)
    high, low = halves(project)
    filter_three = np.concatenate([high, high, low], axis=1)
    filter_back = np.stack([high.T, low.T])
    sides = np.zeros((2, K, 2, fine), np.float32)
    for side in range(2):
        sides[side, :, side, :] = box_table
    high, low = halves(sides.reshape(2 * K, 2 * fine))
    y_three = np.concatenate([high, high, low], axis=0)
    y_back = np.stack([high.T, low.T])
    order = np.concatenate([np.arange(0, K, 2), np.arange(1, K, 2)])
    high, low = halves(box_table[order])
    x_three = np.concatenate([high, high, low], axis=0).T
    x_back = np.concatenate([high, low], axis=0)
    tables = (cas_out, cas_back, filter_three, filter_back, y_three, x_three, x_back, y_back)
    return tuple(jnp.asarray(one) for one in tables)


def swap_pairs(turn):
    place = np.arange(math.prod(SIZES)).reshape(SIZES)
    pairs = []
    for (y, zh, c, x, l2, ll), target in np.ndenumerate(place):
        near = zh if l2 == c else (zh * 2 + l2 + turn) % 4 // 2
        pairs.append((int(place[y, near, l2, x, c, ll]), int(target)))
    return tuple(pairs)


def swapped(block, axis):
    return lax.ppermute(block, axis, ((0, 1), (1, 0)))


def apply_hamiltonian(trial_block, potential, positions, sphere_slots, pieces):
    bands, coefs = trial_block.shape
    planes, grid_cells = potential.shape[:2]
    fft_size = lax.axis_size(FFT)
    rows = coefs // LANES
    slots = sphere_slots.reshape(rows, LANES)
    position_rows = positions.reshape(fft_size, LANES)
    own = position_rows.reshape(SIZES[3], BLOCKS, SIZES[5], LANES)
    own = lax.dynamic_index_in_dim(own, lax.axis_index("x"), 0, keepdims=False)
    own = lax.dynamic_index_in_dim(own, lax.axis_index("ll"), 1, keepdims=False)
    cas_out, cas_back, filter_three, filter_back, *plane_tables = constant_tables(grid_cells)
    i32 = functools.partial(jax.ShapeDtypeStruct, dtype=jnp.int32)
    f32 = functools.partial(jax.ShapeDtypeStruct, dtype=F32)
    params = pltpu.CompilerParams(vmem_limit_bytes=48 * 2**20)
    smem = pl.BlockSpec(memory_space=pltpu.SMEM)
    vmem = pl.BlockSpec(memory_space=pltpu.VMEM)
    filtered = pl.pallas_call(
        potential_kernel,
        out_shape=f32((planes, 2 * K, 2 * K)),
        compiler_params=params,
        name="filter",
    )(filter_three, filter_back, potential)
    filtered, trial_block = lax.optimization_barrier((filtered, trial_block))
    cut = planes // 2
    filtered = [
        lax.ppermute(part, BAND + FFT, swap_pairs(turn))
        for part, turn in ((filtered[:cut], 1), (filtered[cut:], -1))
    ]
    half = lax.axis_index("l2")
    packet = f32((ROWS, LANES))
    kept, sent, inverse, box = pl.pallas_call(
        functools.partial(pack_kernel, grid_cells),
        out_shape=(packet, packet, i32((2 * fft_size, LANES)), i32((fft_size, LANES))),
        in_specs=[smem] + [vmem] * 3,
        out_specs=[vmem] * 4,
        compiler_params=params,
        name="pack",
    )(half.reshape(1), slots, position_rows, trial_block)
    other = swapped(sent, "l2")
    packet = jnp.where(half == 0, jnp.stack([kept, other]), jnp.stack([other, kept]))
    starts = packet[:, START_ROW : START_ROW + 2].reshape(BLOCKS, -1).astype(jnp.int32)
    packet = packet.reshape(BLOCKS * ROWS, LANES)
    dense_rows = grid_cells * GANG
    dense = pltpu.VMEM((dense_rows, LANES), F32)
    mixed = pl.pallas_call(
        functools.partial(forward_kernel, grid_cells),
        out_shape=f32((dense_rows, LANES)),
        in_specs=[smem, vmem, vmem],
        out_specs=vmem,
        scratch_shapes=[pltpu.VMEM((dense_rows, LANES), jnp.int32), dense],
        compiler_params=params,
        name="forward",
    )(starts, packet, cas_out)
    filtered = jnp.concatenate(filtered, axis=0)
    pieces = lax.all_to_all(pieces, SIDE, 0, 0, tiled=True)
    mixed, filtered, pieces = lax.optimization_barrier((mixed, filtered, pieces))
    gathered = lax.all_to_all(mixed, GROUP, 0, 0, tiled=True)
    trial = pieces[:, -bands:].reshape(-1, pieces.shape[2])
    gathered, trial = lax.optimization_barrier((gathered, trial))
    theirs = swapped(trial, "zh")
    weighted = pl.pallas_call(
        plane_kernel,
        out_shape=f32(gathered.shape),
        scratch_shapes=[
            pltpu.VMEM((planes, fft_size * bands, LANES), F32),
            pltpu.VMEM((fft_size, planes, bands, LANES), F32),
        ],
        compiler_params=params,
        cost_estimate=pl.CostEstimate(
            flops=25 * 10**9, bytes_accessed=60 * 10**6, transcendentals=0
        ),
        name="planes",
    )(inverse, box, *plane_tables, filtered, gathered)
    weighted, theirs = lax.optimization_barrier((weighted, theirs))
    returned = lax.all_to_all(weighted, GROUP, 0, 0, tiled=True)
    parts = pieces.shape[0]
    tall = rows + 7 & -8
    applied = pl.pallas_call(
        functools.partial(backward_kernel, grid_cells, rows),
        out_shape=f32((SIZES[1] * parts * GANG * 8, LANES)),
        in_specs=[smem] + [vmem] * 4,
        out_specs=vmem,
        scratch_shapes=[
            dense,
            pltpu.VMEM((BLOCKS, tall * HALF, LANES), F32),
            pltpu.VMEM((BLOCKS, tall, LANES), jnp.int32),
        ],
        compiler_params=params,
        cost_estimate=pl.CostEstimate(flops=8 * 10**9, bytes_accessed=16 * 10**6, transcendentals=0),
        name="backward",
    )(starts, packet, own, cas_back, returned)
    applied = lax.all_to_all(applied, BAND + ("l2",), 0, 0, tiled=True)
    each = pieces.shape[2] // LANES
    applied = applied.reshape(-1, 8, LANES)[:, :each].reshape(2 * trial.shape[0], -1)
    return applied, pieces[:, :-bands], jnp.concatenate([trial, theirs], axis=0)


def per_device(trial_block, all_bands, potential, positions, sphere_slots):
    parts = lax.axis_size(SIDE)
    rows, coefs = all_bands.shape
    width = -(-coefs // (LANES * parts)) * LANES
    pieces = jnp.concatenate([all_bands, trial_block], axis=0)
    pieces = jnp.pad(pieces, ((0, 0), (0, parts * width - coefs)))
    pieces = pieces.reshape(-1, parts, width).transpose(1, 0, 2)
    applied, pieces, trial = apply_hamiltonian(trial_block, potential, positions, sphere_slots, pieces)
    pieces = pieces.reshape(parts * rows, width)
    products = [
        jnp.einsum("ag,bg->ab", pieces, block, precision=lax.Precision.HIGH)
        for block in (trial, applied)
    ]
    products = jnp.concatenate(products, axis=1)
    columns = products.shape[1]
    near = lax.all_to_all(products, NEAR, 0, 0, tiled=True)
    near = jnp.sum(near.reshape(lax.axis_size(NEAR), -1, columns), axis=0)
    far = lax.all_to_all(near, ("l2", "ll"), 0, 0, tiled=True)
    total = jnp.sum(far, axis=0).reshape(2, -1)
    first = total[0].reshape(SIZES[1], SIZES[0], SIZES[2], -1)
    first = jnp.where(lax.axis_index("zh") == 0, first, first[::-1]).transpose(1, 0, 2, 3)
    return (first.reshape(1, -1), total[1:])


def solution(mesh):
    axes = Mesh(mesh.devices.reshape(SIZES), AXES)
    placed = (P(BAND, FFT), P(BAND, FFT), P(FFT, None, None), P(), P(FFT))
    return jax.shard_map(
        per_device,
        mesh=axes,
        in_specs=placed,
        out_specs=(P(BAND + FFT, None), P(BAND + FFT, None)),
        check_vma=False,
    )
```

time: 247 us -> 220 us (0.89)
  waiting for transfers between devices: 110 us -> 76.6 us
  blocking collectives: 16.8 us -> 28.3 us
  local copies, waits for them, and re-layouts: 10.5 us -> 3.79 us
    all_to_all x4, waiting for transfers between devices: 98.6 us -> 67.5 us  [the longest x1 20.3 us: apply_hamiltonian(): gathered = lax.all_to_all(mixed, GROUP, 0, 0, tiled=True)]
    all_to_all x4, starting transfers between devices: 42.7 us -> 25.8 us  [the longest x1 9.93 us: apply_hamiltonian(): applied = lax.all_to_all(applied, BAND + ('l2',), 0, 0, tiled=True)]
    ppermute x2 -> x4, starting transfers between devices: 15.9 us -> 27.5 us  [the longest x2 16.5 us: swapped(): return lax.ppermute(block, axis, ((0, 1), (1, 0)))]
    all_to_all x1, blocking collectives: 16.8 us -> 28.3 us  [per_device(): near = lax.all_to_all(products, NEAR, 0, 0, tiled=True)]
    unnamed x31 -> x26, local copies, waits for them, and re-layouts: 5.05 us -> 0.27 us
    all_to_all x1, starting transfers between devices: 6.37 us -> 10.5 us  [apply_hamiltonian(): pieces = lax.all_to_all(pieces, SIDE, 0, 0, tiled=True)]
    optimization_barrier x1 -> x0, local copies, waits for them, and re-layouts: 2.5 us -> none  [apply_hamiltonian(): gathered, pieces = lax.optimization_barrier((gathered, pieces))]
    ppermute x2 -> x4, waiting for transfers between devices: 11.4 us -> 9.11 us  [the longest x2 9.1 us: swapped(): return lax.ppermute(block, axis, ((0, 1), (1, 0)))]
  transfers between devices with their start and end apart: 7 -> 9, of which waited for: 5 -> 5; matrix products, arithmetic and copies ran while one was open for 1% -> 0% of each run, Pallas kernels for 14% -> 16%
where the time goes in v3:
time: 220 us; the launch traced here: 219 us
  waiting for transfers between devices  76.6 us (35%)
  starting transfers between devices  63.7 us (29%)
  Pallas kernels  43.4 us (20%)
  blocking collectives  28.3 us (13%)
  local copies, waits for them, and re-layouts  3.79 us (2%)
    all_to_all x1, blocking collectives, per_device(): near = lax.all_to_all(products, NEAR, 0, 0, tiled=True)  28.3 us
    pallas_call x1, Pallas kernels, apply_hamiltonian(): pl.pallas_call(plane_kernel, out_shape=f32(gathered.shape), scratch_shape...  25.9 us
    all_to_all x1, waiting for transfers between devices, apply_hamiltonian(): gathered = lax.all_to_all(mixed, GROUP, 0, 0, tiled=True)  20.3 us
    all_to_all x1, waiting for transfers between devices, apply_hamiltonian(): returned = lax.all_to_all(weighted, GROUP, 0, 0, tiled=True)  20.3 us
    all_to_all x1, waiting for transfers between devices, apply_hamiltonian(): applied = lax.all_to_all(applied, BAND + ('l2',), 0, 0, tiled=True)  17.6 us
    ppermute x2, starting transfers between devices, swapped(): return lax.ppermute(block, axis, ((0, 1), (1, 0)))  16.5 us
    ppermute x2, starting transfers between devices, apply_hamiltonian(): lax.ppermute(part, BAND + FFT, swap_pairs(turn))  10.9 us
    all_to_all x1, starting transfers between devices, apply_hamiltonian(): pieces = lax.all_to_all(pieces, SIDE, 0, 0, tiled=True)  10.5 us
  transfers between devices with their start and end apart: 9, of which 5 were waited for; matrix products, arithmetic and copies ran while one was open for 0% of the time, Pallas kernels for 16%

profile of v3, /device:TPU:1, one launch (start us, length us, event | category | flops | bytes accessed | tf_op | source)
XLA Modules:
  0.0 219.4 jit_solution(11165639897984802201)
XLA Ops:
  0.6 1.3 select_maximum_fusion
  2.2 1.2 copy.23
  3.4 10.5 %all-to-all-start = ((f32[8,40,896]{2,1,0:T(8,128)}), f32[8,40,896]{2,1,0:T(8,128)S(1)}, u32[]{:S(2)}, u32[]{:S(2)}) async-start(f32[8,40,896]{2,1,0:T(8,128)} %copy.23), calls=%async_computation | async-start | bytes 2293760 | tf_op jit(solution)/shard_map/all_to_all | solution.py:441
  13.9 1.2 filter.1
  15.1 1.7 pack.1
  16.9 4.4 %collective-permute-start = (f32[256,128]{1,0:T(8,128)S(1)}, f32[256,128]{1,0:T(8,128)S(1)}, u32[]{:S(2)}, u32[]{:S(2)}) collective-permute-start(f32[256,128]{1,0:T(8,128)S(1)} %get-tuple-element.17), channel_id=1, source_target_pairs={{0,4},{4,0},{1,5},{5,1},{2,6},{6,2},{3,7},{7,3},{8,12},{12,8},{9,1... | collective-permute-start | bytes 393224 | tf_op jit(solution)/shard_map/ppermute | solution.py:384
  21.4 9.0 %collective-permute-start.1 = (f32[3,128,128]{2,1,0:T(8,128)S(1)}, f32[3,128,128]{2,1,0:T(8,128)S(1)}, u32[]{:S(2)}, u32[]{:S(2)}) collective-permute-start(f32[3,128,128]{2,1,0:T(8,128)S(1)} %get-tuple-element.28), channel_id=1, source_target_pairs={{0,0},{1,1},{2,2},{3,3},{96,4},{97,5},{98,6},{99,7},{8,8},{9,9},{1... | collective-permute-start | bytes 589832 | tf_op jit(solution)/shard_map/ppermute | solution.py:412
  30.4 1.9 collective-permute-start.2
  32.3 9.1 %collective-permute-done = f32[256,128]{1,0:T(8,128)S(1)} collective-permute-done((f32[256,128]{1,0:T(8,128)S(1)}, f32[256,128]{1,0:T(8,128)S(1)}, u32[]{:S(2)}, u32[]{:S(2)}) %collective-permute-start) | collective-permute-done | bytes 131104 | tf_op jit(solution)/shard_map/ppermute | solution.py:384
  41.5 6.8 %forward.1 = f32[1536,128]{1,0:T(8,128)} custom-call(s32[2,256]{1,0:T(2,128)S(1)} %bitcast.44, f32[512,128]{1,0:T(8,128)S(1)} %bitcast.36, bf16[192,576]{1,0:T(8,128)(2,1)S(1)} %copy-done.2), custom_call_target="tpu_custom_call" | custom-call | tf_op jit(solution)/shard_map/forward/pallas_call | solution.py:431
  48.4 5.5 %all-to-all-start.1 = ((f32[32,48,128]{2,1,0:T(8,128)}), f32[32,48,128]{2,1,0:T(8,128)S(1)}, u32[]{:S(2)}, u32[]{:S(2)}) async-start(f32[32,48,128]{2,1,0:T(8,128)} %bitcast.8), calls=%async_computation.1 | async-start | bytes 1572864 | tf_op jit(solution)/shard_map/all_to_all | solution.py:443
  53.9 20.3 %all-to-all-done.1 = f32[32,48,128]{2,1,0:T(8,128)S(1)} async-done(((f32[32,48,128]{2,1,0:T(8,128)}), f32[32,48,128]{2,1,0:T(8,128)S(1)}, u32[]{:S(2)}, u32[]{:S(2)}) %all-to-all-start.1) | async-done | bytes 786464 | tf_op jit(solution)/shard_map/all_to_all | solution.py:443
  74.2 12.1 %collective-permute-start.3 = (f32[64,896]{1,0:T(8,128)S(1)}, f32[64,896]{1,0:T(8,128)S(1)}, u32[]{:S(2)}, u32[]{:S(2)}) collective-permute-start(f32[64,896]{1,0:T(8,128)S(1)} %slice_bitcast_fusion), channel_id=1, source_target_pairs={{0,64},{64,0},{1,65},{65,1},{2,66},{66,2},{3,67},{67,3},{4,68},{68... | collective-permute-start | bytes 688136 | tf_op jit(solution)/shard_map/ppermute | solution.py:384
  86.4 25.9 %planes.1 = f32[1536,128]{1,0:T(8,128)} custom-call(s32[64,128]{1,0:T(8,128)S(1)} %get-tuple-element.22.inverse_ref, s32[32,128]{1,0:T(8,128)S(1)} %get-tuple-element.23.box_ref, bf16[384,256]{1,0:T(8,128)(2,1)S(1)} %copy-done.8, bf16[128,192]{1,0:T(8,128)(2,1)S(1)} %copy-done.10, bf16[128,128]{1,0:T(8,128)(2,1)S(1)} %copy-done.11, ...), custom_call_target="tpu_custom_call" | custom-call | flops 24999999488 | bytes 60000000 | tf_op jit(solution)/shard_map/planes/pallas_call | solution.py:447
  112.3 6.1 %all-to-all-start.2 = ((f32[32,48,128]{2,1,0:T(8,128)}), f32[32,48,128]{2,1,0:T(8,128)S(1)}, u32[]{:S(2)}, u32[]{:S(2)}) async-start(f32[32,48,128]{2,1,0:T(8,128)} %bitcast.13), calls=%async_computation.2 | async-start | bytes 1572864 | tf_op jit(solution)/shard_map/all_to_all | solution.py:461
  118.4 20.3 %all-to-all-done.2 = f32[32,48,128]{2,1,0:T(8,128)S(1)} async-done(((f32[32,48,128]{2,1,0:T(8,128)}), f32[32,48,128]{2,1,0:T(8,128)S(1)}, u32[]{:S(2)}, u32[]{:S(2)}) %all-to-all-start.2) | async-done | bytes 786464 | tf_op jit(solution)/shard_map/all_to_all | solution.py:461
  138.7 7.7 %backward.1 = f32[1024,128]{1,0:T(8,128)} custom-call(s32[2,256]{1,0:T(2,128)S(1)} %bitcast.45, f32[512,128]{1,0:T(8,128)S(1)} %bitcast.37, s32[2,128]{1,0:T(2,128)S(1)} %bitcast.46, bf16[192,576]{1,0:T(8,128)(2,1)S(1)} %copy-done.7, f32[1536,128]{1,0:T(8,128)S(1)} %bitcast.38), custom_call_target="tpu_custom_call" | custom-call | flops 8000000000 | bytes 16000000 | tf_op jit(solution)/shard_map/backward/pallas_call | solution.py:464
  146.4 9.9 %all-to-all-start.3 = ((f32[32,32,128]{2,1,0:T(8,128)}), f32[32,32,128]{2,1,0:T(8,128)S(1)}, u32[]{:S(2)}, u32[]{:S(2)}) async-start(f32[32,32,128]{2,1,0:T(8,128)} %bitcast.15), calls=%async_computation.3 | async-start | bytes 1048576 | tf_op jit(solution)/shard_map/all_to_all | solution.py:478
  157.0 17.6 %all-to-all-done.3 = f32[32,32,128]{2,1,0:T(8,128)S(1)} async-done(((f32[32,32,128]{2,1,0:T(8,128)}), f32[32,32,128]{2,1,0:T(8,128)S(1)}, u32[]{:S(2)}, u32[]{:S(2)}) %all-to-all-start.3) | async-done | bytes 524320 | tf_op jit(solution)/shard_map/all_to_all | solution.py:478
  175.5 28.3 %all_to_all.55 = f32[32,8,256]{2,1,0:T(8,128)S(1)} all-to-all(f32[32,8,256]{2,1,0:T(8,128)S(1)} %bitcast.53), channel_id=1, replica_groups=mesh['y'=4,'zh'=2,'c'=2,'x'=4,'l2'=2,'ll'=4] {'y','c','x'}, dimensions={0} | all-to-all | bytes 524288 | tf_op jit(solution)/shard_map/all_to_all | solution.py:499
  203.9 0.6 all_to_all.47
  204.5 4.3 %all-to-all-start.5 = ((f32[8,1,256]{2,1,0:T(1,128)}), f32[8,1,256]{2,1,0:T(1,128)S(1)}, u32[]{:S(2)}, u32[]{:S(2)}) async-start(f32[8,1,256]{2,1,0:T(1,128)} %all_to_all.47), calls=%async_computation.5 | async-start | bytes 16384 | tf_op jit(solution)/shard_map/all_to_all | solution.py:501
  208.8 9.3 %all-to-all-done.5 = f32[8,1,256]{2,1,0:T(1,128)S(1)} async-done(((f32[8,1,256]{2,1,0:T(1,128)}), f32[8,1,256]{2,1,0:T(1,128)S(1)}, u32[]{:S(2)}, u32[]{:S(2)}) %all-to-all-start.5) | async-done | bytes 8224 | tf_op jit(solution)/shard_map/all_to_all | solution.py:501
  218.8 0.6 reshape.73
  (48 shorter events, 2.6 us)
Async XLA Ops:
  3.4 10.5 %copy-start = (f32[6,192,192]{2,1,0:T(8,128)S(1)}, f32[6,192,192]{2,1,0:T(8,128)}, u32[]{:S(2)}) copy-start(f32[6,192,192]{2,1,0:T(8,128)} %potential_ref.1) | copy-start | bytes 2654212
  3.4 10.5 %copy-start.3 = (bf16[128,576]{1,0:T(8,128)(2,1)S(1)}, bf16[128,576]{1,0:T(8,128)(2,1)}, u32[]{:S(2)}) copy-start(bf16[128,576]{1,0:T(8,128)(2,1)} %constant.69.clone.filter_ref) | copy-start | bytes 442372
  3.4 10.5 %copy-start.4 = (bf16[2,192,128]{2,1,0:T(8,128)(2,1)S(1)}, bf16[2,192,128]{2,1,0:T(8,128)(2,1)}, u32[]{:S(2)}) copy-start(bf16[2,192,128]{2,1,0:T(8,128)(2,1)} %constant.70.clone.filter_t_ref) | copy-start | bytes 294916
  3.4 45.0 %all-to-all-start = ((f32[8,40,896]{2,1,0:T(8,128)}), f32[8,40,896]{2,1,0:T(8,128)S(1)}, u32[]{:S(2)}, u32[]{:S(2)}) async-start(f32[8,40,896]{2,1,0:T(8,128)} %copy.23), calls=%async_computation | async-start | bytes 2293760 | tf_op jit(solution)/shard_map/all_to_all | solution.py:441
  13.9 1.2 copy-start.1
  13.9 1.2 copy-start.5
  13.9 1.2 copy-start.6
  15.1 26.4 %copy-start.2 = (bf16[192,576]{1,0:T(8,128)(2,1)S(1)}, bf16[192,576]{1,0:T(8,128)(2,1)}, u32[]{:S(2)}) copy-start(bf16[192,576]{1,0:T(8,128)(2,1)} %constant.67.clone.cas_ref) | copy-start | bytes 663556
  16.9 24.5 %collective-permute-start = (f32[256,128]{1,0:T(8,128)S(1)}, f32[256,128]{1,0:T(8,128)S(1)}, u32[]{:S(2)}, u32[]{:S(2)}) collective-permute-start(f32[256,128]{1,0:T(8,128)S(1)} %get-tuple-element.17), channel_id=1, source_target_pairs={{0,4},{4,0},{1,5},{5,1},{2,6},{6,2},{3,7},{7,3},{8,12},{12,8},{9,1... | collective-permute-start | bytes 393224 | tf_op jit(solution)/shard_map/ppermute | solution.py:384
  21.4 26.9 %collective-permute-start.1 = (f32[3,128,128]{2,1,0:T(8,128)S(1)}, f32[3,128,128]{2,1,0:T(8,128)S(1)}, u32[]{:S(2)}, u32[]{:S(2)}) collective-permute-start(f32[3,128,128]{2,1,0:T(8,128)S(1)} %get-tuple-element.28), channel_id=1, source_target_pairs={{0,0},{1,1},{2,2},{3,3},{96,4},{97,5},{98,6},{99,7},{8,8},{9,9},{1... | collective-permute-start | bytes 589832 | tf_op jit(solution)/shard_map/ppermute | solution.py:412
  30.4 17.9 %collective-permute-start.2 = (f32[3,128,128]{2,1,0:T(8,128)S(1)}, f32[3,128,128]{2,1,0:T(8,128)S(1)}, u32[]{:S(2)}, u32[]{:S(2)}) collective-permute-start(f32[3,128,128]{2,1,0:T(8,128)S(1)} %get-tuple-element.29), channel_id=1, source_target_pairs={{0,0},{1,1},{2,2},{3,3},{32,4},{33,5},{34,6},{35,7},{8,8},{9,9},{1... | collective-permute-start | bytes 589832 | tf_op jit(solution)/shard_map/ppermute | solution.py:412
  48.3 38.0 %copy-start.8 = (bf16[384,256]{1,0:T(8,128)(2,1)S(1)}, bf16[384,256]{1,0:T(8,128)(2,1)}, u32[]{:S(2)}) copy-start(bf16[384,256]{1,0:T(8,128)(2,1)} %constant.71.clone.y_ref) | copy-start | bytes 589828
  48.4 38.0 %copy-start.9 = (bf16[2,256,128]{2,1,0:T(8,128)(2,1)S(1)}, bf16[2,256,128]{2,1,0:T(8,128)(2,1)}, u32[]{:S(2)}) copy-start(bf16[2,256,128]{2,1,0:T(8,128)(2,1)} %constant.74.clone.y_back_ref) | copy-start | bytes 393220
  48.4 38.0 %copy-start.10 = (bf16[128,192]{1,0:T(8,128)(2,1)S(1)}, bf16[128,192]{1,0:T(8,128)(2,1)}, u32[]{:S(2)}) copy-start(bf16[128,192]{1,0:T(8,128)(2,1)} %constant.72.clone.x_ref) | copy-start | bytes 147460
  48.4 38.0 %copy-start.11 = (bf16[128,128]{1,0:T(8,128)(2,1)S(1)}, bf16[128,128]{1,0:T(8,128)(2,1)}, u32[]{:S(2)}) copy-start(bf16[128,128]{1,0:T(8,128)(2,1)} %constant.73.clone.x_back_ref) | copy-start | bytes 98308
  48.4 25.8 %all-to-all-start.1 = ((f32[32,48,128]{2,1,0:T(8,128)}), f32[32,48,128]{2,1,0:T(8,128)S(1)}, u32[]{:S(2)}, u32[]{:S(2)}) async-start(f32[32,48,128]{2,1,0:T(8,128)} %bitcast.8), calls=%async_computation.1 | async-start | bytes 1572864 | tf_op jit(solution)/shard_map/all_to_all | solution.py:443
  74.2 38.1 %collective-permute-start.3 = (f32[64,896]{1,0:T(8,128)S(1)}, f32[64,896]{1,0:T(8,128)S(1)}, u32[]{:S(2)}, u32[]{:S(2)}) collective-permute-start(f32[64,896]{1,0:T(8,128)S(1)} %slice_bitcast_fusion), channel_id=1, source_target_pairs={{0,64},{64,0},{1,65},{65,1},{2,66},{66,2},{3,67},{67,3},{4,68},{68... | collective-permute-start | bytes 688136 | tf_op jit(solution)/shard_map/ppermute | solution.py:384
  112.3 26.4 %copy-start.7 = (bf16[192,576]{1,0:T(8,128)(2,1)S(1)}, bf16[192,576]{1,0:T(8,128)(2,1)}, u32[]{:S(2)}) copy-start(bf16[192,576]{1,0:T(8,128)(2,1)} %constant.68.clone.cas_ref) | copy-start | bytes 663556
  112.3 26.4 %all-to-all-start.2 = ((f32[32,48,128]{2,1,0:T(8,128)}), f32[32,48,128]{2,1,0:T(8,128)S(1)}, u32[]{:S(2)}, u32[]{:S(2)}) async-start(f32[32,48,128]{2,1,0:T(8,128)} %bitcast.13), calls=%async_computation.2 | async-start | bytes 1572864 | tf_op jit(solution)/shard_map/all_to_all | solution.py:461
  146.4 28.1 %all-to-all-start.3 = ((f32[32,32,128]{2,1,0:T(8,128)}), f32[32,32,128]{2,1,0:T(8,128)S(1)}, u32[]{:S(2)}, u32[]{:S(2)}) async-start(f32[32,32,128]{2,1,0:T(8,128)} %bitcast.15), calls=%async_computation.3 | async-start | bytes 1048576 | tf_op jit(solution)/shard_map/all_to_all | solution.py:478
  204.5 13.6 %all-to-all-start.5 = ((f32[8,1,256]{2,1,0:T(1,128)}), f32[8,1,256]{2,1,0:T(1,128)S(1)}, u32[]{:S(2)}, u32[]{:S(2)}) async-start(f32[8,1,256]{2,1,0:T(1,128)} %all_to_all.47), calls=%async_computation.5 | async-start | bytes 16384 | tf_op jit(solution)/shard_map/all_to_all | solution.py:501

commit v4 on v3

--- a/solution.py
+++ b/solution.py
@@ -73,7 +73,7 @@
 
 
 def pack_kernel(
-    grid_cells, half, slots_ref, positions_ref, trial_ref, own_ref, send_ref, inverse_ref, box_ref
+    grid_cells, half, slots_ref, trial_ref, own_ref, send_ref
 ):
     rows = slots_ref.shape[0]
     first_half = half[0] == 0
@@ -106,6 +106,10 @@
         packet_ref[START_ROW + 2 : SLOT_ROW, :] = jnp.zeros((2, LANES), F32)
         packet_ref[SLOT_ROW : SLOT_ROW + rows, :] = own_slots
         packet_ref[SLOT_ROW + rows :, :] = jnp.zeros((ROWS - SLOT_ROW - rows, LANES), F32)
+
+
+def boxes_kernel(grid_cells, positions_ref, inverse_ref, box_ref):
+    lane_ids = lax.broadcasted_iota(jnp.int32, (LANES, LANES), 0)
     first, second = column_box(positions_ref[...], grid_cells)
     box = (first + K // 2) * K + second + K // 2
     box_ref[...] = box
@@ -171,7 +175,7 @@
         dense[cut, :] = jnp.where(place < 0, 0.0, value)
         return carry
 
-    lax.fori_loop(0, grid_cells, expand, 0, unroll=4)
+    lax.fori_loop(0, grid_cells, expand, 0, unroll=8)
     z_transform(cas_ref, dense, out_ref, grid_cells)
 
 
@@ -197,6 +201,7 @@
     out_ref,
     boxes,
     staged,
+    products,
 ):
     sources, planes, bands = staged.shape[:3]
     blocks = sources
@@ -258,24 +263,47 @@
 
     lax.fori_loop(0, planes, transform, 0)
 
-    def pick(source, carry):
-        place = jnp.broadcast_to(box_ref[pl.ds(source, 1), :], (bands, LANES))
-        lane_of = place & (LANES - 1)
-        block_of = lax.shift_right_logical(place, 7)
-        values = [jnp.zeros((bands, LANES), F32) for _ in range(planes)]
-        for block in range(blocks):
-            here = block_of == block
+    first_product = blocks - 2 * products.shape[0]
+    for pair in range(products.shape[0]):
+        for plane in range(0, planes, 2):
+            sides = []
+            for block in (first_product + 2 * pair, first_product + 2 * pair + 1):
+                cut = slice(block * bands, (block + 1) * bands)
+                sides.append(jnp.concatenate([boxes[plane, cut, :], boxes[plane + 1, cut, :]], axis=0))
+            high, low = split(jnp.concatenate(sides, axis=1))
+            products[pair, plane * bands : (plane + 2) * bands, :] = high
+            products[pair, (planes + plane) * bands : (planes + plane + 2) * bands, :] = low
+    lane_rows = lax.broadcasted_iota(jnp.int32, (2 * LANES, 2 * LANES), 0)
+
+    def pick(pair, carry):
+        places = [box_ref[pl.ds(pair * 2 + side, 1), :] for side in range(2)]
+        wide = jnp.concatenate(places, axis=1)
+        rest = jnp.zeros((2 * planes * bands, 2 * LANES), F32)
+        for step in range(products.shape[0]):
+            low = (first_product + 2 * step) * LANES
+            rest = rest + dot(products[step], (wide - low == lane_rows).astype(F32).astype(BF16))
+        rest = rest[: planes * bands] + rest[planes * bands :]
+        for side in range(2):
+            place = jnp.broadcast_to(places[side], (bands, LANES))
+            lane_of = place & (LANES - 1)
+            block_of = lax.shift_right_logical(place, 7)
+            values = [jnp.zeros((bands, LANES), F32) for _ in range(planes)]
+            for block in range(first_product):
+                here = block_of == block
+                for plane in range(planes):
+                    values[plane] = jnp.where(
+                        here,
+                        take_lanes(boxes[plane, block * bands : (block + 1) * bands, :], lane_of),
+                        values[plane],
+                    )
             for plane in range(planes):
-                values[plane] = jnp.where(
-                    here,
-                    take_lanes(boxes[plane, block * bands : (block + 1) * bands, :], lane_of),
-                    values[plane],
+                cut = slice(plane * bands, (plane + 1) * bands)
+                staged[pair * 2 + side, plane] = (
+                    values[plane] + rest[cut, side * LANES : (side + 1) * LANES]
                 )
-        for plane in range(planes):
-            staged[source, plane] = values[plane]
         return carry
 
-    lax.fori_loop(0, sources, pick, 0)
+    lax.fori_loop(0, sources // 2, pick, 0)
     for source, plane, core, row in places:
         out_ref[row : row + HALF, :] = staged[source, plane, core * HALF : (core + 1) * HALF]
 
@@ -308,7 +336,7 @@
                 packed[block, cuts[block], :] = new[block * HALF : (block + 1) * HALF, :]
         return carry
 
-    lax.fori_loop(0, grid_cells, compact, 0, unroll=4)
+    lax.fori_loop(0, grid_cells, compact, 0, unroll=8)
     first, second = column_box(own_ref[...], grid_cells)
     radial = (first * first + second * second).astype(F32)
     radial = for_bands([radial[block : block + 1, :] for block in range(BLOCKS)])
@@ -384,7 +412,14 @@
     return lax.ppermute(block, axis, ((0, 1), (1, 0)))
 
 
-def apply_hamiltonian(trial_block, potential, positions, sphere_slots, pieces):
+def arrange(block):
+    parts = lax.axis_size(SIDE)
+    width = -(-block.shape[1] // (LANES * parts)) * LANES
+    block = jnp.pad(block, ((0, 0), (0, parts * width - block.shape[1])))
+    return block.reshape(-1, parts, width).transpose(1, 0, 2)
+
+
+def apply_hamiltonian(trial_block, potential, positions, sphere_slots, all_bands):
     bands, coefs = trial_block.shape
     planes, grid_cells = potential.shape[:2]
     fft_size = lax.axis_size(FFT)
@@ -400,29 +435,38 @@
     params = pltpu.CompilerParams(vmem_limit_bytes=48 * 2**20)
     smem = pl.BlockSpec(memory_space=pltpu.SMEM)
     vmem = pl.BlockSpec(memory_space=pltpu.VMEM)
+    half = lax.axis_index("l2")
+    packet = f32((ROWS, LANES))
+    kept, sent = pl.pallas_call(
+        functools.partial(pack_kernel, grid_cells),
+        out_shape=(packet, packet),
+        in_specs=[smem] + [vmem] * 2,
+        out_specs=[vmem] * 2,
+        compiler_params=params,
+        name="pack",
+    )(half.reshape(1), slots, trial_block)
+    sent, potential, pieces, position_rows = lax.optimization_barrier(
+        (sent, potential, all_bands, position_rows)
+    )
+    other = swapped(sent, "l2")
+    pieces = arrange(jnp.concatenate([pieces, trial_block], axis=0))
+    inverse, box = pl.pallas_call(
+        functools.partial(boxes_kernel, grid_cells),
+        out_shape=(i32((2 * fft_size, LANES)), i32((fft_size, LANES))),
+        compiler_params=params,
+        name="boxes",
+    )(position_rows)
     filtered = pl.pallas_call(
         potential_kernel,
         out_shape=f32((planes, 2 * K, 2 * K)),
         compiler_params=params,
         name="filter",
     )(filter_three, filter_back, potential)
-    filtered, trial_block = lax.optimization_barrier((filtered, trial_block))
     cut = planes // 2
     filtered = [
         lax.ppermute(part, BAND + FFT, swap_pairs(turn))
         for part, turn in ((filtered[:cut], 1), (filtered[cut:], -1))
     ]
-    half = lax.axis_index("l2")
-    packet = f32((ROWS, LANES))
-    kept, sent, inverse, box = pl.pallas_call(
-        functools.partial(pack_kernel, grid_cells),
-        out_shape=(packet, packet, i32((2 * fft_size, LANES)), i32((fft_size, LANES))),
-        in_specs=[smem] + [vmem] * 3,
-        out_specs=[vmem] * 4,
-        compiler_params=params,
-        name="pack",
-    )(half.reshape(1), slots, position_rows, trial_block)
-    other = swapped(sent, "l2")
     packet = jnp.where(half == 0, jnp.stack([kept, other]), jnp.stack([other, kept]))
     starts = packet[:, START_ROW : START_ROW + 2].reshape(BLOCKS, -1).astype(jnp.int32)
     packet = packet.reshape(BLOCKS * ROWS, LANES)
@@ -450,6 +494,7 @@
         scratch_shapes=[
             pltpu.VMEM((planes, fft_size * bands, LANES), F32),
             pltpu.VMEM((fft_size, planes, bands, LANES), F32),
+            pltpu.VMEM((8, 2 * planes * bands, 2 * LANES), BF16),
         ],
         compiler_params=params,
         cost_estimate=pl.CostEstimate(
@@ -482,14 +527,10 @@
 
 
 def per_device(trial_block, all_bands, potential, positions, sphere_slots):
-    parts = lax.axis_size(SIDE)
-    rows, coefs = all_bands.shape
-    width = -(-coefs // (LANES * parts)) * LANES
-    pieces = jnp.concatenate([all_bands, trial_block], axis=0)
-    pieces = jnp.pad(pieces, ((0, 0), (0, parts * width - coefs)))
-    pieces = pieces.reshape(-1, parts, width).transpose(1, 0, 2)
-    applied, pieces, trial = apply_hamiltonian(trial_block, potential, positions, sphere_slots, pieces)
-    pieces = pieces.reshape(parts * rows, width)
+    applied, pieces, trial = apply_hamiltonian(
+        trial_block, potential, positions, sphere_slots, all_bands
+    )
+    pieces = pieces.reshape(-1, pieces.shape[2])
     products = [
         jnp.einsum("ag,bg->ab", pieces, block, precision=lax.Precision.HIGH)
         for block in (trial, applied)

time: 220 us -> 216 us (0.982)
  Pallas kernels: 43.4 us -> 36.8 us
  starting transfers between devices: 63.7 us -> 66.7 us
    pallas_call x1, Pallas kernels: 25.9 us -> 22.3 us  [apply_hamiltonian(): pl.pallas_call(plane_kernel, out_shape=f32(gathered.shape), scratch_shape...]
    all_to_all x1, starting transfers between devices: 5.5 us -> 8.75 us  [apply_hamiltonian(): gathered = lax.all_to_all(mixed, GROUP, 0, 0, tiled=True)]
    ppermute x2, starting transfers between devices: 16.5 us -> 13.4 us  [swapped(): return lax.ppermute(block, axis, ((0, 1), (1, 0)))]
    all_to_all x1, starting transfers between devices: 9.93 us -> 12.5 us  [apply_hamiltonian(): applied = lax.all_to_all(applied, BAND + ('l2',), 0, 0, tiled=True)]
  transfers between devices with their start and end apart: 9 -> 9, of which waited for: 5 -> 5; matrix products, arithmetic and copies ran while one was open for 0% -> 0% of each run, Pallas kernels for 16% -> 14%
where the time goes in v4:
time: 216 us; the launch traced here: 215 us
  waiting for transfers between devices  74.7 us (35%)
  starting transfers between devices  66.7 us (31%)
  Pallas kernels  36.8 us (17%)
  blocking collectives  28.2 us (13%)
  local copies, waits for them, and re-layouts  5.45 us (3%)
    all_to_all x1, blocking collectives, per_device(): near = lax.all_to_all(products, NEAR, 0, 0, tiled=True)  28.2 us
    pallas_call x1, Pallas kernels, apply_hamiltonian(): pl.pallas_call(plane_kernel, out_shape=f32(gathered.shape), scratch_shape...  22.3 us
    all_to_all x1, waiting for transfers between devices, apply_hamiltonian(): returned = lax.all_to_all(weighted, GROUP, 0, 0, tiled=True)  20.3 us
    all_to_all x1, waiting for transfers between devices, apply_hamiltonian(): gathered = lax.all_to_all(mixed, GROUP, 0, 0, tiled=True)  19.5 us
    all_to_all x1, waiting for transfers between devices, apply_hamiltonian(): applied = lax.all_to_all(applied, BAND + ('l2',), 0, 0, tiled=True)  17.7 us
    ppermute x2, starting transfers between devices, swapped(): return lax.ppermute(block, axis, ((0, 1), (1, 0)))  13.4 us
    all_to_all x1, starting transfers between devices, apply_hamiltonian(): applied = lax.all_to_all(applied, BAND + ('l2',), 0, 0, tiled=True)  12.5 us
    ppermute x2, starting transfers between devices, apply_hamiltonian(): lax.ppermute(part, BAND + FFT, swap_pairs(turn))  10.9 us
  transfers between devices with their start and end apart: 9, of which 5 were waited for; matrix products, arithmetic and copies ran while one was open for 0% of the time, Pallas kernels for 14%

profile of v4, /device:TPU:1, one launch (start us, length us, event | category | flops | bytes accessed | tf_op | source)
XLA Modules:
  0.0 215.4 jit_solution(2819887276583699950)
XLA Ops:
  0.6 0.9 copy-done.1
  2.3 1.2 pack.1
  3.6 1.2 select_maximum_fusion
  5.0 1.2 copy.23
  6.3 10.5 %all-to-all-start = ((f32[8,40,896]{2,1,0:T(8,128)}), f32[8,40,896]{2,1,0:T(8,128)S(1)}, u32[]{:S(2)}, u32[]{:S(2)}) async-start(f32[8,40,896]{2,1,0:T(8,128)} %copy.23), calls=%async_computation | async-start | bytes 2293760 | tf_op jit(solution)/shard_map/all_to_all | solution.py:485
  16.7 4.6 %collective-permute-start = (f32[256,128]{1,0:T(8,128)S(1)}, f32[256,128]{1,0:T(8,128)S(1)}, u32[]{:S(2)}, u32[]{:S(2)}) collective-permute-start(f32[256,128]{1,0:T(8,128)S(1)} %get-tuple-element.19), channel_id=1, source_target_pairs={{0,4},{4,0},{1,5},{5,1},{2,6},{6,2},{3,7},{7,3},{8,12},{12,8},{9,1... | collective-permute-start | bytes 393224 | tf_op jit(solution)/shard_map/ppermute | solution.py:412
  21.3 1.1 filter.1
  22.5 9.0 %collective-permute-start.1 = (f32[3,128,128]{2,1,0:T(8,128)S(1)}, f32[3,128,128]{2,1,0:T(8,128)S(1)}, u32[]{:S(2)}, u32[]{:S(2)}) collective-permute-start(f32[3,128,128]{2,1,0:T(8,128)S(1)} %get-tuple-element.32), channel_id=1, source_target_pairs={{0,0},{1,1},{2,2},{3,3},{96,4},{97,5},{98,6},{99,7},{8,8},{9,9},{1... | collective-permute-start | bytes 589832 | tf_op jit(solution)/shard_map/ppermute | solution.py:467
  31.5 1.9 collective-permute-start.2
  33.5 7.9 %collective-permute-done = f32[256,128]{1,0:T(8,128)S(1)} collective-permute-done((f32[256,128]{1,0:T(8,128)S(1)}, f32[256,128]{1,0:T(8,128)S(1)}, u32[]{:S(2)}, u32[]{:S(2)}) %collective-permute-start) | collective-permute-done | bytes 131104 | tf_op jit(solution)/shard_map/ppermute | solution.py:412
  41.5 5.2 %forward.1 = f32[1536,128]{1,0:T(8,128)} custom-call(s32[2,256]{1,0:T(2,128)S(1)} %bitcast.44, f32[512,128]{1,0:T(8,128)S(1)} %bitcast.36, bf16[192,576]{1,0:T(8,128)(2,1)S(1)} %copy-done.2), custom_call_target="tpu_custom_call" | custom-call | tf_op jit(solution)/shard_map/forward/pallas_call | solution.py:475
  46.7 8.7 %all-to-all-start.1 = ((f32[32,48,128]{2,1,0:T(8,128)}), f32[32,48,128]{2,1,0:T(8,128)S(1)}, u32[]{:S(2)}, u32[]{:S(2)}) async-start(f32[32,48,128]{2,1,0:T(8,128)} %bitcast.8), calls=%async_computation.1 | async-start | bytes 1572864 | tf_op jit(solution)/shard_map/all_to_all | solution.py:487
  55.5 0.8 boxes.1
  56.3 19.5 %all-to-all-done.1 = f32[32,48,128]{2,1,0:T(8,128)S(1)} async-done(((f32[32,48,128]{2,1,0:T(8,128)}), f32[32,48,128]{2,1,0:T(8,128)S(1)}, u32[]{:S(2)}, u32[]{:S(2)}) %all-to-all-start.1) | async-done | bytes 786464 | tf_op jit(solution)/shard_map/all_to_all | solution.py:487
  75.8 8.8 %collective-permute-start.3 = (f32[64,896]{1,0:T(8,128)S(1)}, f32[64,896]{1,0:T(8,128)S(1)}, u32[]{:S(2)}, u32[]{:S(2)}) collective-permute-start(f32[64,896]{1,0:T(8,128)S(1)} %slice_bitcast_fusion), channel_id=1, source_target_pairs={{0,64},{64,0},{1,65},{65,1},{2,66},{66,2},{3,67},{67,3},{4,68},{68... | collective-permute-start | bytes 688136 | tf_op jit(solution)/shard_map/ppermute | solution.py:412
  84.7 22.3 %planes.1 = f32[1536,128]{1,0:T(8,128)} custom-call(s32[64,128]{1,0:T(8,128)S(1)} %get-tuple-element.26.inverse_ref, s32[32,128]{1,0:T(8,128)S(1)} %get-tuple-element.27.box_ref, bf16[384,256]{1,0:T(8,128)(2,1)S(1)} %copy-done.8, bf16[128,192]{1,0:T(8,128)(2,1)S(1)} %copy-done.10, bf16[128,128]{1,0:T(8,128)(2,1)S(1)} %copy-done.11, ...), custom_call_target="tpu_custom_call" | custom-call | flops 24999999488 | bytes 60000000 | tf_op jit(solution)/shard_map/planes/pallas_call | solution.py:491
  107.1 6.4 %all-to-all-start.2 = ((f32[32,48,128]{2,1,0:T(8,128)}), f32[32,48,128]{2,1,0:T(8,128)S(1)}, u32[]{:S(2)}, u32[]{:S(2)}) async-start(f32[32,48,128]{2,1,0:T(8,128)} %bitcast.13), calls=%async_computation.2 | async-start | bytes 1572864 | tf_op jit(solution)/shard_map/all_to_all | solution.py:506
  113.5 20.3 %all-to-all-done.2 = f32[32,48,128]{2,1,0:T(8,128)S(1)} async-done(((f32[32,48,128]{2,1,0:T(8,128)}), f32[32,48,128]{2,1,0:T(8,128)S(1)}, u32[]{:S(2)}, u32[]{:S(2)}) %all-to-all-start.2) | async-done | bytes 786464 | tf_op jit(solution)/shard_map/all_to_all | solution.py:506
  133.8 6.1 %backward.1 = f32[1024,128]{1,0:T(8,128)} custom-call(s32[2,256]{1,0:T(2,128)S(1)} %bitcast.45, f32[512,128]{1,0:T(8,128)S(1)} %bitcast.37, s32[2,128]{1,0:T(2,128)S(1)} %bitcast.46, bf16[192,576]{1,0:T(8,128)(2,1)S(1)} %copy-done.7, f32[1536,128]{1,0:T(8,128)S(1)} %bitcast.38), custom_call_target="tpu_custom_call" | custom-call | flops 8000000000 | bytes 16000000 | tf_op jit(solution)/shard_map/backward/pallas_call | solution.py:509
  139.9 12.5 %all-to-all-start.3 = ((f32[32,32,128]{2,1,0:T(8,128)}), f32[32,32,128]{2,1,0:T(8,128)S(1)}, u32[]{:S(2)}, u32[]{:S(2)}) async-start(f32[32,32,128]{2,1,0:T(8,128)} %bitcast.15), calls=%async_computation.3 | async-start | bytes 1048576 | tf_op jit(solution)/shard_map/all_to_all | solution.py:523
  153.0 17.7 %all-to-all-done.3 = f32[32,32,128]{2,1,0:T(8,128)S(1)} async-done(((f32[32,32,128]{2,1,0:T(8,128)}), f32[32,32,128]{2,1,0:T(8,128)S(1)}, u32[]{:S(2)}, u32[]{:S(2)}) %all-to-all-start.3) | async-done | bytes 524320 | tf_op jit(solution)/shard_map/all_to_all | solution.py:523
  171.6 28.2 %all_to_all.55 = f32[32,8,256]{2,1,0:T(8,128)S(1)} all-to-all(f32[32,8,256]{2,1,0:T(8,128)S(1)} %bitcast.53), channel_id=1, replica_groups=mesh['y'=4,'zh'=2,'c'=2,'x'=4,'l2'=2,'ll'=4] {'y','c','x'}, dimensions={0} | all-to-all | bytes 524288 | tf_op jit(solution)/shard_map/all_to_all | solution.py:540
  200.5 4.2 %all-to-all-start.5 = ((f32[8,1,256]{2,1,0:T(1,128)}), f32[8,1,256]{2,1,0:T(1,128)S(1)}, u32[]{:S(2)}, u32[]{:S(2)}) async-start(f32[8,1,256]{2,1,0:T(1,128)} %all_to_all.47), calls=%async_computation.5 | async-start | bytes 16384 | tf_op jit(solution)/shard_map/all_to_all | solution.py:542
  204.8 9.3 %all-to-all-done.5 = f32[8,1,256]{2,1,0:T(1,128)S(1)} async-done(((f32[8,1,256]{2,1,0:T(1,128)}), f32[8,1,256]{2,1,0:T(1,128)S(1)}, u32[]{:S(2)}, u32[]{:S(2)}) %all-to-all-start.5) | async-done | bytes 8224 | tf_op jit(solution)/shard_map/all_to_all | solution.py:542
  (49 shorter events, 4.6 us)
Async XLA Ops:
  0.6 0.9 copy-start.1
  1.6 0.7 copy-start.5
  6.3 15.1 %copy-start = (f32[6,192,192]{2,1,0:T(8,128)S(1)}, f32[6,192,192]{2,1,0:T(8,128)}, u32[]{:S(2)}) copy-start(f32[6,192,192]{2,1,0:T(8,128)} %potential_ref) | copy-start | bytes 2654212
  6.3 15.1 %copy-start.3 = (bf16[128,576]{1,0:T(8,128)(2,1)S(1)}, bf16[128,576]{1,0:T(8,128)(2,1)}, u32[]{:S(2)}) copy-start(bf16[128,576]{1,0:T(8,128)(2,1)} %constant.69.clone.filter_ref) | copy-start | bytes 442372
  6.3 15.1 %copy-start.4 = (bf16[2,192,128]{2,1,0:T(8,128)(2,1)S(1)}, bf16[2,192,128]{2,1,0:T(8,128)(2,1)}, u32[]{:S(2)}) copy-start(bf16[2,192,128]{2,1,0:T(8,128)(2,1)} %constant.70.clone.filter_t_ref) | copy-start | bytes 294916
  6.3 40.5 %all-to-all-start = ((f32[8,40,896]{2,1,0:T(8,128)}), f32[8,40,896]{2,1,0:T(8,128)S(1)}, u32[]{:S(2)}, u32[]{:S(2)}) async-start(f32[8,40,896]{2,1,0:T(8,128)} %copy.23), calls=%async_computation | async-start | bytes 2293760 | tf_op jit(solution)/shard_map/all_to_all | solution.py:485
  16.7 24.7 %copy-start.2 = (bf16[192,576]{1,0:T(8,128)(2,1)S(1)}, bf16[192,576]{1,0:T(8,128)(2,1)}, u32[]{:S(2)}) copy-start(bf16[192,576]{1,0:T(8,128)(2,1)} %constant.67.clone.cas_ref) | copy-start | bytes 663556
  16.7 24.7 %collective-permute-start = (f32[256,128]{1,0:T(8,128)S(1)}, f32[256,128]{1,0:T(8,128)S(1)}, u32[]{:S(2)}, u32[]{:S(2)}) collective-permute-start(f32[256,128]{1,0:T(8,128)S(1)} %get-tuple-element.19), channel_id=1, source_target_pairs={{0,4},{4,0},{1,5},{5,1},{2,6},{6,2},{3,7},{7,3},{8,12},{12,8},{9,1... | collective-permute-start | bytes 393224 | tf_op jit(solution)/shard_map/ppermute | solution.py:412
  22.5 24.1 %collective-permute-start.1 = (f32[3,128,128]{2,1,0:T(8,128)S(1)}, f32[3,128,128]{2,1,0:T(8,128)S(1)}, u32[]{:S(2)}, u32[]{:S(2)}) collective-permute-start(f32[3,128,128]{2,1,0:T(8,128)S(1)} %get-tuple-element.32), channel_id=1, source_target_pairs={{0,0},{1,1},{2,2},{3,3},{96,4},{97,5},{98,6},{99,7},{8,8},{9,9},{1... | collective-permute-start | bytes 589832 | tf_op jit(solution)/shard_map/ppermute | solution.py:467
  31.5 15.1 %collective-permute-start.2 = (f32[3,128,128]{2,1,0:T(8,128)S(1)}, f32[3,128,128]{2,1,0:T(8,128)S(1)}, u32[]{:S(2)}, u32[]{:S(2)}) collective-permute-start(f32[3,128,128]{2,1,0:T(8,128)S(1)} %get-tuple-element.33), channel_id=1, source_target_pairs={{0,0},{1,1},{2,2},{3,3},{32,4},{33,5},{34,6},{35,7},{8,8},{9,9},{1... | collective-permute-start | bytes 589832 | tf_op jit(solution)/shard_map/ppermute | solution.py:467
  46.6 8.9 %copy-start.6 = (s32[4096]{0:T(1024)S(1)}, s32[4096]{0:T(1024)}, u32[]{:S(2)}) copy-start(s32[4096]{0:T(1024)} %param.16) | copy-start | bytes 49156
  46.7 38.0 %copy-start.8 = (bf16[384,256]{1,0:T(8,128)(2,1)S(1)}, bf16[384,256]{1,0:T(8,128)(2,1)}, u32[]{:S(2)}) copy-start(bf16[384,256]{1,0:T(8,128)(2,1)} %constant.71.clone.y_ref) | copy-start | bytes 589828
  46.7 38.0 %copy-start.9 = (bf16[2,256,128]{2,1,0:T(8,128)(2,1)S(1)}, bf16[2,256,128]{2,1,0:T(8,128)(2,1)}, u32[]{:S(2)}) copy-start(bf16[2,256,128]{2,1,0:T(8,128)(2,1)} %constant.74.clone.y_back_ref) | copy-start | bytes 393220
  46.7 38.0 %copy-start.10 = (bf16[128,192]{1,0:T(8,128)(2,1)S(1)}, bf16[128,192]{1,0:T(8,128)(2,1)}, u32[]{:S(2)}) copy-start(bf16[128,192]{1,0:T(8,128)(2,1)} %constant.72.clone.x_ref) | copy-start | bytes 147460
  46.7 38.0 %copy-start.11 = (bf16[128,128]{1,0:T(8,128)(2,1)S(1)}, bf16[128,128]{1,0:T(8,128)(2,1)}, u32[]{:S(2)}) copy-start(bf16[128,128]{1,0:T(8,128)(2,1)} %constant.73.clone.x_back_ref) | copy-start | bytes 98308
  46.7 29.1 %all-to-all-start.1 = ((f32[32,48,128]{2,1,0:T(8,128)}), f32[32,48,128]{2,1,0:T(8,128)S(1)}, u32[]{:S(2)}, u32[]{:S(2)}) async-start(f32[32,48,128]{2,1,0:T(8,128)} %bitcast.8), calls=%async_computation.1 | async-start | bytes 1572864 | tf_op jit(solution)/shard_map/all_to_all | solution.py:487
  75.8 31.2 %collective-permute-start.3 = (f32[64,896]{1,0:T(8,128)S(1)}, f32[64,896]{1,0:T(8,128)S(1)}, u32[]{:S(2)}, u32[]{:S(2)}) collective-permute-start(f32[64,896]{1,0:T(8,128)S(1)} %slice_bitcast_fusion), channel_id=1, source_target_pairs={{0,64},{64,0},{1,65},{65,1},{2,66},{66,2},{3,67},{67,3},{4,68},{68... | collective-permute-start | bytes 688136 | tf_op jit(solution)/shard_map/ppermute | solution.py:412
  107.1 26.7 %copy-start.7 = (bf16[192,576]{1,0:T(8,128)(2,1)S(1)}, bf16[192,576]{1,0:T(8,128)(2,1)}, u32[]{:S(2)}) copy-start(bf16[192,576]{1,0:T(8,128)(2,1)} %constant.68.clone.cas_ref) | copy-start | bytes 663556
  107.1 26.7 %all-to-all-start.2 = ((f32[32,48,128]{2,1,0:T(8,128)}), f32[32,48,128]{2,1,0:T(8,128)S(1)}, u32[]{:S(2)}, u32[]{:S(2)}) async-start(f32[32,48,128]{2,1,0:T(8,128)} %bitcast.13), calls=%async_computation.2 | async-start | bytes 1572864 | tf_op jit(solution)/shard_map/all_to_all | solution.py:506
  139.9 30.8 %all-to-all-start.3 = ((f32[32,32,128]{2,1,0:T(8,128)}), f32[32,32,128]{2,1,0:T(8,128)S(1)}, u32[]{:S(2)}, u32[]{:S(2)}) async-start(f32[32,32,128]{2,1,0:T(8,128)} %bitcast.15), calls=%async_computation.3 | async-start | bytes 1048576 | tf_op jit(solution)/shard_map/all_to_all | solution.py:523
  200.5 13.6 %all-to-all-start.5 = ((f32[8,1,256]{2,1,0:T(1,128)}), f32[8,1,256]{2,1,0:T(1,128)S(1)}, u32[]{:S(2)}, u32[]{:S(2)}) async-start(f32[8,1,256]{2,1,0:T(1,128)} %all_to_all.47), calls=%async_computation.5 | async-start | bytes 16384 | tf_op jit(solution)/shard_map/all_to_all | solution.py:542

commit v5 on v4

--- a/solution.py
+++ b/solution.py
@@ -215,21 +215,62 @@
     for source, plane, core, row in places:
         staged[source, plane, core * HALF : (core + 1) * HALF] = columns_ref[row : row + HALF, :]
 
-    def fill(block, carry):
-        source_of = jnp.broadcast_to(inverse_ref[pl.ds(block, 1), :], (bands, LANES))
-        lane_of = jnp.broadcast_to(inverse_ref[pl.ds(block + blocks, 1), :], (bands, LANES))
+    steps = products.shape[0]
+    first_product = blocks - 2 * steps
+    lane_rows = lax.broadcasted_iota(jnp.int32, (2 * LANES, 2 * LANES), 0)
+
+    def stage_products(piece):
+        for step in range(steps):
+            for plane in range(0, planes, 2):
+                sides = [
+                    jnp.concatenate([piece(plane, at), piece(plane + 1, at)], axis=0)
+                    for at in (first_product + 2 * step, first_product + 2 * step + 1)
+                ]
+                high, low = split(jnp.concatenate(sides, axis=1))
+                products[step, plane * bands : (plane + 2) * bands, :] = high
+                products[step, (planes + plane) * bands : (planes + plane + 2) * bands, :] = low
+
+    def one_hot_part(wide):
+        rest = jnp.zeros((2 * planes * bands, 2 * LANES), F32)
+        for step in range(steps):
+            low = (first_product + 2 * step) * LANES
+            rest = rest + dot(products[step], (wide - low == lane_rows).astype(F32).astype(BF16))
+        return rest[: planes * bands] + rest[planes * bands :]
+
+    def gather_part(piece, from_of, lane_of):
         values = [jnp.zeros((bands, LANES), F32) for _ in range(planes)]
-        for source in range(sources):
-            here = source_of == source
+        for at in range(first_product):
+            here = from_of == at
             for plane in range(planes):
-                values[plane] = jnp.where(
-                    here, take_lanes(staged[source, plane], lane_of), values[plane]
+                values[plane] = jnp.where(here, take_lanes(piece(plane, at), lane_of), values[plane])
+        return values
+
+    def column_piece(plane, source):
+        return staged[source, plane]
+
+    def box_piece(plane, block):
+        return boxes[plane, block * bands : (block + 1) * bands, :]
+
+    stage_products(column_piece)
+
+    def fill(pair, carry):
+        from_rows = [inverse_ref[pl.ds(pair * 2 + side, 1), :] for side in range(2)]
+        lane_rows_of = [inverse_ref[pl.ds(pair * 2 + side + blocks, 1), :] for side in range(2)]
+        wide = [from_rows[side] * LANES + lane_rows_of[side] for side in range(2)]
+        rest = one_hot_part(jnp.concatenate(wide, axis=1))
+        for side in range(2):
+            from_of = jnp.broadcast_to(from_rows[side], (bands, LANES))
+            lane_of = jnp.broadcast_to(lane_rows_of[side], (bands, LANES))
+            values = gather_part(column_piece, from_of, lane_of)
+            goal = pl.ds(pl.multiple_of((pair * 2 + side) * bands, bands), bands)
+            for plane in range(planes):
+                cut = slice(plane * bands, (plane + 1) * bands)
+                boxes[plane, goal, :] = (
+                    values[plane] + rest[cut, side * LANES : (side + 1) * LANES]
                 )
-        for plane in range(planes):
-            boxes[plane, pl.ds(pl.multiple_of(block * bands, bands), bands), :] = values[plane]
         return carry
 
-    lax.fori_loop(0, blocks, fill, 0)
+    lax.fori_loop(0, blocks // 2, fill, 0)
 
     def transform(plane, carry):
         stacked = jnp.concatenate(
@@ -263,39 +304,16 @@
 
     lax.fori_loop(0, planes, transform, 0)
 
-    first_product = blocks - 2 * products.shape[0]
-    for pair in range(products.shape[0]):
-        for plane in range(0, planes, 2):
-            sides = []
-            for block in (first_product + 2 * pair, first_product + 2 * pair + 1):
-                cut = slice(block * bands, (block + 1) * bands)
-                sides.append(jnp.concatenate([boxes[plane, cut, :], boxes[plane + 1, cut, :]], axis=0))
-            high, low = split(jnp.concatenate(sides, axis=1))
-            products[pair, plane * bands : (plane + 2) * bands, :] = high
-            products[pair, (planes + plane) * bands : (planes + plane + 2) * bands, :] = low
-    lane_rows = lax.broadcasted_iota(jnp.int32, (2 * LANES, 2 * LANES), 0)
+    stage_products(box_piece)
 
     def pick(pair, carry):
         places = [box_ref[pl.ds(pair * 2 + side, 1), :] for side in range(2)]
-        wide = jnp.concatenate(places, axis=1)
-        rest = jnp.zeros((2 * planes * bands, 2 * LANES), F32)
-        for step in range(products.shape[0]):
-            low = (first_product + 2 * step) * LANES
-            rest = rest + dot(products[step], (wide - low == lane_rows).astype(F32).astype(BF16))
-        rest = rest[: planes * bands] + rest[planes * bands :]
+        rest = one_hot_part(jnp.concatenate(places, axis=1))
         for side in range(2):
             place = jnp.broadcast_to(places[side], (bands, LANES))
-            lane_of = place & (LANES - 1)
-            block_of = lax.shift_right_logical(place, 7)
-            values = [jnp.zeros((bands, LANES), F32) for _ in range(planes)]
-            for block in range(first_product):
-                here = block_of == block
-                for plane in range(planes):
-                    values[plane] = jnp.where(
-                        here,
-                        take_lanes(boxes[plane, block * bands : (block + 1) * bands, :], lane_of),
-                        values[plane],
-                    )
+            values = gather_part(
+                box_piece, lax.shift_right_logical(place, 7), place & (LANES - 1)
+            )
             for plane in range(planes):
                 cut = slice(plane * bands, (plane + 1) * bands)
                 staged[pair * 2 + side, plane] = (

time: 216 us -> 216 us (level)
  starting transfers between devices: 66.7 us -> 70.4 us
  Pallas kernels: 36.8 us -> 33.2 us
    all_to_all x1, starting transfers between devices: 6.4 us -> 9.92 us  [apply_hamiltonian(): returned = lax.all_to_all(weighted, GROUP, 0, 0, tiled=True)]
    pallas_call x1, Pallas kernels: 22.3 us -> 18.8 us  [apply_hamiltonian(): pl.pallas_call(plane_kernel, out_shape=f32(gathered.shape), scratch_shape...]
  transfers between devices with their start and end apart: 9 -> 9, of which waited for: 5 -> 5; matrix products, arithmetic and copies ran while one was open for 0% -> 0% of each run, Pallas kernels for 14% -> 12%
where the time goes in v5:
time: 216 us; the launch traced here: 215 us
  waiting for transfers between devices  74.7 us (35%)
  starting transfers between devices  70.4 us (33%)
  Pallas kernels  33.2 us (15%)
  blocking collectives  28.2 us (13%)
  local copies, waits for them, and re-layouts  5.45 us (3%)
    all_to_all x1, blocking collectives, per_device(): near = lax.all_to_all(products, NEAR, 0, 0, tiled=True)  28.2 us
    all_to_all x1, waiting for transfers between devices, apply_hamiltonian(): returned = lax.all_to_all(weighted, GROUP, 0, 0, tiled=True)  20.3 us
    all_to_all x1, waiting for transfers between devices, apply_hamiltonian(): gathered = lax.all_to_all(mixed, GROUP, 0, 0, tiled=True)  19.5 us
    pallas_call x1, Pallas kernels, apply_hamiltonian(): pl.pallas_call(plane_kernel, out_shape=f32(gathered.shape), scratch_shape...  18.8 us
    all_to_all x1, waiting for transfers between devices, apply_hamiltonian(): applied = lax.all_to_all(applied, BAND + ('l2',), 0, 0, tiled=True)  17.6 us
    ppermute x2, starting transfers between devices, swapped(): return lax.ppermute(block, axis, ((0, 1), (1, 0)))  13.4 us
    all_to_all x1, starting transfers between devices, apply_hamiltonian(): applied = lax.all_to_all(applied, BAND + ('l2',), 0, 0, tiled=True)  12.6 us
    ppermute x2, starting transfers between devices, apply_hamiltonian(): lax.ppermute(part, BAND + FFT, swap_pairs(turn))  10.9 us
  transfers between devices with their start and end apart: 9, of which 5 were waited for; matrix products, arithmetic and copies ran while one was open for 0% of the time, Pallas kernels for 12%

profile of v5, /device:TPU:1, one launch (start us, length us, event | category | flops | bytes accessed | tf_op | source)
XLA Modules:
  0.0 215.5 jit_solution(3534780864306321460)
XLA Ops:
  0.6 0.9 copy-done.1
  2.3 1.2 pack.1
  3.6 1.2 select_maximum_fusion
  5.0 1.2 copy.23
  6.3 10.5 %all-to-all-start = ((f32[8,40,896]{2,1,0:T(8,128)}), f32[8,40,896]{2,1,0:T(8,128)S(1)}, u32[]{:S(2)}, u32[]{:S(2)}) async-start(f32[8,40,896]{2,1,0:T(8,128)} %copy.23), calls=%async_computation | async-start | bytes 2293760 | tf_op jit(solution)/shard_map/all_to_all | solution.py:503
  16.7 4.6 %collective-permute-start = (f32[256,128]{1,0:T(8,128)S(1)}, f32[256,128]{1,0:T(8,128)S(1)}, u32[]{:S(2)}, u32[]{:S(2)}) collective-permute-start(f32[256,128]{1,0:T(8,128)S(1)} %get-tuple-element.19), channel_id=1, source_target_pairs={{0,4},{4,0},{1,5},{5,1},{2,6},{6,2},{3,7},{7,3},{8,12},{12,8},{9,1... | collective-permute-start | bytes 393224 | tf_op jit(solution)/shard_map/ppermute | solution.py:430
  21.3 1.1 filter.1
  22.5 9.0 %collective-permute-start.1 = (f32[3,128,128]{2,1,0:T(8,128)S(1)}, f32[3,128,128]{2,1,0:T(8,128)S(1)}, u32[]{:S(2)}, u32[]{:S(2)}) collective-permute-start(f32[3,128,128]{2,1,0:T(8,128)S(1)} %get-tuple-element.32), channel_id=1, source_target_pairs={{0,0},{1,1},{2,2},{3,3},{96,4},{97,5},{98,6},{99,7},{8,8},{9,9},{1... | collective-permute-start | bytes 589832 | tf_op jit(solution)/shard_map/ppermute | solution.py:485
  31.5 1.9 collective-permute-start.2
  33.5 7.9 %collective-permute-done = f32[256,128]{1,0:T(8,128)S(1)} collective-permute-done((f32[256,128]{1,0:T(8,128)S(1)}, f32[256,128]{1,0:T(8,128)S(1)}, u32[]{:S(2)}, u32[]{:S(2)}) %collective-permute-start) | collective-permute-done | bytes 131104 | tf_op jit(solution)/shard_map/ppermute | solution.py:430
  41.5 5.2 %forward.1 = f32[1536,128]{1,0:T(8,128)} custom-call(s32[2,256]{1,0:T(2,128)S(1)} %bitcast.44, f32[512,128]{1,0:T(8,128)S(1)} %bitcast.36, bf16[192,576]{1,0:T(8,128)(2,1)S(1)} %copy-done.2), custom_call_target="tpu_custom_call" | custom-call | tf_op jit(solution)/shard_map/forward/pallas_call | solution.py:493
  46.7 8.7 %all-to-all-start.1 = ((f32[32,48,128]{2,1,0:T(8,128)}), f32[32,48,128]{2,1,0:T(8,128)S(1)}, u32[]{:S(2)}, u32[]{:S(2)}) async-start(f32[32,48,128]{2,1,0:T(8,128)} %bitcast.8), calls=%async_computation.1 | async-start | bytes 1572864 | tf_op jit(solution)/shard_map/all_to_all | solution.py:505
  55.5 0.8 boxes.1
  56.3 19.5 %all-to-all-done.1 = f32[32,48,128]{2,1,0:T(8,128)S(1)} async-done(((f32[32,48,128]{2,1,0:T(8,128)}), f32[32,48,128]{2,1,0:T(8,128)S(1)}, u32[]{:S(2)}, u32[]{:S(2)}) %all-to-all-start.1) | async-done | bytes 786464 | tf_op jit(solution)/shard_map/all_to_all | solution.py:505
  75.8 8.8 %collective-permute-start.3 = (f32[64,896]{1,0:T(8,128)S(1)}, f32[64,896]{1,0:T(8,128)S(1)}, u32[]{:S(2)}, u32[]{:S(2)}) collective-permute-start(f32[64,896]{1,0:T(8,128)S(1)} %slice_bitcast_fusion), channel_id=1, source_target_pairs={{0,64},{64,0},{1,65},{65,1},{2,66},{66,2},{3,67},{67,3},{4,68},{68... | collective-permute-start | bytes 688136 | tf_op jit(solution)/shard_map/ppermute | solution.py:430
  84.7 18.8 %planes.1 = f32[1536,128]{1,0:T(8,128)} custom-call(s32[64,128]{1,0:T(8,128)S(1)} %get-tuple-element.26.inverse_ref, s32[32,128]{1,0:T(8,128)S(1)} %get-tuple-element.27.box_ref, bf16[384,256]{1,0:T(8,128)(2,1)S(1)} %copy-done.8, bf16[128,192]{1,0:T(8,128)(2,1)S(1)} %copy-done.10, bf16[128,128]{1,0:T(8,128)(2,1)S(1)} %copy-done.11, ...), custom_call_target="tpu_custom_call" | custom-call | flops 24999999488 | bytes 60000000 | tf_op jit(solution)/shard_map/planes/pallas_call | solution.py:509
  103.5 9.9 %all-to-all-start.2 = ((f32[32,48,128]{2,1,0:T(8,128)}), f32[32,48,128]{2,1,0:T(8,128)S(1)}, u32[]{:S(2)}, u32[]{:S(2)}) async-start(f32[32,48,128]{2,1,0:T(8,128)} %bitcast.13), calls=%async_computation.2 | async-start | bytes 1572864 | tf_op jit(solution)/shard_map/all_to_all | solution.py:524
  113.5 20.3 %all-to-all-done.2 = f32[32,48,128]{2,1,0:T(8,128)S(1)} async-done(((f32[32,48,128]{2,1,0:T(8,128)}), f32[32,48,128]{2,1,0:T(8,128)S(1)}, u32[]{:S(2)}, u32[]{:S(2)}) %all-to-all-start.2) | async-done | bytes 786464 | tf_op jit(solution)/shard_map/all_to_all | solution.py:524
  133.8 6.1 %backward.1 = f32[1024,128]{1,0:T(8,128)} custom-call(s32[2,256]{1,0:T(2,128)S(1)} %bitcast.45, f32[512,128]{1,0:T(8,128)S(1)} %bitcast.37, s32[2,128]{1,0:T(2,128)S(1)} %bitcast.46, bf16[192,576]{1,0:T(8,128)(2,1)S(1)} %copy-done.7, f32[1536,128]{1,0:T(8,128)S(1)} %bitcast.38), custom_call_target="tpu_custom_call" | custom-call | flops 8000000000 | bytes 16000000 | tf_op jit(solution)/shard_map/backward/pallas_call | solution.py:527
  139.9 12.6 %all-to-all-start.3 = ((f32[32,32,128]{2,1,0:T(8,128)}), f32[32,32,128]{2,1,0:T(8,128)S(1)}, u32[]{:S(2)}, u32[]{:S(2)}) async-start(f32[32,32,128]{2,1,0:T(8,128)} %bitcast.15), calls=%async_computation.3 | async-start | bytes 1048576 | tf_op jit(solution)/shard_map/all_to_all | solution.py:541
  153.1 17.6 %all-to-all-done.3 = f32[32,32,128]{2,1,0:T(8,128)S(1)} async-done(((f32[32,32,128]{2,1,0:T(8,128)}), f32[32,32,128]{2,1,0:T(8,128)S(1)}, u32[]{:S(2)}, u32[]{:S(2)}) %all-to-all-start.3) | async-done | bytes 524320 | tf_op jit(solution)/shard_map/all_to_all | solution.py:541
  171.7 28.2 %all_to_all.55 = f32[32,8,256]{2,1,0:T(8,128)S(1)} all-to-all(f32[32,8,256]{2,1,0:T(8,128)S(1)} %bitcast.53), channel_id=1, replica_groups=mesh['y'=4,'zh'=2,'c'=2,'x'=4,'l2'=2,'ll'=4] {'y','c','x'}, dimensions={0} | all-to-all | bytes 524288 | tf_op jit(solution)/shard_map/all_to_all | solution.py:558
  200.6 4.3 %all-to-all-start.5 = ((f32[8,1,256]{2,1,0:T(1,128)}), f32[8,1,256]{2,1,0:T(1,128)S(1)}, u32[]{:S(2)}, u32[]{:S(2)}) async-start(f32[8,1,256]{2,1,0:T(1,128)} %all_to_all.47), calls=%async_computation.5 | async-start | bytes 16384 | tf_op jit(solution)/shard_map/all_to_all | solution.py:560
  204.9 9.3 %all-to-all-done.5 = f32[8,1,256]{2,1,0:T(1,128)S(1)} async-done(((f32[8,1,256]{2,1,0:T(1,128)}), f32[8,1,256]{2,1,0:T(1,128)S(1)}, u32[]{:S(2)}, u32[]{:S(2)}) %all-to-all-start.5) | async-done | bytes 8224 | tf_op jit(solution)/shard_map/all_to_all | solution.py:560
  (49 shorter events, 4.6 us)
Async XLA Ops:
  0.6 0.9 copy-start.1
  1.6 0.7 copy-start.5
  6.3 15.1 %copy-start = (f32[6,192,192]{2,1,0:T(8,128)S(1)}, f32[6,192,192]{2,1,0:T(8,128)}, u32[]{:S(2)}) copy-start(f32[6,192,192]{2,1,0:T(8,128)} %potential_ref) | copy-start | bytes 2654212
  6.3 15.1 %copy-start.3 = (bf16[128,576]{1,0:T(8,128)(2,1)S(1)}, bf16[128,576]{1,0:T(8,128)(2,1)}, u32[]{:S(2)}) copy-start(bf16[128,576]{1,0:T(8,128)(2,1)} %constant.69.clone.filter_ref) | copy-start | bytes 442372
  6.3 15.1 %copy-start.4 = (bf16[2,192,128]{2,1,0:T(8,128)(2,1)S(1)}, bf16[2,192,128]{2,1,0:T(8,128)(2,1)}, u32[]{:S(2)}) copy-start(bf16[2,192,128]{2,1,0:T(8,128)(2,1)} %constant.70.clone.filter_t_ref) | copy-start | bytes 294916
  6.3 40.5 %all-to-all-start = ((f32[8,40,896]{2,1,0:T(8,128)}), f32[8,40,896]{2,1,0:T(8,128)S(1)}, u32[]{:S(2)}, u32[]{:S(2)}) async-start(f32[8,40,896]{2,1,0:T(8,128)} %copy.23), calls=%async_computation | async-start | bytes 2293760 | tf_op jit(solution)/shard_map/all_to_all | solution.py:503
  16.7 24.7 %copy-start.2 = (bf16[192,576]{1,0:T(8,128)(2,1)S(1)}, bf16[192,576]{1,0:T(8,128)(2,1)}, u32[]{:S(2)}) copy-start(bf16[192,576]{1,0:T(8,128)(2,1)} %constant.67.clone.cas_ref) | copy-start | bytes 663556
  16.7 24.7 %collective-permute-start = (f32[256,128]{1,0:T(8,128)S(1)}, f32[256,128]{1,0:T(8,128)S(1)}, u32[]{:S(2)}, u32[]{:S(2)}) collective-permute-start(f32[256,128]{1,0:T(8,128)S(1)} %get-tuple-element.19), channel_id=1, source_target_pairs={{0,4},{4,0},{1,5},{5,1},{2,6},{6,2},{3,7},{7,3},{8,12},{12,8},{9,1... | collective-permute-start | bytes 393224 | tf_op jit(solution)/shard_map/ppermute | solution.py:430
  22.5 24.1 %collective-permute-start.1 = (f32[3,128,128]{2,1,0:T(8,128)S(1)}, f32[3,128,128]{2,1,0:T(8,128)S(1)}, u32[]{:S(2)}, u32[]{:S(2)}) collective-permute-start(f32[3,128,128]{2,1,0:T(8,128)S(1)} %get-tuple-element.32), channel_id=1, source_target_pairs={{0,0},{1,1},{2,2},{3,3},{96,4},{97,5},{98,6},{99,7},{8,8},{9,9},{1... | collective-permute-start | bytes 589832 | tf_op jit(solution)/shard_map/ppermute | solution.py:485
  31.5 15.1 %collective-permute-start.2 = (f32[3,128,128]{2,1,0:T(8,128)S(1)}, f32[3,128,128]{2,1,0:T(8,128)S(1)}, u32[]{:S(2)}, u32[]{:S(2)}) collective-permute-start(f32[3,128,128]{2,1,0:T(8,128)S(1)} %get-tuple-element.33), channel_id=1, source_target_pairs={{0,0},{1,1},{2,2},{3,3},{32,4},{33,5},{34,6},{35,7},{8,8},{9,9},{1... | collective-permute-start | bytes 589832 | tf_op jit(solution)/shard_map/ppermute | solution.py:485
  46.6 8.9 %copy-start.6 = (s32[4096]{0:T(1024)S(1)}, s32[4096]{0:T(1024)}, u32[]{:S(2)}) copy-start(s32[4096]{0:T(1024)} %param.16) | copy-start | bytes 49156
  46.7 38.0 %copy-start.8 = (bf16[384,256]{1,0:T(8,128)(2,1)S(1)}, bf16[384,256]{1,0:T(8,128)(2,1)}, u32[]{:S(2)}) copy-start(bf16[384,256]{1,0:T(8,128)(2,1)} %constant.71.clone.y_ref) | copy-start | bytes 589828
  46.7 38.0 %copy-start.9 = (bf16[2,256,128]{2,1,0:T(8,128)(2,1)S(1)}, bf16[2,256,128]{2,1,0:T(8,128)(2,1)}, u32[]{:S(2)}) copy-start(bf16[2,256,128]{2,1,0:T(8,128)(2,1)} %constant.74.clone.y_back_ref) | copy-start | bytes 393220
  46.7 38.0 %copy-start.10 = (bf16[128,192]{1,0:T(8,128)(2,1)S(1)}, bf16[128,192]{1,0:T(8,128)(2,1)}, u32[]{:S(2)}) copy-start(bf16[128,192]{1,0:T(8,128)(2,1)} %constant.72.clone.x_ref) | copy-start | bytes 147460
  46.7 38.0 %copy-start.11 = (bf16[128,128]{1,0:T(8,128)(2,1)S(1)}, bf16[128,128]{1,0:T(8,128)(2,1)}, u32[]{:S(2)}) copy-start(bf16[128,128]{1,0:T(8,128)(2,1)} %constant.73.clone.x_back_ref) | copy-start | bytes 98308
  46.7 29.1 %all-to-all-start.1 = ((f32[32,48,128]{2,1,0:T(8,128)}), f32[32,48,128]{2,1,0:T(8,128)S(1)}, u32[]{:S(2)}, u32[]{:S(2)}) async-start(f32[32,48,128]{2,1,0:T(8,128)} %bitcast.8), calls=%async_computation.1 | async-start | bytes 1572864 | tf_op jit(solution)/shard_map/all_to_all | solution.py:505
  75.8 27.7 %collective-permute-start.3 = (f32[64,896]{1,0:T(8,128)S(1)}, f32[64,896]{1,0:T(8,128)S(1)}, u32[]{:S(2)}, u32[]{:S(2)}) collective-permute-start(f32[64,896]{1,0:T(8,128)S(1)} %slice_bitcast_fusion), channel_id=1, source_target_pairs={{0,64},{64,0},{1,65},{65,1},{2,66},{66,2},{3,67},{67,3},{4,68},{68... | collective-permute-start | bytes 688136 | tf_op jit(solution)/shard_map/ppermute | solution.py:430
  103.5 30.3 %copy-start.7 = (bf16[192,576]{1,0:T(8,128)(2,1)S(1)}, bf16[192,576]{1,0:T(8,128)(2,1)}, u32[]{:S(2)}) copy-start(bf16[192,576]{1,0:T(8,128)(2,1)} %constant.68.clone.cas_ref) | copy-start | bytes 663556
  103.5 30.3 %all-to-all-start.2 = ((f32[32,48,128]{2,1,0:T(8,128)}), f32[32,48,128]{2,1,0:T(8,128)S(1)}, u32[]{:S(2)}, u32[]{:S(2)}) async-start(f32[32,48,128]{2,1,0:T(8,128)} %bitcast.13), calls=%async_computation.2 | async-start | bytes 1572864 | tf_op jit(solution)/shard_map/all_to_all | solution.py:524
  139.9 30.9 %all-to-all-start.3 = ((f32[32,32,128]{2,1,0:T(8,128)}), f32[32,32,128]{2,1,0:T(8,128)S(1)}, u32[]{:S(2)}, u32[]{:S(2)}) async-start(f32[32,32,128]{2,1,0:T(8,128)} %bitcast.15), calls=%async_computation.3 | async-start | bytes 1048576 | tf_op jit(solution)/shard_map/all_to_all | solution.py:541
  200.6 13.6 %all-to-all-start.5 = ((f32[8,1,256]{2,1,0:T(1,128)}), f32[8,1,256]{2,1,0:T(1,128)S(1)}, u32[]{:S(2)}, u32[]{:S(2)}) async-start(f32[8,1,256]{2,1,0:T(1,128)} %all_to_all.47), calls=%async_computation.5 | async-start | bytes 16384 | tf_op jit(solution)/shard_map/all_to_all | solution.py:560

commit v6 on v5

--- a/solution.py
+++ b/solution.py
@@ -504,7 +504,6 @@
     mixed, filtered, pieces = lax.optimization_barrier((mixed, filtered, pieces))
     gathered = lax.all_to_all(mixed, GROUP, 0, 0, tiled=True)
     trial = pieces[:, -bands:].reshape(-1, pieces.shape[2])
-    gathered, trial = lax.optimization_barrier((gathered, trial))
     theirs = swapped(trial, "zh")
     weighted = pl.pallas_call(
         plane_kernel,

time: 216 us -> 223 us (1.032)
  waiting for transfers between devices: 74.7 us -> 85.4 us
  starting transfers between devices: 70.4 us -> 66.4 us
    all_to_all x1, waiting for transfers between devices: 19.5 us -> 30.3 us  [apply_hamiltonian(): gathered = lax.all_to_all(mixed, GROUP, 0, 0, tiled=True)]
    all_to_all x1, starting transfers between devices: 9.92 us -> 6.04 us  [apply_hamiltonian(): returned = lax.all_to_all(weighted, GROUP, 0, 0, tiled=True)]
where the time goes in v6:
time: 223 us; the launch traced here: 222 us
  waiting for transfers between devices  85.4 us (38%)
  starting transfers between devices  66.4 us (30%)
  Pallas kernels  33.2 us (15%)
  blocking collectives  28.3 us (13%)
  local copies, waits for them, and re-layouts  5.45 us (2%)
    all_to_all x1, waiting for transfers between devices, apply_hamiltonian(): gathered = lax.all_to_all(mixed, GROUP, 0, 0, tiled=True)  30.3 us
    all_to_all x1, blocking collectives, per_device(): near = lax.all_to_all(products, NEAR, 0, 0, tiled=True)  28.3 us
    all_to_all x1, waiting for transfers between devices, apply_hamiltonian(): returned = lax.all_to_all(weighted, GROUP, 0, 0, tiled=True)  20.3 us
    pallas_call x1, Pallas kernels, apply_hamiltonian(): pl.pallas_call(plane_kernel, out_shape=f32(gathered.shape), scratch_shape...  18.8 us
    all_to_all x1, waiting for transfers between devices, apply_hamiltonian(): applied = lax.all_to_all(applied, BAND + ('l2',), 0, 0, tiled=True)  17.6 us
    ppermute x2, starting transfers between devices, swapped(): return lax.ppermute(block, axis, ((0, 1), (1, 0)))  13.4 us
    all_to_all x1, starting transfers between devices, apply_hamiltonian(): applied = lax.all_to_all(applied, BAND + ('l2',), 0, 0, tiled=True)  12.5 us
    ppermute x2, starting transfers between devices, apply_hamiltonian(): lax.ppermute(part, BAND + FFT, swap_pairs(turn))  10.9 us
  transfers between devices with their start and end apart: 9, of which 5 were waited for; matrix products, arithmetic and copies ran while one was open for 0% of the time, Pallas kernels for 12%

profile of v6, /device:TPU:1, one launch (start us, length us, event | category | flops | bytes accessed | tf_op | source)
XLA Modules:
  0.0 222.3 jit_solution(7053961820159120696)
XLA Ops:
  0.6 0.9 copy-done.1
  2.3 1.2 pack.1
  3.6 1.2 select_maximum_fusion
  5.0 1.2 copy.23
  6.3 10.5 %all-to-all-start = ((f32[8,40,896]{2,1,0:T(8,128)}), f32[8,40,896]{2,1,0:T(8,128)S(1)}, u32[]{:S(2)}, u32[]{:S(2)}) async-start(f32[8,40,896]{2,1,0:T(8,128)} %copy.23), calls=%async_computation | async-start | bytes 2293760 | tf_op jit(solution)/shard_map/all_to_all | solution.py:503
  16.7 4.6 %collective-permute-start = (f32[256,128]{1,0:T(8,128)S(1)}, f32[256,128]{1,0:T(8,128)S(1)}, u32[]{:S(2)}, u32[]{:S(2)}) collective-permute-start(f32[256,128]{1,0:T(8,128)S(1)} %get-tuple-element.17), channel_id=1, source_target_pairs={{0,4},{4,0},{1,5},{5,1},{2,6},{6,2},{3,7},{7,3},{8,12},{12,8},{9,1... | collective-permute-start | bytes 393224 | tf_op jit(solution)/shard_map/ppermute | solution.py:430
  21.3 1.1 filter.1
  22.5 9.0 %collective-permute-start.1 = (f32[3,128,128]{2,1,0:T(8,128)S(1)}, f32[3,128,128]{2,1,0:T(8,128)S(1)}, u32[]{:S(2)}, u32[]{:S(2)}) collective-permute-start(f32[3,128,128]{2,1,0:T(8,128)S(1)} %get-tuple-element.28), channel_id=1, source_target_pairs={{0,0},{1,1},{2,2},{3,3},{96,4},{97,5},{98,6},{99,7},{8,8},{9,9},{1... | collective-permute-start | bytes 589832 | tf_op jit(solution)/shard_map/ppermute | solution.py:485
  31.5 1.9 collective-permute-start.2
  33.5 7.9 %collective-permute-done = f32[256,128]{1,0:T(8,128)S(1)} collective-permute-done((f32[256,128]{1,0:T(8,128)S(1)}, f32[256,128]{1,0:T(8,128)S(1)}, u32[]{:S(2)}, u32[]{:S(2)}) %collective-permute-start) | collective-permute-done | bytes 131104 | tf_op jit(solution)/shard_map/ppermute | solution.py:430
  41.5 5.2 %forward.1 = f32[1536,128]{1,0:T(8,128)} custom-call(s32[2,256]{1,0:T(2,128)S(1)} %bitcast.44, f32[512,128]{1,0:T(8,128)S(1)} %bitcast.36, bf16[192,576]{1,0:T(8,128)(2,1)S(1)} %copy-done.2), custom_call_target="tpu_custom_call" | custom-call | tf_op jit(solution)/shard_map/forward/pallas_call | solution.py:493
  46.7 8.7 %all-to-all-start.1 = ((f32[32,48,128]{2,1,0:T(8,128)}), f32[32,48,128]{2,1,0:T(8,128)S(1)}, u32[]{:S(2)}, u32[]{:S(2)}) async-start(f32[32,48,128]{2,1,0:T(8,128)} %bitcast.9), calls=%async_computation.1 | async-start | bytes 1572864 | tf_op jit(solution)/shard_map/all_to_all | solution.py:505
  55.5 0.8 boxes.1
  56.3 8.9 %collective-permute-start.3 = (f32[64,896]{1,0:T(8,128)S(1)}, f32[64,896]{1,0:T(8,128)S(1)}, u32[]{:S(2)}, u32[]{:S(2)}) collective-permute-start(f32[64,896]{1,0:T(8,128)S(1)} %slice_bitcast_fusion), channel_id=1, source_target_pairs={{0,64},{64,0},{1,65},{65,1},{2,66},{66,2},{3,67},{67,3},{4,68},{68... | collective-permute-start | bytes 688136 | tf_op jit(solution)/shard_map/ppermute | solution.py:430
  65.2 30.3 %all-to-all-done.1 = f32[32,48,128]{2,1,0:T(8,128)S(1)} async-done(((f32[32,48,128]{2,1,0:T(8,128)}), f32[32,48,128]{2,1,0:T(8,128)S(1)}, u32[]{:S(2)}, u32[]{:S(2)}) %all-to-all-start.1) | async-done | bytes 786464 | tf_op jit(solution)/shard_map/all_to_all | solution.py:505
  95.5 18.8 %planes.1 = f32[1536,128]{1,0:T(8,128)} custom-call(s32[64,128]{1,0:T(8,128)S(1)} %get-tuple-element.22.inverse_ref, s32[32,128]{1,0:T(8,128)S(1)} %get-tuple-element.23.box_ref, bf16[384,256]{1,0:T(8,128)(2,1)S(1)} %copy-done.8, bf16[128,192]{1,0:T(8,128)(2,1)S(1)} %copy-done.10, bf16[128,128]{1,0:T(8,128)(2,1)S(1)} %copy-done.11, ...), custom_call_target="tpu_custom_call" | custom-call | flops 24999999488 | bytes 60000000 | tf_op jit(solution)/shard_map/planes/pallas_call | solution.py:508
  114.3 6.0 %all-to-all-start.2 = ((f32[32,48,128]{2,1,0:T(8,128)}), f32[32,48,128]{2,1,0:T(8,128)S(1)}, u32[]{:S(2)}, u32[]{:S(2)}) async-start(f32[32,48,128]{2,1,0:T(8,128)} %bitcast.13), calls=%async_computation.2 | async-start | bytes 1572864 | tf_op jit(solution)/shard_map/all_to_all | solution.py:523
  120.4 20.3 %all-to-all-done.2 = f32[32,48,128]{2,1,0:T(8,128)S(1)} async-done(((f32[32,48,128]{2,1,0:T(8,128)}), f32[32,48,128]{2,1,0:T(8,128)S(1)}, u32[]{:S(2)}, u32[]{:S(2)}) %all-to-all-start.2) | async-done | bytes 786464 | tf_op jit(solution)/shard_map/all_to_all | solution.py:523
  140.7 6.1 %backward.1 = f32[1024,128]{1,0:T(8,128)} custom-call(s32[2,256]{1,0:T(2,128)S(1)} %bitcast.45, f32[512,128]{1,0:T(8,128)S(1)} %bitcast.37, s32[2,128]{1,0:T(2,128)S(1)} %bitcast.46, bf16[192,576]{1,0:T(8,128)(2,1)S(1)} %copy-done.7, f32[1536,128]{1,0:T(8,128)S(1)} %bitcast.38), custom_call_target="tpu_custom_call" | custom-call | flops 8000000000 | bytes 16000000 | tf_op jit(solution)/shard_map/backward/pallas_call | solution.py:526
  146.8 12.5 %all-to-all-start.3 = ((f32[32,32,128]{2,1,0:T(8,128)}), f32[32,32,128]{2,1,0:T(8,128)S(1)}, u32[]{:S(2)}, u32[]{:S(2)}) async-start(f32[32,32,128]{2,1,0:T(8,128)} %bitcast.15), calls=%async_computation.3 | async-start | bytes 1048576 | tf_op jit(solution)/shard_map/all_to_all | solution.py:540
  159.9 17.6 %all-to-all-done.3 = f32[32,32,128]{2,1,0:T(8,128)S(1)} async-done(((f32[32,32,128]{2,1,0:T(8,128)}), f32[32,32,128]{2,1,0:T(8,128)S(1)}, u32[]{:S(2)}, u32[]{:S(2)}) %all-to-all-start.3) | async-done | bytes 524320 | tf_op jit(solution)/shard_map/all_to_all | solution.py:540
  178.5 28.3 %all_to_all.54 = f32[32,8,256]{2,1,0:T(8,128)S(1)} all-to-all(f32[32,8,256]{2,1,0:T(8,128)S(1)} %bitcast.53), channel_id=1, replica_groups=mesh['y'=4,'zh'=2,'c'=2,'x'=4,'l2'=2,'ll'=4] {'y','c','x'}, dimensions={0} | all-to-all | bytes 524288 | tf_op jit(solution)/shard_map/all_to_all | solution.py:557
  207.4 4.2 %all-to-all-start.5 = ((f32[8,1,256]{2,1,0:T(1,128)}), f32[8,1,256]{2,1,0:T(1,128)S(1)}, u32[]{:S(2)}, u32[]{:S(2)}) async-start(f32[8,1,256]{2,1,0:T(1,128)} %all_to_all.46), calls=%async_computation.5 | async-start | bytes 16384 | tf_op jit(solution)/shard_map/all_to_all | solution.py:559
  211.7 9.3 %all-to-all-done.5 = f32[8,1,256]{2,1,0:T(1,128)S(1)} async-done(((f32[8,1,256]{2,1,0:T(1,128)}), f32[8,1,256]{2,1,0:T(1,128)S(1)}, u32[]{:S(2)}, u32[]{:S(2)}) %all-to-all-start.5) | async-done | bytes 8224 | tf_op jit(solution)/shard_map/all_to_all | solution.py:559
  (49 shorter events, 4.6 us)
Async XLA Ops:
  0.6 0.9 copy-start.1
  1.6 0.7 copy-start.5
  6.3 15.1 %copy-start = (f32[6,192,192]{2,1,0:T(8,128)S(1)}, f32[6,192,192]{2,1,0:T(8,128)}, u32[]{:S(2)}) copy-start(f32[6,192,192]{2,1,0:T(8,128)} %potential_ref) | copy-start | bytes 2654212
  6.3 15.1 %copy-start.3 = (bf16[128,576]{1,0:T(8,128)(2,1)S(1)}, bf16[128,576]{1,0:T(8,128)(2,1)}, u32[]{:S(2)}) copy-start(bf16[128,576]{1,0:T(8,128)(2,1)} %constant.69.clone.filter_ref) | copy-start | bytes 442372
  6.3 15.1 %copy-start.4 = (bf16[2,192,128]{2,1,0:T(8,128)(2,1)S(1)}, bf16[2,192,128]{2,1,0:T(8,128)(2,1)}, u32[]{:S(2)}) copy-start(bf16[2,192,128]{2,1,0:T(8,128)(2,1)} %constant.70.clone.filter_t_ref) | copy-start | bytes 294916
  6.3 40.5 %all-to-all-start = ((f32[8,40,896]{2,1,0:T(8,128)}), f32[8,40,896]{2,1,0:T(8,128)S(1)}, u32[]{:S(2)}, u32[]{:S(2)}) async-start(f32[8,40,896]{2,1,0:T(8,128)} %copy.23), calls=%async_computation | async-start | bytes 2293760 | tf_op jit(solution)/shard_map/all_to_all | solution.py:503
  16.7 24.7 %copy-start.2 = (bf16[192,576]{1,0:T(8,128)(2,1)S(1)}, bf16[192,576]{1,0:T(8,128)(2,1)}, u32[]{:S(2)}) copy-start(bf16[192,576]{1,0:T(8,128)(2,1)} %constant.67.clone.cas_ref) | copy-start | bytes 663556
  16.7 24.7 %collective-permute-start = (f32[256,128]{1,0:T(8,128)S(1)}, f32[256,128]{1,0:T(8,128)S(1)}, u32[]{:S(2)}, u32[]{:S(2)}) collective-permute-start(f32[256,128]{1,0:T(8,128)S(1)} %get-tuple-element.17), channel_id=1, source_target_pairs={{0,4},{4,0},{1,5},{5,1},{2,6},{6,2},{3,7},{7,3},{8,12},{12,8},{9,1... | collective-permute-start | bytes 393224 | tf_op jit(solution)/shard_map/ppermute | solution.py:430
  22.5 24.1 %collective-permute-start.1 = (f32[3,128,128]{2,1,0:T(8,128)S(1)}, f32[3,128,128]{2,1,0:T(8,128)S(1)}, u32[]{:S(2)}, u32[]{:S(2)}) collective-permute-start(f32[3,128,128]{2,1,0:T(8,128)S(1)} %get-tuple-element.28), channel_id=1, source_target_pairs={{0,0},{1,1},{2,2},{3,3},{96,4},{97,5},{98,6},{99,7},{8,8},{9,9},{1... | collective-permute-start | bytes 589832 | tf_op jit(solution)/shard_map/ppermute | solution.py:485
  31.5 15.1 %collective-permute-start.2 = (f32[3,128,128]{2,1,0:T(8,128)S(1)}, f32[3,128,128]{2,1,0:T(8,128)S(1)}, u32[]{:S(2)}, u32[]{:S(2)}) collective-permute-start(f32[3,128,128]{2,1,0:T(8,128)S(1)} %get-tuple-element.29), channel_id=1, source_target_pairs={{0,0},{1,1},{2,2},{3,3},{32,4},{33,5},{34,6},{35,7},{8,8},{9,9},{1... | collective-permute-start | bytes 589832 | tf_op jit(solution)/shard_map/ppermute | solution.py:485
  46.6 8.9 %copy-start.6 = (s32[4096]{0:T(1024)S(1)}, s32[4096]{0:T(1024)}, u32[]{:S(2)}) copy-start(s32[4096]{0:T(1024)} %param.16) | copy-start | bytes 49156
  46.7 48.8 %copy-start.8 = (bf16[384,256]{1,0:T(8,128)(2,1)S(1)}, bf16[384,256]{1,0:T(8,128)(2,1)}, u32[]{:S(2)}) copy-start(bf16[384,256]{1,0:T(8,128)(2,1)} %constant.71.clone.y_ref) | copy-start | bytes 589828
  46.7 48.8 %copy-start.9 = (bf16[2,256,128]{2,1,0:T(8,128)(2,1)S(1)}, bf16[2,256,128]{2,1,0:T(8,128)(2,1)}, u32[]{:S(2)}) copy-start(bf16[2,256,128]{2,1,0:T(8,128)(2,1)} %constant.74.clone.y_back_ref) | copy-start | bytes 393220
  46.7 48.8 %copy-start.10 = (bf16[128,192]{1,0:T(8,128)(2,1)S(1)}, bf16[128,192]{1,0:T(8,128)(2,1)}, u32[]{:S(2)}) copy-start(bf16[128,192]{1,0:T(8,128)(2,1)} %constant.72.clone.x_ref) | copy-start | bytes 147460
  46.7 48.8 %copy-start.11 = (bf16[128,128]{1,0:T(8,128)(2,1)S(1)}, bf16[128,128]{1,0:T(8,128)(2,1)}, u32[]{:S(2)}) copy-start(bf16[128,128]{1,0:T(8,128)(2,1)} %constant.73.clone.x_back_ref) | copy-start | bytes 98308
  46.7 48.7 %all-to-all-start.1 = ((f32[32,48,128]{2,1,0:T(8,128)}), f32[32,48,128]{2,1,0:T(8,128)S(1)}, u32[]{:S(2)}, u32[]{:S(2)}) async-start(f32[32,48,128]{2,1,0:T(8,128)} %bitcast.9), calls=%async_computation.1 | async-start | bytes 1572864 | tf_op jit(solution)/shard_map/all_to_all | solution.py:505
  56.3 58.0 %collective-permute-start.3 = (f32[64,896]{1,0:T(8,128)S(1)}, f32[64,896]{1,0:T(8,128)S(1)}, u32[]{:S(2)}, u32[]{:S(2)}) collective-permute-start(f32[64,896]{1,0:T(8,128)S(1)} %slice_bitcast_fusion), channel_id=1, source_target_pairs={{0,64},{64,0},{1,65},{65,1},{2,66},{66,2},{3,67},{67,3},{4,68},{68... | collective-permute-start | bytes 688136 | tf_op jit(solution)/shard_map/ppermute | solution.py:430
  114.3 26.4 %copy-start.7 = (bf16[192,576]{1,0:T(8,128)(2,1)S(1)}, bf16[192,576]{1,0:T(8,128)(2,1)}, u32[]{:S(2)}) copy-start(bf16[192,576]{1,0:T(8,128)(2,1)} %constant.68.clone.cas_ref) | copy-start | bytes 663556
  114.3 26.4 %all-to-all-start.2 = ((f32[32,48,128]{2,1,0:T(8,128)}), f32[32,48,128]{2,1,0:T(8,128)S(1)}, u32[]{:S(2)}, u32[]{:S(2)}) async-start(f32[32,48,128]{2,1,0:T(8,128)} %bitcast.13), calls=%async_computation.2 | async-start | bytes 1572864 | tf_op jit(solution)/shard_map/all_to_all | solution.py:523
  146.8 30.7 %all-to-all-start.3 = ((f32[32,32,128]{2,1,0:T(8,128)}), f32[32,32,128]{2,1,0:T(8,128)S(1)}, u32[]{:S(2)}, u32[]{:S(2)}) async-start(f32[32,32,128]{2,1,0:T(8,128)} %bitcast.15), calls=%async_computation.3 | async-start | bytes 1048576 | tf_op jit(solution)/shard_map/all_to_all | solution.py:540
  207.4 13.6 %all-to-all-start.5 = ((f32[8,1,256]{2,1,0:T(1,128)}), f32[8,1,256]{2,1,0:T(1,128)S(1)}, u32[]{:S(2)}, u32[]{:S(2)}) async-start(f32[8,1,256]{2,1,0:T(1,128)} %all_to_all.46), calls=%async_computation.5 | async-start | bytes 16384 | tf_op jit(solution)/shard_map/all_to_all | solution.py:559
